TPU v7x, 32 devices: a whole 2x2x4 slice. The times are simulated.
32 devices in a mesh: replica: 8 (over y, x, core), dp: 4 (over z).
Axes of the slice: x: 2, y: 2, z: 4, core: 2. Of those that a mesh axis runs over, the one named last changes fastest.
Arguments:
- block_input: bfloat16 [64, 288, 680], P(('replica', 'dp')), may hold values from -40 to 40
- time_shift: bfloat16 [64, 680], P(('replica', 'dp')), may hold values from -4 to 4
- out_grad: bfloat16 [64, 288, 680], P(('replica', 'dp')), may hold values from -6 to 6
- params: float32 [8, 680, 680], P('replica', 'dp'), may hold values from -0.21875 to 0.21875
- first_moment: float32 [8, 680, 680], P('replica', 'dp'), may hold values from -8 to 8
- second_moment: float32 [8, 680, 680], P('replica', 'dp'), may hold values from 1 to 20
- push_weight: float32 [8], P('replica'), may hold values from 0.5 to 2
- step: int32 [1], replicated, may hold values from 0 to 999
Outputs:
- grad_input: bfloat16 [64, 288, 680], P(('replica', 'dp'))
- new_params: float32 [8, 680, 680], P('replica', 'dp')
- new_first: float32 [8, 680, 680], P('replica', 'dp')
- new_second: float32 [8, 680, 680], P('replica', 'dp')
- new_weight: float32 [8], P('replica')
All inputs are finite; a program needn't handle non-finite values.
Results may differ from a plain program's by a relative error of at most 0.006.
Values may be sent and summed in bfloat16 or wider, within the bound.
No kernel may reach another device: no remote copies, remote signals or barrier semaphores. Data moves between devices by JAX's collectives and lax.ppermute only.
A program may use at most 64 MiB of HBM per device.

v0:
```python
import functools

import jax
import jax.numpy as jnp
from jax import lax
from jax.sharding import PartitionSpec as P

GSIZE = 40


NORM_EPS = 1e-05
BETA_ONE = 0.9
BETA_TWO = 0.999
LEARN_RATE = 0.002
ADAM_EPS = 1e-08


def as_sent(shard):

    def short(part):
        return part.astype(jnp.bfloat16) if part.dtype == jnp.float32 else part

    return jax.tree.map(short, shard)


def from_behind(block, axis, distance):
    devices = range(lax.axis_size(axis))
    route = [((i - distance) % len(devices), i) for i in devices]
    return lax.ppermute(block, axis, route)


def group_spread(totals, group_table):
    by_group = jnp.dot(totals, group_table, precision=lax.Precision.HIGHEST)
    return jnp.dot(by_group, group_table.T, precision=lax.Precision.HIGHEST)


def norm_stats(values, group_table):
    entries = values.shape[1] * GSIZE
    average = group_spread(jnp.sum(values, axis=1), group_table) / entries
    centered = values - average[:, None, :]
    variance = group_spread(jnp.sum(centered * centered, axis=1), group_table) / entries
    inverse = lax.rsqrt(variance + NORM_EPS)
    return (centered * inverse[:, None, :], inverse)


def norm_back(grad_val, normed, inverse, group_table):
    entries = grad_val.shape[1] * GSIZE
    first_mean = group_spread(jnp.sum(grad_val, axis=1), group_table) / entries
    second_mean = group_spread(jnp.sum(grad_val * normed, axis=1), group_table) / entries
    return inverse[:, None, :] * (
        grad_val - first_mean[:, None, :] - normed * second_mean[:, None, :]
    )


def silu_grad(values):
    sigmoid_v = jax.nn.sigmoid(values)
    return sigmoid_v * (1.0 + values * (1.0 - sigmoid_v))


def send_rows(payload, distance):
    return jax.tree.map(
        lambda part, own: part.astype(own.dtype),
        from_behind(as_sent(payload), "replica", distance),
        payload,
    )


def local(
    block_input, time_shift, out_grad, params, first_moment, second_moment, push_weight, step
):
    samples, positions, channels = block_input.shape
    groups = channels // GSIZE
    group_table = (
        lax.broadcasted_iota(jnp.int32, (channels, groups), 0) // GSIZE
        == lax.broadcasted_iota(jnp.int32, (channels, groups), 1)
    ).astype(jnp.float32)
    scaled_rows = (params[0] / push_weight[0]).astype(jnp.bfloat16)
    full_weight = lax.all_gather(scaled_rows, "dp", axis=0, tiled=True)
    normed_in, inverse_in = norm_stats(block_input.astype(jnp.float32), group_table)
    activation = jax.nn.silu(normed_in).astype(jnp.bfloat16).reshape(-1, channels)
    hidden = jnp.dot(activation, full_weight, preferred_element_type=jnp.float32).reshape(
        samples, positions, channels
    )
    hidden = hidden + time_shift.astype(jnp.float32)[:, None, :]
    normed_mid, inverse_mid = norm_stats(hidden, group_table)
    grad_mid = out_grad.astype(jnp.float32) * silu_grad(normed_mid)
    grad_hidden = (
        norm_back(grad_mid, normed_mid, inverse_mid, group_table)
        .astype(jnp.bfloat16)
        .reshape(-1, channels)
    )
    grad = lax.psum_scatter(
        lax.dot_general(
            activation, grad_hidden, (((0,), (0,)), ((), ())), preferred_element_type=jnp.float32
        ).astype(jnp.bfloat16),
        "dp",
        scatter_dimension=0,
        tiled=True,
    ).astype(jnp.float32) / lax.axis_size("dp")
    grad_act = lax.dot_general(
        grad_hidden, full_weight, (((1,), (1,)), ((), ())), preferred_element_type=jnp.float32
    )
    grad_act = grad_act.reshape(samples, positions, channels)
    grad_input = norm_back(
        grad_act * silu_grad(normed_in), normed_in, inverse_in, group_table
    ).astype(jnp.bfloat16)
    step_count = (step[0] + 1).astype(jnp.float32)
    first_new = BETA_ONE * first_moment[0] + (1.0 - BETA_ONE) * grad
    second_new = BETA_TWO * second_moment[0] + (1.0 - BETA_TWO) * grad * grad
    update = LEARN_RATE * (first_new / (1.0 - jnp.power(BETA_ONE, step_count)))
    update = update / (jnp.sqrt(second_new / (1.0 - jnp.power(BETA_TWO, step_count))) + ADAM_EPS)
    moved = params[0] - update
    level_count = lax.axis_size("replica").bit_length() - 1
    distance_bits = step[0] % level_count
    branches = [functools.partial(send_rows, distance=1 << power) for power in range(level_count)]
    neighbour, neighbour_weight = lax.switch(distance_bits, branches, (moved, push_weight))
    averaged = 0.5 * (moved + neighbour)
    new_weight = 0.5 * (push_weight + neighbour_weight)
    return (grad_input, averaged[None], first_new[None], second_new[None], new_weight)


def solution(mesh):
    placed = (
        P(("replica", "dp"), None, None),
        P(("replica", "dp"), None),
        P(("replica", "dp"), None, None),
        P("replica", "dp", None),
        P("replica", "dp", None),
        P("replica", "dp", None),
        P("replica"),
        P(),
    )
    return jax.shard_map(
        local,
        mesh=mesh,
        in_specs=placed,
        out_specs=(
            P(("replica", "dp"), None, None),
            P("replica", "dp", None),
            P("replica", "dp", None),
            P("replica", "dp", None),
            P("replica"),
        ),
        check_vma=False,
    )
```

profile of v0, /device:TPU:0, one launch (start us, length us, event | category | flops | bytes accessed | tf_op | source)
XLA Modules:
  0.0 89.9 jit_solution(4606506213630666379)
XLA Ops:
  0.6 0.0 copy-start
  0.7 0.0 copy-start.8
  0.7 1.4 %convert_reduce_fusion = f32[2,680]{1,0:T(2,128)S(1)} fusion(bf16[2,288,680]{2,1,0:T(8,128)(2,1)} %param.11), kind=kLoop, calls=%fused_computation.1 | loop fusion | flops 782000 | bytes 788800 | tf_op jit(solution)/shard_map/reduce_sum | solution.py:39
  2.1 0.4 fusion.35
  2.6 0.5 convolution_multiply_fusion.7
  3.2 0.3 fusion.19
  3.4 0.4 fusion.34
  3.9 0.0 copy-done.12
  3.9 1.2 %fusion.23 = f32[2,680]{1,0:T(2,128)} fusion(f32[2,17]{1,0:T(2,128)S(1)} %fusion.34, s32[680]{0:T(1024)S(1)} %iota_divide_fusion, s32[680]{0:T(1024)S(1)} %broadcast_add_fusion, pred[680]{0:T(1024)(128)(4,1)S(1)} %fusion.89), kind=kOutput, calls=%fused_computation.38 | convolution fusion | flops 303280 | bytes 11696 | tf_op jit(solution)/shard_map/dot_general | solution.py:34
  5.8 24.6 %all-gather = bf16[4,170,680]{2,1,0:T(8,128)(2,1)S(1)} all-gather(bf16[1,170,680]{2,1,0:T(8,128)(2,1)S(1)} %fusion.38), channel_id=1, replica_groups=mesh['replica'=8,'dp'=4] {'dp'}, dimensions={0}, use_global_device_ids=true | all-gather | bytes 1156000 | tf_op jit(solution)/shard_map/all_gather | solution.py:78
  30.4 0.5 reshape.46
  30.9 2.0 %add_reduce_fusion = (f32[2,680]{1,0:T(2,128)S(1)}, f32[2,288,680]{2,1,0:T(8,128)S(1)}) fusion(f32[2,680]{1,0:T(2,128)S(1)} %convert_element_type.87, bf16[680,680,1]{1,0,2:T(8,128)(2,1)S(1)} %reshape.46, bf16[2,288,680]{2,1,0:T(8,128)(2,1)S(1)} %copy-done, f32[2,680]{1,0:T(2,128)} %fusion.23, f32[2,680]{1,0:T(2,128)S(1)} %convolution_multiply_fusion.7), kind=kOutput, calls=%fused_computation.27 | convolution fusion | flops 536600256 | bytes 3296640 | tf_op jit(solution)/shard_map/dot_general | solution.py:81
  32.9 0.4 fusion.33
  33.3 0.5 convolution_multiply_fusion.5
  33.9 0.3 multiply_reduce_fusion.1
  34.2 0.4 fusion.32
  34.6 0.6 fusion.21
  35.2 0.0 copy-done.1
  35.2 1.0 %fusion.93 = (f32[2,680]{1,0:T(2,128)S(1)}, f32[2,680]{1,0:T(2,128)S(1)}) fusion(f32[2,680]{1,0:T(2,128)S(1)} %fusion.21, f32[2,680]{1,0:T(2,128)S(1)} %convolution_multiply_fusion.5, f32[2,288,680]{2,1,0:T(8,128)S(1)} %get-tuple-element.68, f32[2,680]{1,0:T(2,128)S(1)} %convert_element_type.87, bf16[2,288,680]{2,1,0:T(8,128)(2,1)S(1)} %copy-done.1), kind=kLoop, calls=%fused_computation.120 | loop fusion | flops 5872480 | bytes 2377280 | tf_op jit(solution)/shard_map/reduce_sum | solution.py:48
  36.2 0.4 fusion.30
  36.7 0.5 convolution_multiply_fusion.2
  37.2 0.5 fusion.31
  37.7 0.5 convolution_multiply_fusion.3
  38.3 0.0 copy-start.7
  38.3 1.1 %multiply_convert_fusion = bf16[2,288,680]{2,1,0:T(8,128)(2,1)S(1)} fusion(f32[2,288,680]{2,1,0:T(8,128)S(1)} %get-tuple-element.68, f32[2,680]{1,0:T(2,128)S(1)} %convolution_multiply_fusion.2, f32[2,680]{1,0:T(2,128)S(1)} %convolution_multiply_fusion.3, f32[2,680]{1,0:T(2,128)S(1)} %fusion.21, f32[2,680]{1,0:T(2,128)S(1)} %convolution_multiply_fusion.5, ...), kind=kLoop, calls=%fused_computation.22 | loop fusion | flops 6658560 | bytes 3160640 | tf_op jit(solution)/shard_map/convert_element_type | solution.py:89
  39.4 0.9 %copy-done.4 = bf16[2,288,680]{2,1,0:T(8,128)(2,1)} copy-done((bf16[2,288,680]{2,1,0:T(8,128)(2,1)}, bf16[2,288,680]{2,1,0:T(8,128)(2,1)S(1)}, u32[]{:S(2)}) %copy-start.4) | copy-done | bytes 783384
  40.3 1.2 %bitcast_convert_fusion = bf16[680,680]{1,0:T(8,128)(2,1)S(1)} fusion(bf16[2,288,680]{2,1,0:T(8,128)(2,1)S(1)} %multiply_convert_fusion, bf16[2,288,680]{2,1,0:T(8,128)(2,1)S(1)} %copy-done, f32[2,680]{1,0:T(2,128)S(1)} %copy-done.7, f32[2,680]{1,0:T(2,128)S(1)} %convolution_multiply_fusion.7), kind=kOutput, calls=%fused_computation.9 | convolution fusion | flops 536280640 | bytes 2502400 | tf_op jit(solution)/shard_map/dot_general | solution.py:93
  41.5 25.0 %fusion = bf16[176,680]{1,0:T(8,128)(2,1)S(1)} fusion(bf16[680,680]{1,0:T(8,128)(2,1)S(1)} %bitcast_convert_fusion), kind=kCustom, calls=%all-reduce-scatter | all-reduce-scatter fusion | flops 478721 | bytes 1164672
  66.5 1.5 %collective-permute-start.6 = (bf16[18,680]{1,0:T(8,128)(2,1)S(1)}, bf16[18,680]{1,0:T(8,128)(2,1)S(1)}, u32[]{:S(2)}, u32[]{:S(2)}) collective-permute-start(bf16[18,680]{1,0:T(8,128)(2,1)S(1)} %slice), channel_id=1, source_target_pairs={{0,1},{1,2},{2,3},{4,5},{5,6},{6,7},{8,9},{9,10},{10,11},{12,13},{... | collective-permute-start | bytes 73448
  68.0 2.9 %fusion.94 = (f32[2,680]{1,0:T(2,128)S(1)}, f32[2,680]{1,0:T(2,128)S(1)}, f32[2,288,680]{2,1,0:T(8,128)S(1)}) fusion(f32[2,680]{1,0:T(2,128)S(1)} %copy-done.7, f32[2,680]{1,0:T(2,128)S(1)} %convolution_multiply_fusion.7, bf16[2,288,680]{2,1,0:T(8,128)(2,1)S(1)} %copy-done, bf16[2,288,680]{2,1,0:T(8,128)(2,1)} %copy-done.4, bf16[680,680,1]{1,0,2:T(8,128)(2,1)} %copy-done.3), kind=kOutput, calls=%fused_computation.121 | convolution fusion | flops 538165632 | bytes 4080000 | tf_op jit(solution)/shard_map/dot_general | solution.py:100
  70.8 0.4 fusion.28
  71.3 0.5 convolution_multiply_fusion
  71.8 0.5 fusion.29
  72.3 0.5 convolution_multiply_fusion.1
  72.9 0.0 copy-start.11
  72.9 0.0 copy-start.6
  72.9 1.4 %fusion.18 = bf16[2,288,680]{2,1,0:T(8,128)(2,1)} fusion(bf16[2,288,680]{2,1,0:T(8,128)(2,1)S(1)} %copy-done, f32[2,288,680]{2,1,0:T(8,128)S(1)} %get-tuple-element.69, f32[2,680]{1,0:T(2,128)S(1)} %convolution_multiply_fusion, f32[2,680]{1,0:T(2,128)S(1)} %convolution_multiply_fusion.1, f32[2,680]{1,0:T(2,128)S(1)} %copy-done.7, ...), kind=kLoop, calls=%fused_computation.20 | loop fusion | flops 3133440 | bytes 3155200 | tf_op jit(solution)/shard_map/convert_element_type | solution.py:106
  75.1 0.6 dynamic-slice.4
  76.3 0.5 concatenate
  76.8 0.5 fusion.37
  77.3 7.4 %conditional.4 = (f32[170,680]{1,0:T(8,128)S(1)}, f32[1]{0:T(128)}) conditional(s32[]{:T(128)} %clamp.3, (f32[170,680]{1,0:T(8,128)S(1)}, f32[1]{0:T(128)}) %tuple.40, (f32[170,680]{1,0:T(8,128)S(1)}, f32[1]{0:T(128)}) %tuple.40, (f32[170,680]{1,0:T(8,128)S(1)}, f32[1]{0:T(128)}) %tuple.40), branch_computations={%region_9.10_spmd, %region_10.11_spmd, %region_11.12_spmd} | conditional | flops 231202 | bytes 2312116
  77.4 1.6 %collective-permute-start.4 = (bf16[170,680]{1,0:T(8,128)(2,1)S(1)}, bf16[170,680]{1,0:T(8,128)(2,1)S(1)}, u32[]{:S(2)}, u32[]{:S(2)}) collective-permute-start(bf16[170,680]{1,0:T(8,128)(2,1)S(1)} %convert_element_type.70), channel_id=1, source_target_pairs={{16,0},{20,4},{24,8},{28,12},{0,16},{4,20},{8,24},{12,28},{17,1},{... | collective-permute-start | bytes 693608 | tf_op jit(solution)/shard_map/cond/branch_2_fun/ppermute | solution.py:29
  79.6 3.4 %collective-permute-start.5 = (bf16[1]{0:T(256)(128)(2,1)}, bf16[1]{0:T(256)(128)(2,1)}, u32[]{:S(2)}, u32[]{:S(2)}) collective-permute-start(bf16[1]{0:T(256)(128)(2,1)} %convert_element_type.72), channel_id=1, source_target_pairs={{16,0},{20,4},{24,8},{28,12},{0,16},{4,20},{8,24},{12,28},{17,1},{... | collective-permute-start | bytes 14 | tf_op jit(solution)/shard_map/cond/branch_2_fun/ppermute | solution.py:29
  83.0 1.1 %collective-permute-done.5 = bf16[1]{0:T(256)(128)(2,1)} collective-permute-done((bf16[1]{0:T(256)(128)(2,1)}, bf16[1]{0:T(256)(128)(2,1)}, u32[]{:S(2)}, u32[]{:S(2)}) %collective-permute-start.5) | collective-permute-done | bytes 34 | tf_op jit(solution)/shard_map/cond/branch_2_fun/ppermute | solution.py:29
  84.7 0.1 multiply_bitcast_fusion
  84.8 1.3 %copy.25 = f32[1,170,680]{2,0,1:T(1,128)} copy(f32[1,170,680]{2,1,0:T(8,128)S(1)} %multiply_bitcast_fusion) | data formatting | bytes 924800
  86.1 1.3 %copy.26 = f32[1,170,680]{2,0,1:T(1,128)} copy(f32[1,170,680]{2,1,0:T(8,128)S(1)} %get-tuple-element.66) | data formatting | bytes 924800
  87.4 1.3 %copy.27 = f32[1,170,680]{2,0,1:T(1,128)} copy(f32[1,170,680]{2,1,0:T(8,128)S(1)} %get-tuple-element.64) | data formatting | bytes 924800
  (30 shorter events, 0.2 us)
Async XLA Ops:
  0.6 2.5 %copy-start = (bf16[2,288,680]{2,1,0:T(8,128)(2,1)S(1)}, bf16[2,288,680]{2,1,0:T(8,128)(2,1)}, u32[]{:S(2)}) copy-start(bf16[2,288,680]{2,1,0:T(8,128)(2,1)} %param.11) | copy-start | bytes 2350084
  0.6 4.5 %copy-start.10 = (bf16[2,680]{1,0:T(2,128)(2,1)S(1)}, bf16[2,680]{1,0:T(2,128)(2,1)}, u32[]{:S(2)}) copy-start(bf16[2,680]{1,0:T(2,128)(2,1)} %param.12) | copy-start | bytes 8164
  0.7 5.1 %copy-start.2 = (f32[1,170,680]{2,0,1:T(1,128)S(1)}, f32[1,170,680]{2,0,1:T(1,128)}, u32[]{:S(2)}) copy-start(f32[1,170,680]{2,0,1:T(1,128)} %param.14) | copy-start | bytes 1387204
  0.7 3.2 %copy-start.8 = (s32[680]{0:T(1024)}, s32[680]{0:T(1024)S(1)}, u32[]{:S(2)}) copy-start(s32[680]{0:T(1024)S(1)} %broadcast_add_fusion) | copy-start | bytes 8164
  0.7 3.2 %copy-start.12 = (pred[680]{0:T(1024)(128)(4,1)}, pred[680]{0:T(1024)(128)(4,1)S(1)}, u32[]{:S(2)}) copy-start(pred[680]{0:T(1024)(128)(4,1)S(1)} %fusion.89) | copy-start | bytes 2044
  30.9 2.0 %copy-start.3 = (bf16[680,680,1]{1,0,2:T(8,128)(2,1)}, bf16[680,680,1]{1,0,2:T(8,128)(2,1)S(1)}, u32[]{:S(2)}) copy-start(bf16[680,680,1]{1,0,2:T(8,128)(2,1)S(1)} %reshape.46) | copy-start | bytes 2774404
  30.9 2.0 %copy-start.9 = (s32[680]{0:T(1024)S(1)}, s32[680]{0:T(1024)}, u32[]{:S(2)}) copy-start(s32[680]{0:T(1024)} %copy-done.8) | copy-start | bytes 8164
  30.9 2.0 %copy-start.13 = (pred[680]{0:T(1024)(128)(4,1)S(1)}, pred[680]{0:T(1024)(128)(4,1)}, u32[]{:S(2)}) copy-start(pred[680]{0:T(1024)(128)(4,1)} %copy-done.12) | copy-start | bytes 2044
  32.9 2.4 %copy-start.1 = (bf16[2,288,680]{2,1,0:T(8,128)(2,1)S(1)}, bf16[2,288,680]{2,1,0:T(8,128)(2,1)}, u32[]{:S(2)}) copy-start(bf16[2,288,680]{2,1,0:T(8,128)(2,1)} %param.13) | copy-start | bytes 2350084
  38.3 2.0 %copy-start.7 = (f32[2,680]{1,0:T(2,128)S(1)}, f32[2,680]{1,0:T(2,128)}, u32[]{:S(2)}) copy-start(f32[2,680]{1,0:T(2,128)} %fusion.23) | copy-start | bytes 16324
  39.3 0.9 %copy-start.4 = (bf16[2,288,680]{2,1,0:T(8,128)(2,1)}, bf16[2,288,680]{2,1,0:T(8,128)(2,1)S(1)}, u32[]{:S(2)}) copy-start(bf16[2,288,680]{2,1,0:T(8,128)(2,1)S(1)} %multiply_convert_fusion) | copy-start | bytes 2350084
  66.5 9.8 %collective-permute-start.6 = (bf16[18,680]{1,0:T(8,128)(2,1)S(1)}, bf16[18,680]{1,0:T(8,128)(2,1)S(1)}, u32[]{:S(2)}, u32[]{:S(2)}) collective-permute-start(bf16[18,680]{1,0:T(8,128)(2,1)S(1)} %slice), channel_id=1, source_target_pairs={{0,1},{1,2},{2,3},{4,5},{5,6},{6,7},{8,9},{9,10},{10,11},{12,13},{... | collective-permute-start | bytes 73448
  72.9 2.2 %copy-start.11 = (u32[32]{0:T(128)S(1)}, u32[32]{0:T(128)}, u32[]{:S(2)}) copy-start(u32[32]{0:T(128)} %constant.86) | copy-start | bytes 388
  72.9 3.9 %copy-start.5 = (f32[1,170,680]{2,0,1:T(1,128)S(1)}, f32[1,170,680]{2,0,1:T(1,128)}, u32[]{:S(2)}) copy-start(f32[1,170,680]{2,0,1:T(1,128)} %param.16) | copy-start | bytes 1387204
  72.9 3.9 %copy-start.6 = (f32[1,170,680]{2,0,1:T(1,128)S(1)}, f32[1,170,680]{2,0,1:T(1,128)}, u32[]{:S(2)}) copy-start(f32[1,170,680]{2,0,1:T(1,128)} %param.15) | copy-start | bytes 1387204
  77.4 7.3 %collective-permute-start.4 = (bf16[170,680]{1,0:T(8,128)(2,1)S(1)}, bf16[170,680]{1,0:T(8,128)(2,1)S(1)}, u32[]{:S(2)}, u32[]{:S(2)}) collective-permute-start(bf16[170,680]{1,0:T(8,128)(2,1)S(1)} %convert_element_type.70), channel_id=1, source_target_pairs={{16,0},{20,4},{24,8},{28,12},{0,16},{4,20},{8,24},{12,28},{17,1},{... | collective-permute-start | bytes 693608 | tf_op jit(solution)/shard_map/cond/branch_2_fun/ppermute | solution.py:29
  79.6 4.5 %collective-permute-start.5 = (bf16[1]{0:T(256)(128)(2,1)}, bf16[1]{0:T(256)(128)(2,1)}, u32[]{:S(2)}, u32[]{:S(2)}) collective-permute-start(bf16[1]{0:T(256)(128)(2,1)} %convert_element_type.72), channel_id=1, source_target_pairs={{16,0},{20,4},{24,8},{28,12},{0,16},{4,20},{8,24},{12,28},{17,1},{... | collective-permute-start | bytes 14 | tf_op jit(solution)/shard_map/cond/branch_2_fun/ppermute | solution.py:29
where the time goes:
time: 90.2 us; the launch traced here: 89.9 us
  blocking collectives  49.5 us (55%)
  matrix products  14.6 us (16%)
  local copies, waits for them, and re-layouts  6.56 us (7%)
  starting transfers between devices  6.42 us (7%)
  other arithmetic  6.1 us (7%)
  between operations  4.26 us (5%)
  loops' own time  1.29 us (1%)
  waiting for transfers between devices  1.09 us (1%)
    unnamed x1, blocking collectives  25 us
    all_gather x1, blocking collectives, local(): full_weight = lax.all_gather(scaled_rows, 'dp', axis=0, tiled=True)  24.6 us
    unnamed x35, local copies, waits for them, and re-layouts  6.56 us
    ppermute x2, starting transfers between devices, from_behind(): return lax.ppermute(block, axis, route)  4.95 us
    dot_general x8, matrix products, group_spread(): return jnp.dot(by_group, group_table.T, precision=lax.Precision.HIGHEST)  4.88 us
    dot_general x8, matrix products, group_spread(): by_group = jnp.dot(totals, group_table, precision=lax.Precision.HIGHEST)  3.67 us
    dot_general x1, matrix products, local(): lax.dot_general(grad_hidden, full_weight, (((1,), (1,)), ((), ())), prefe...  2.88 us
    dot_general x1, matrix products, local(): jnp.dot(activation, full_weight, preferred_element_type=jnp.float32)  1.96 us
  transfers between devices with their start and end apart: 3, of which 1 were waited for; matrix products, arithmetic and copies ran while one was open for 8% of the time, Pallas kernels for 0%

commit v1 on v0

v1 whole, which is shorter than its diff:
```python
import functools

import jax
import jax.numpy as jnp
from jax import lax
from jax.experimental import pallas as pl
from jax.experimental.pallas import tpu as pltpu
from jax.sharding import PartitionSpec as P

GSIZE = 40

NORM_EPS = 1e-05
BETA_ONE = 0.9
BETA_TWO = 0.999
LEARN_RATE = 0.002
ADAM_EPS = 1e-08

VMEM_BYTES = 48 * 1024 * 1024


def whole_in_vmem(count):
    return [pl.BlockSpec(memory_space=pltpu.VMEM)] * count


def group_sums(rows, same_group):
    high = rows.astype(jnp.bfloat16)
    rest = rows - high.astype(jnp.float32)
    middle = rest.astype(jnp.bfloat16)
    low = (rest - middle.astype(jnp.float32)).astype(jnp.bfloat16)
    count = rows.shape[0]
    stacked = jnp.concatenate([high.astype(jnp.float32), middle.astype(jnp.float32), low.astype(jnp.float32)], axis=0)
    sums = jnp.dot(stacked.astype(jnp.bfloat16), same_group, preferred_element_type=jnp.float32)
    return sums[:count] + (sums[count : 2 * count] + sums[2 * count :])


def position_sums(parts):
    return jnp.concatenate([jnp.sum(part, axis=0, keepdims=True) for part in parts], axis=0)


def sigmoid(values):
    return 0.5 * jnp.tanh(0.5 * values) + 0.5


def silu_grad(values):
    gate = sigmoid(values)
    return gate * (1.0 + values * (1.0 - gate))


def norm_in_kernel(x_ref, same_group_ref, act_ref, mean_ref, inverse_ref):
    samples, positions, channels = x_ref.shape
    entries = positions * GSIZE
    same_group = same_group_ref[...]
    parts = [x_ref[i].astype(jnp.float32) for i in range(samples)]
    mean = group_sums(position_sums(parts), same_group) / entries
    centered = [parts[i] - mean[i : i + 1] for i in range(samples)]
    variance = group_sums(position_sums([part * part for part in centered]), same_group) / entries
    inverse = lax.rsqrt(variance + NORM_EPS)
    mean_ref[...] = mean
    inverse_ref[...] = inverse
    for i in range(samples):
        normed = centered[i] * inverse[i : i + 1]
        act_ref[i * positions : (i + 1) * positions, :] = (normed * sigmoid(normed)).astype(jnp.bfloat16)


def mix_kernel(shards, me_ref, act_ref, act_t_ref, shift_ref, out_grad_ref, same_group_ref, *refs):
    weight_refs, refs = refs[:shards], refs[shards:]
    grad_hidden_ref, weight_ref, own_ref = refs[:3]
    send_refs, rows_ref = refs[3 : 2 + shards], refs[2 + shards]
    samples, positions, columns = out_grad_ref.shape
    rows = own_ref.shape[0]
    entries = positions * GSIZE
    turn = me_ref[0] * rows
    for slot, shard_ref in enumerate(weight_refs):
        rows_ref[slot * rows : (slot + 1) * rows, :] = shard_ref[...].astype(jnp.float32)
    weight = pltpu.roll(rows_ref[...], turn, 0).astype(jnp.bfloat16)
    weight_ref[...] = weight
    same_group = same_group_ref[:columns, :columns]
    hidden = jnp.dot(act_ref[...], weight, preferred_element_type=jnp.float32)
    parts = [
        hidden[i * positions : (i + 1) * positions] + shift_ref[i : i + 1, :].astype(jnp.float32)
        for i in range(samples)
    ]
    mean = group_sums(position_sums(parts), same_group) / entries
    parts = [parts[i] - mean[i : i + 1] for i in range(samples)]
    variance = group_sums(position_sums([part * part for part in parts]), same_group) / entries
    inverse = lax.rsqrt(variance + NORM_EPS)
    normed = [parts[i] * inverse[i : i + 1] for i in range(samples)]
    grads = [out_grad_ref[i].astype(jnp.float32) * silu_grad(normed[i]) for i in range(samples)]
    means = group_sums(
        jnp.concatenate(
            [position_sums(grads), position_sums([g * n for g, n in zip(grads, normed)])], axis=0
        ),
        same_group,
    ) / entries
    for i in range(samples):
        first, second = means[i : i + 1], means[samples + i : samples + i + 1]
        grad_hidden_ref[i * positions : (i + 1) * positions, :] = (
            inverse[i : i + 1] * (grads[i] - first - normed[i] * second)
        ).astype(jnp.bfloat16)
    grad = jnp.dot(act_t_ref[...], grad_hidden_ref[...], preferred_element_type=jnp.float32)
    rows_ref[...] = pltpu.roll(grad, rows * shards - turn, 0)
    own_ref[...] = rows_ref[:rows, :]
    for slot, send_ref in enumerate(send_refs, 1):
        send_ref[...] = rows_ref[slot * rows : (slot + 1) * rows, :].astype(jnp.bfloat16)


def input_grad_kernel(pieces, x_ref, mean_ref, inverse_ref, same_group_ref, *refs):
    grad_refs, weight_refs, out_ref = refs[:pieces], refs[pieces : 2 * pieces], refs[2 * pieces]
    samples, positions, channels = x_ref.shape
    entries = positions * GSIZE
    grad_act = sum(
        lax.dot_general(
            grad_ref[...], weight_ref[...], (((1,), (1,)), ((), ())), preferred_element_type=jnp.float32
        )
        for grad_ref, weight_ref in zip(grad_refs, weight_refs)
    )
    inverse = inverse_ref[...]
    normed = [
        (x_ref[i].astype(jnp.float32) - mean_ref[i : i + 1, :]) * inverse[i : i + 1] for i in range(samples)
    ]
    grads = [grad_act[i * positions : (i + 1) * positions] * silu_grad(normed[i]) for i in range(samples)]
    means = group_sums(
        jnp.concatenate(
            [position_sums(grads), position_sums([g * n for g, n in zip(grads, normed)])], axis=0
        ),
        same_group_ref[...],
    ) / entries
    for i in range(samples):
        first, second = means[i : i + 1], means[samples + i : samples + i + 1]
        out_ref[i] = (inverse[i : i + 1] * (grads[i] - first - normed[i] * second)).astype(jnp.bfloat16)


def kernel_options():
    return pltpu.CompilerParams(vmem_limit_bytes=VMEM_BYTES)


def work(tokens, deep, wide, products=1):
    return pl.CostEstimate(
        flops=2 * products * tokens * deep * wide, bytes_accessed=8 * tokens * wide, transcendentals=tokens * wide
    )


def norm_in(block_input, same_group):
    samples, positions, channels = block_input.shape
    return pl.pallas_call(
        norm_in_kernel,
        out_shape=(
            jax.ShapeDtypeStruct((samples * positions, channels), jnp.bfloat16),
            jax.ShapeDtypeStruct((samples, channels), jnp.float32),
            jax.ShapeDtypeStruct((samples, channels), jnp.float32),
        ),
        in_specs=whole_in_vmem(2),
        out_specs=tuple(whole_in_vmem(3)),
        compiler_params=kernel_options(),
        cost_estimate=work(samples * positions, 8, channels),
        name="norm_in",
    )(block_input, same_group)


def mix(me, activation, activation_t, shift, out_grad, same_group, weights):
    shards = len(weights)
    rows, columns = weights[0].shape
    tokens, channels = activation.shape
    return pl.pallas_call(
        functools.partial(mix_kernel, shards),
        out_shape=(
            jax.ShapeDtypeStruct((tokens, columns), jnp.bfloat16),
            jax.ShapeDtypeStruct((channels, columns), jnp.bfloat16),
            jax.ShapeDtypeStruct((rows, columns), jnp.float32),
        )
        + (jax.ShapeDtypeStruct((rows, columns), jnp.bfloat16),) * (shards - 1),
        in_specs=[pl.BlockSpec(memory_space=pltpu.SMEM)] + whole_in_vmem(5 + shards),
        out_specs=tuple(whole_in_vmem(2 + shards)),
        scratch_shapes=[pltpu.VMEM((channels, columns), jnp.float32)],
        compiler_params=kernel_options(),
        cost_estimate=work(tokens, channels, columns, 2),
        name="mix",
    )(me, activation, activation_t, shift, out_grad, same_group, *weights)


def input_grad(block_input, mean, inverse, same_group, grads, weights):
    samples, positions, channels = block_input.shape
    return pl.pallas_call(
        functools.partial(input_grad_kernel, len(grads)),
        out_shape=jax.ShapeDtypeStruct(block_input.shape, jnp.bfloat16),
        in_specs=whole_in_vmem(4 + 2 * len(grads)),
        out_specs=pl.BlockSpec(memory_space=pltpu.VMEM),
        compiler_params=kernel_options(),
        cost_estimate=work(samples * positions, channels, channels),
        name="input_grad",
    )(block_input, mean, inverse, same_group, *grads, *weights)


def moved_on(block, axis, distance):
    size = lax.axis_size(axis)
    return lax.ppermute(block, axis, [(i, (i + distance) % size) for i in range(size)])


def column_cuts(channels):
    groups = channels // GSIZE
    half = (groups + 1) // 2 * GSIZE
    return [(0, half), (half, channels)]


def local(
    block_input, time_shift, out_grad, params, first_moment, second_moment, push_weight, step
):
    samples, positions, channels = block_input.shape
    shards = lax.axis_size("dp")
    me = lax.axis_index("dp").astype(jnp.int32).reshape(1)
    cuts = column_cuts(channels)
    group_of = jnp.arange(channels, dtype=jnp.int32) // GSIZE
    same_group = (group_of[:, None] == group_of[None, :]).astype(jnp.bfloat16)

    scaled_rows = (params[0] / push_weight[0]).astype(jnp.bfloat16)
    weights = []
    for start, stop in cuts:
        piece = scaled_rows[:, start:stop]
        weights.append([piece] + [moved_on(piece, "dp", -slot) for slot in range(1, shards)])

    level_count = lax.axis_size("replica").bit_length() - 1
    distance_bits = step[0] % level_count

    def from_behind(block):
        branches = [
            functools.partial(moved_on, axis="replica", distance=1 << power) for power in range(level_count)
        ]
        return lax.switch(distance_bits, branches, block)

    activation, mean_in, inverse_in = norm_in(block_input, same_group)
    activation_t = activation.T

    step_count = (step[0] + 1).astype(jnp.float32)
    first_scale = LEARN_RATE / (1.0 - jnp.power(BETA_ONE, step_count))
    second_scale = 1.0 / (1.0 - jnp.power(BETA_TWO, step_count))

    hidden_grads, full_weights, arrived = [], [], []
    for (start, stop), shard_list in zip(cuts, weights):
        grad_hidden, full_weight, own, *sends = mix(
            me,
            activation,
            activation_t,
            time_shift[:, start:stop],
            out_grad[:, :, start:stop],
            same_group,
            shard_list,
        )
        hidden_grads.append(grad_hidden)
        full_weights.append(full_weight)
        arrived.append(
            (own, [moved_on(send, "dp", slot) for slot, send in zip(range(1, shards), sends)])
        )
    grad_input = input_grad(block_input, mean_in, inverse_in, same_group, hidden_grads, full_weights)

    outs = []
    for (start, stop), (own, others) in zip(cuts, arrived):
        grad = (own + sum(other.astype(jnp.float32) for other in others)) / shards
        first_new = BETA_ONE * first_moment[0, :, start:stop] + (1.0 - BETA_ONE) * grad
        second_new = BETA_TWO * second_moment[0, :, start:stop] + (1.0 - BETA_TWO) * grad * grad
        update = (first_scale * first_new) / (jnp.sqrt(second_scale * second_new) + ADAM_EPS)
        moved = params[0, :, start:stop] - update
        neighbour = from_behind(moved.astype(jnp.bfloat16))
        outs.append((0.5 * (moved + neighbour.astype(jnp.float32)), first_new, second_new))
    averaged, first_new, second_new = (jnp.concatenate(pieces, axis=1) for pieces in zip(*outs))
    neighbour_weight = from_behind(push_weight.astype(jnp.bfloat16)).astype(jnp.float32)
    new_weight = 0.5 * (push_weight + neighbour_weight)
    return (grad_input, averaged[None], first_new[None], second_new[None], new_weight)


def solution(mesh):
    placed = (
        P(("replica", "dp"), None, None),
        P(("replica", "dp"), None),
        P(("replica", "dp"), None, None),
        P("replica", "dp", None),
        P("replica", "dp", None),
        P("replica", "dp", None),
        P("replica"),
        P(),
    )
    return jax.shard_map(
        local,
        mesh=mesh,
        in_specs=placed,
        out_specs=(
            P(("replica", "dp"), None, None),
            P("replica", "dp", None),
            P("replica", "dp", None),
            P("replica", "dp", None),
            P("replica"),
        ),
        check_vma=False,
    )
```

time: 90.2 us -> 79.2 us (0.88)
  blocking collectives: 49.5 us -> 0 us
  starting transfers between devices: 6.42 us -> 31.2 us
  matrix products: 14.6 us -> 0 us
  waiting for transfers between devices: 1.09 us -> 14.8 us
  Pallas kernels: 0 us -> 13.5 us
  local copies, waits for them, and re-layouts: 6.56 us -> 10.8 us
  loops' own time: 1.29 us -> 0.06 us
  other arithmetic: 6.1 us -> 5.02 us
    ppermute x2 -> x15, starting transfers between devices: 4.95 us -> 31.2 us  [moved_on(): lax.ppermute(block, axis, [(i, (i + distance) % size) for i in range(size)])]
    unnamed x1 -> x0, blocking collectives: 25 us -> none
    all_gather x1 -> x0, blocking collectives: 24.6 us -> none  [local(): full_weight = lax.all_gather(scaled_rows, 'dp', axis=0, tiled=True)]
    dot_general x19 -> x0, matrix products: 14.6 us -> none  [the longest x8 4.88 us: group_spread(): return jnp.dot(by_group, group_table.T, precision=lax.Precision.HIGHEST)]
    ppermute x2 -> x15, waiting for transfers between devices: 1.09 us -> 14.8 us  [moved_on(): lax.ppermute(block, axis, [(i, (i + distance) % size) for i in range(size)])]
    pallas_call x0 -> x4, Pallas kernels: none -> 13.5 us  [the longest x2 9.11 us: mix(): pl.pallas_call(functools.partial(mix_kernel, shards), out_shape=(jax.Shap...]
    reduce_sum x4 -> x0, other arithmetic: 3 us -> none  [the longest x1 1.42 us: norm_stats(): average = group_spread(jnp.sum(values, axis=1), group_table) / entries]
    slice x0 -> x12, local copies, waits for them, and re-layouts: none -> 2.74 us  [the longest x2 1.32 us: local(): out_grad[:, :, start:stop]]
  transfers between devices with their start and end apart: 3 -> 15, of which waited for: 1 -> 4; matrix products, arithmetic and copies ran while one was open for 8% -> 6% of each run, Pallas kernels for 0% -> 17%
where the time goes in v1:
time: 79.2 us; the launch traced here: 79.5 us
  starting transfers between devices  31.2 us (39%)
  waiting for transfers between devices  14.8 us (19%)
  Pallas kernels  13.5 us (17%)
  local copies, waits for them, and re-layouts  10.8 us (14%)
  other arithmetic  5.02 us (6%)
  between operations  4.18 us (5%)
    ppermute x15, starting transfers between devices, moved_on(): lax.ppermute(block, axis, [(i, (i + distance) % size) for i in range(size)])  31.2 us
    ppermute x15, waiting for transfers between devices, moved_on(): lax.ppermute(block, axis, [(i, (i + distance) % size) for i in range(size)])  14.8 us
    pallas_call x2, Pallas kernels, mix(): pl.pallas_call(functools.partial(mix_kernel, shards), out_shape=(jax.Shap...  9.11 us
    unnamed x25, local copies, waits for them, and re-layouts  7.13 us
    pallas_call x1, Pallas kernels, input_grad(): pl.pallas_call(functools.partial(input_grad_kernel, len(grads)), out_shap...  3.16 us
    unnamed x1, other arithmetic  1.9 us
    mul x2, other arithmetic, local(): 0.5 * (moved + neighbour.astype(jnp.float32))  1.88 us
  transfers between devices with their start and end apart: 15, of which 4 were waited for; matrix products, arithmetic and copies ran while one was open for 6% of the time, Pallas kernels for 17%

profile of v1, /device:TPU:0, one launch (start us, length us, event | category | flops | bytes accessed | tf_op | source)
XLA Modules:
  0.0 79.5 jit_solution(8743542995312672732)
XLA Ops:
  1.3 1.9 %fusion.22 = (f32[1,170,680]{2,1,0:T(8,128)}, bf16[170,680]{1,0:T(8,128)(2,1)S(1)}) fusion(f32[1,170,680]{2,0,1:T(1,128)} %param.20, f32[]{:T(128)} %bitcast.44), kind=kLoop, calls=%fused_computation.35 | loop fusion | flops 231200 | bytes 1156004 | tf_op args[3]
  3.2 5.1 %collective-permute-start.9 = (bf16[170,360]{1,0:T(8,128)(2,1)S(1)}, bf16[170,360]{1,0:T(8,128)(2,1)S(1)}, u32[]{:S(2)}, u32[]{:S(2)}) collective-permute-start(bf16[170,360]{1,0:T(8,128)(2,1)S(1)} %slice.48.refs_0_), channel_id=1, source_target_pairs={{0,3},{1,0},{2,1},{3,2},{4,7},{5,4},{6,5},{7,6},{8,11},{9,8},{10,9... | collective-permute-start | bytes 367208 | tf_op jit(solution)/shard_map/ppermute | solution.py:196
  8.3 1.0 %collective-permute-start.11 = (bf16[170,360]{1,0:T(8,128)(2,1)S(1)}, bf16[170,360]{1,0:T(8,128)(2,1)S(1)}, u32[]{:S(2)}, u32[]{:S(2)}) collective-permute-start(bf16[170,360]{1,0:T(8,128)(2,1)S(1)} %slice.48.refs_0_), channel_id=1, source_target_pairs={{0,1},{1,2},{2,3},{3,0},{4,5},{5,6},{6,7},{7,4},{8,9},{9,10},{10,1... | collective-permute-start | bytes 367208 | tf_op jit(solution)/shard_map/ppermute | solution.py:196
  9.3 0.1 slice.49.refs_0_
  9.4 2.9 %collective-permute-start.12 = (bf16[170,320]{1,0:T(8,128)(2,1)S(1)}, bf16[170,320]{1,0:T(8,128)(2,1)S(1)}, u32[]{:S(2)}, u32[]{:S(2)}) collective-permute-start(bf16[170,320]{1,0:T(8,128)(2,1)S(1)} %slice.49.refs_0_), channel_id=1, source_target_pairs={{0,3},{1,0},{2,1},{3,2},{4,7},{5,4},{6,5},{7,6},{8,11},{9,8},{10,9... | collective-permute-start | bytes 326408 | tf_op jit(solution)/shard_map/ppermute | solution.py:196
  13.0 4.6 %conditional.14 = (bf16[1]{0:T(256)(128)(2,1)}) conditional(s32[]{:T(128)} %clamp.2, bf16[1]{0:T(256)(128)(2,1)} %convert_element_type.120, bf16[1]{0:T(256)(128)(2,1)} %convert_element_type.120, bf16[1]{0:T(256)(128)(2,1)} %convert_element_type.120), branch_computations={%region_6.7_spmd, %region_7.8_spmd, %region_8.9_spmd} | conditional | bytes 56
  13.0 2.8 %collective-permute-start.7 = (bf16[1]{0:T(256)(128)(2,1)}, bf16[1]{0:T(256)(128)(2,1)}, u32[]{:S(2)}, u32[]{:S(2)}) collective-permute-start(bf16[1]{0:T(256)(128)(2,1)} %param.7), channel_id=1, source_target_pairs={{0,8},{4,12},{8,16},{12,20},{16,24},{20,28},{24,0},{28,4},{1,9},{5... | collective-permute-start | bytes 14 | tf_op jit(solution)/shard_map/cond/branch_1_fun/ppermute | solution.py:196
  15.8 1.8 %collective-permute-done.7 = bf16[1]{0:T(256)(128)(2,1)} collective-permute-done((bf16[1]{0:T(256)(128)(2,1)}, bf16[1]{0:T(256)(128)(2,1)}, u32[]{:S(2)}, u32[]{:S(2)}) %collective-permute-start.7) | collective-permute-done | bytes 34 | tf_op jit(solution)/shard_map/cond/branch_1_fun/ppermute | solution.py:196
  17.6 1.1 %collective-permute-start.13 = (bf16[170,320]{1,0:T(8,128)(2,1)S(1)}, bf16[170,320]{1,0:T(8,128)(2,1)}, u32[]{:S(2)}, u32[]{:S(2)}) collective-permute-start(bf16[170,320]{1,0:T(8,128)(2,1)S(1)} %slice.49.refs_0_), channel_id=1, source_target_pairs={{0,2},{1,3},{2,0},{3,1},{4,6},{5,7},{6,4},{7,5},{8,10},{9,11},{10,... | collective-permute-start | bytes 326408 | tf_op jit(solution)/shard_map/ppermute | solution.py:196
  18.7 2.3 %collective-permute-done.12.refs_1_ = bf16[170,320]{1,0:T(8,128)(2,1)S(1)} collective-permute-done((bf16[170,320]{1,0:T(8,128)(2,1)S(1)}, bf16[170,320]{1,0:T(8,128)(2,1)S(1)}, u32[]{:S(2)}, u32[]{:S(2)}) %collective-permute-start.12) | collective-permute-done | bytes 108832 | tf_op jit(solution)/shard_map/ppermute | solution.py:196
  21.0 0.7 copy-done.4
  21.7 8.8 %collective-permute-start.14 = (bf16[170,320]{1,0:T(8,128)(2,1)S(1)}, bf16[170,320]{1,0:T(8,128)(2,1)}, u32[]{:S(2)}, u32[]{:S(2)}) collective-permute-start(bf16[170,320]{1,0:T(8,128)(2,1)S(1)} %slice.49.refs_0_), channel_id=1, source_target_pairs={{0,1},{1,2},{2,3},{3,0},{4,5},{5,6},{6,7},{7,4},{8,9},{9,10},{10,1... | collective-permute-start | bytes 326408 | tf_op jit(solution)/shard_map/ppermute | solution.py:196
  30.5 0.2 compare_convert_fusion.same_group_ref
  30.8 1.2 %norm_in.1 = (bf16[576,680]{1,0:T(8,128)(2,1)S(1)}, f32[2,680]{1,0:T(2,128)S(1)}, f32[2,680]{1,0:T(2,128)S(1)}) custom-call(bf16[2,288,680]{2,1,0:T(8,128)(2,1)S(1)} %copy-done, bf16[680,680]{1,0:T(8,128)(2,1)S(1)} %compare_convert_fusion.same_group_ref), custom_call_target="tpu_custom_call" | custom-call | flops 6266880 | bytes 3133440 | tf_op jit(solution)/shard_map/norm_in/pallas_call | solution.py:145
  32.0 1.0 %copy.13 = bf16[576,680]{0,1:T(8,128)(2,1)S(1)} copy(bf16[576,680]{1,0:T(8,128)(2,1)S(1)} %get-tuple-element.61.act_ref) | data formatting | bytes 1566720 | tf_op jit(solution)/shard_map/norm_in/pallas_call | solution.py:145
  33.0 0.1 slice.39.shift_ref
  33.0 1.3 %slice.40.out_grad_ref = bf16[2,288,320]{2,1,0:T(8,128)(2,1)S(1)} slice(bf16[2,288,680]{2,1,0:T(8,128)(2,1)} %param.19), slice={[0:2], [0:288], [360:680]} | slice | bytes 737280 | tf_op jit(solution)/shard_map/slice | solution.py:244
  34.4 0.9 %copy-done.5 = bf16[170,320]{1,0:T(8,128)(2,1)S(1)} copy-done((bf16[170,320]{1,0:T(8,128)(2,1)S(1)}, bf16[170,320]{1,0:T(8,128)(2,1)}, u32[]{:S(2)}) %copy-start.5) | copy-done | bytes 108824
  35.3 4.7 %mix.3 = (bf16[576,320]{1,0:T(8,128)(2,1)S(1)}, bf16[680,320]{1,0:T(8,128)(2,1)S(1)}, f32[170,320]{1,0:T(8,128)S(1)}, bf16[170,320]{1,0:T(8,128)(2,1)S(1)}, bf16...) custom-call(s32[1]{0:T(128)} %bitcast.me_ref, bf16[576,680]{1,0:T(8,128)(2,1)S(1)} %get-tuple-element.61.act_ref, ...), custom_call_target="tpu_custom_call" | custom-call | flops 501350400 | bytes 1474560 | tf_op jit(solution)/shard_map/mix/pallas_call | solution.py:164
  40.0 0.0 copy-start.8
  40.0 0.1 collective-permute-start.20
  40.1 2.7 %collective-permute-start.19 = (bf16[170,320]{1,0:T(8,128)(2,1)S(1)}, bf16[170,320]{1,0:T(8,128)(2,1)S(1)}, u32[]{:S(2)}, u32[]{:S(2)}) collective-permute-start(bf16[170,320]{1,0:T(8,128)(2,1)S(1)} %get-tuple-element.72), channel_id=1, source_target_pairs={{0,2},{1,3},{2,0},{3,1},{4,6},{5,7},{6,4},{7,5},{8,10},{9,11},{10,... | collective-permute-start | bytes 326408 | tf_op jit(solution)/shard_map/ppermute | solution.py:196
  42.9 0.6 slice.46
  43.5 0.6 slice.47
  44.9 0.0 copy-start.1
  45.0 0.6 copy-done.2
  45.6 0.9 %copy-done.3 = bf16[170,360]{1,0:T(8,128)(2,1)S(1)} copy-done((bf16[170,360]{1,0:T(8,128)(2,1)S(1)}, bf16[170,360]{1,0:T(8,128)(2,1)}, u32[]{:S(2)}) %copy-start.3) | copy-done | bytes 122424
  46.5 4.4 %mix.2 = (bf16[576,360]{1,0:T(8,128)(2,1)S(1)}, bf16[680,360]{1,0:T(8,128)(2,1)S(1)}, f32[170,360]{1,0:T(8,128)S(1)}, bf16[170,360]{1,0:T(8,128)(2,1)}, bf16[170...) custom-call(s32[1]{0:T(128)} %bitcast.me_ref, bf16[576,680]{1,0:T(8,128)(2,1)S(1)} %get-tuple-element.61.act_ref, ...), custom_call_target="tpu_custom_call" | custom-call | flops 564019200 | bytes 1658880 | tf_op jit(solution)/shard_map/mix/pallas_call | solution.py:164
  50.9 3.8 %collective-permute-start.17 = (bf16[170,360]{1,0:T(8,128)(2,1)}, bf16[170,360]{1,0:T(8,128)(2,1)S(1)}, u32[]{:S(2)}, u32[]{:S(2)}) collective-permute-start(bf16[170,360]{1,0:T(8,128)(2,1)} %get-tuple-element.69), channel_id=1, source_target_pairs={{0,3},{1,0},{2,1},{3,2},{4,7},{5,4},{6,5},{7,6},{8,11},{9,8},{10,9... | collective-permute-start | bytes 367208 | tf_op jit(solution)/shard_map/ppermute | solution.py:196
  54.7 3.2 %input_grad.1 = bf16[2,288,680]{2,1,0:T(8,128)(2,1)} custom-call(bf16[2,288,680]{2,1,0:T(8,128)(2,1)S(1)} %copy-done.1, f32[2,680]{1,0:T(2,128)S(1)} %get-tuple-element.59.mean_ref, f32[2,680]{1,0:T(2,128)S(1)} %get-tuple-element.60.inverse_ref, bf16[680,680]{1,0:T(8,128)(2,1)S(1)} %compare_convert_fusion.same_group_ref, ...), custom_call_target="tpu_custom_call" | custom-call | flops 532684800 | bytes 3133440 | tf_op jit(solution)/shard_map/input_grad/pallas_call | solution.py:183
  57.9 0.6 collective-permute-start.15
  58.5 0.0 slice-start
  58.5 0.0 slice-start.1
  58.5 0.3 fusion.18
  58.8 6.9 %conditional.13 = (bf16[170,320]{1,0:T(8,128)(2,1)}) conditional(s32[]{:T(128)} %clamp.2, bf16[170,320]{1,0:T(8,128)(2,1)S(1)} %get-tuple-element.83, bf16[170,320]{1,0:T(8,128)(2,1)S(1)} %get-tuple-element.83, bf16[170,320]{1,0:T(8,128)(2,1)S(1)} %get-tuple-element.83), branch_computations={%region_3.4_spmd, %region_4.5_spmd, %region_5.6_spmd} | conditional | bytes 435248
  58.8 1.5 %collective-permute-start.4 = (bf16[170,320]{1,0:T(8,128)(2,1)S(1)}, bf16[170,320]{1,0:T(8,128)(2,1)}, u32[]{:S(2)}, u32[]{:S(2)}) collective-permute-start(bf16[170,320]{1,0:T(8,128)(2,1)S(1)} %param.4), channel_id=1, source_target_pairs={{0,8},{4,12},{8,16},{12,20},{16,24},{20,28},{24,0},{28,4},{1,9},{5... | collective-permute-start | bytes 326408 | tf_op jit(solution)/shard_map/cond/branch_1_fun/ppermute | solution.py:196
  60.4 5.3 %collective-permute-done.4 = bf16[170,320]{1,0:T(8,128)(2,1)} collective-permute-done((bf16[170,320]{1,0:T(8,128)(2,1)S(1)}, bf16[170,320]{1,0:T(8,128)(2,1)}, u32[]{:S(2)}, u32[]{:S(2)}) %collective-permute-start.4) | collective-permute-done | bytes 108832 | tf_op jit(solution)/shard_map/cond/branch_1_fun/ppermute | solution.py:196
  65.7 0.9 %add_multiply_fusion = f32[170,320]{1,0:T(8,128)S(1)} fusion(f32[170,320]{1,0:T(8,128)S(1)} %get-tuple-element.84, bf16[170,320]{1,0:T(8,128)(2,1)} %get-tuple-element.92), kind=kLoop, calls=%fused_computation.21 | loop fusion | flops 163200 | bytes 544000 | tf_op jit(solution)/shard_map/mul | solution.py:263
  66.7 0.3 fusion.14
  67.0 6.1 %conditional.12 = (bf16[170,360]{1,0:T(8,128)(2,1)}) conditional(s32[]{:T(128)} %clamp.2, bf16[170,360]{1,0:T(8,128)(2,1)S(1)} %get-tuple-element.79, bf16[170,360]{1,0:T(8,128)(2,1)S(1)} %get-tuple-element.79, bf16[170,360]{1,0:T(8,128)(2,1)S(1)} %get-tuple-element.79), branch_computations={%region_0.1_spmd, %region_1.2_spmd, %region_2.3_spmd} | conditional | bytes 489648
  67.0 0.7 collective-permute-start.1
  67.6 5.4 %collective-permute-done.1 = bf16[170,360]{1,0:T(8,128)(2,1)} collective-permute-done((bf16[170,360]{1,0:T(8,128)(2,1)S(1)}, bf16[170,360]{1,0:T(8,128)(2,1)}, u32[]{:S(2)}, u32[]{:S(2)}) %collective-permute-start.1) | collective-permute-done | bytes 122432 | tf_op jit(solution)/shard_map/cond/branch_1_fun/ppermute | solution.py:196
  73.0 0.9 %add_multiply_fusion.1 = f32[170,360]{1,0:T(8,128)S(1)} fusion(f32[170,360]{1,0:T(8,128)S(1)} %get-tuple-element.80, bf16[170,360]{1,0:T(8,128)(2,1)} %get-tuple-element.91), kind=kLoop, calls=%fused_computation.23 | loop fusion | flops 183600 | bytes 612000 | tf_op jit(solution)/shard_map/mul | solution.py:263
  74.0 0.2 maximum_bitcast_fusion
  74.2 1.3 %copy.21 = f32[1,170,680]{2,0,1:T(1,128)} copy(f32[1,170,680]{2,1,0:T(8,128)S(1)} %maximum_bitcast_fusion) | data formatting | bytes 924800
  75.5 0.3 maximum_bitcast_fusion.1
  75.7 1.3 %copy.22 = f32[1,170,680]{2,0,1:T(1,128)} copy(f32[1,170,680]{2,1,0:T(8,128)S(1)} %get-tuple-element.89) | data formatting | bytes 924800
  77.1 1.3 %copy.23 = f32[1,170,680]{2,0,1:T(1,128)} copy(f32[1,170,680]{2,1,0:T(8,128)S(1)} %get-tuple-element.90) | data formatting | bytes 924800
  (36 shorter events, 0.2 us)
Async XLA Ops:
  3.2 27.6 %copy-start = (bf16[2,288,680]{2,1,0:T(8,128)(2,1)S(1)}, bf16[2,288,680]{2,1,0:T(8,128)(2,1)}, u32[]{:S(2)}) copy-start(bf16[2,288,680]{2,1,0:T(8,128)(2,1)} %x_ref.3) | copy-start | bytes 2350084
  3.2 39.6 %collective-permute-start.9 = (bf16[170,360]{1,0:T(8,128)(2,1)S(1)}, bf16[170,360]{1,0:T(8,128)(2,1)S(1)}, u32[]{:S(2)}, u32[]{:S(2)}) collective-permute-start(bf16[170,360]{1,0:T(8,128)(2,1)S(1)} %slice.48.refs_0_), channel_id=1, source_target_pairs={{0,3},{1,0},{2,1},{3,2},{4,7},{5,4},{6,5},{7,6},{8,11},{9,8},{10,9... | collective-permute-start | bytes 367208 | tf_op jit(solution)/shard_map/ppermute | solution.py:196
  8.3 36.6 %collective-permute-start.10 = (bf16[170,360]{1,0:T(8,128)(2,1)S(1)}, bf16[170,360]{1,0:T(8,128)(2,1)S(1)}, u32[]{:S(2)}, u32[]{:S(2)}) collective-permute-start(bf16[170,360]{1,0:T(8,128)(2,1)S(1)} %slice.48.refs_0_), channel_id=1, source_target_pairs={{0,2},{1,3},{2,0},{3,1},{4,6},{5,7},{6,4},{7,5},{8,10},{9,11},{10,... | collective-permute-start | bytes 367208 | tf_op jit(solution)/shard_map/ppermute | solution.py:196
  8.3 36.6 %collective-permute-start.11 = (bf16[170,360]{1,0:T(8,128)(2,1)S(1)}, bf16[170,360]{1,0:T(8,128)(2,1)S(1)}, u32[]{:S(2)}, u32[]{:S(2)}) collective-permute-start(bf16[170,360]{1,0:T(8,128)(2,1)S(1)} %slice.48.refs_0_), channel_id=1, source_target_pairs={{0,1},{1,2},{2,3},{3,0},{4,5},{5,6},{6,7},{7,4},{8,9},{9,10},{10,1... | collective-permute-start | bytes 367208 | tf_op jit(solution)/shard_map/ppermute | solution.py:196
  9.4 11.6 %collective-permute-start.12 = (bf16[170,320]{1,0:T(8,128)(2,1)S(1)}, bf16[170,320]{1,0:T(8,128)(2,1)S(1)}, u32[]{:S(2)}, u32[]{:S(2)}) collective-permute-start(bf16[170,320]{1,0:T(8,128)(2,1)S(1)} %slice.49.refs_0_), channel_id=1, source_target_pairs={{0,3},{1,0},{2,1},{3,2},{4,7},{5,4},{6,5},{7,6},{8,11},{9,8},{10,9... | collective-permute-start | bytes 326408 | tf_op jit(solution)/shard_map/ppermute | solution.py:196
  13.0 4.6 %collective-permute-start.7 = (bf16[1]{0:T(256)(128)(2,1)}, bf16[1]{0:T(256)(128)(2,1)}, u32[]{:S(2)}, u32[]{:S(2)}) collective-permute-start(bf16[1]{0:T(256)(128)(2,1)} %param.7), channel_id=1, source_target_pairs={{0,8},{4,12},{8,16},{12,20},{16,24},{20,28},{24,0},{28,4},{1,9},{5... | collective-permute-start | bytes 14 | tf_op jit(solution)/shard_map/cond/branch_1_fun/ppermute | solution.py:196
  17.6 16.7 %collective-permute-start.13 = (bf16[170,320]{1,0:T(8,128)(2,1)S(1)}, bf16[170,320]{1,0:T(8,128)(2,1)}, u32[]{:S(2)}, u32[]{:S(2)}) collective-permute-start(bf16[170,320]{1,0:T(8,128)(2,1)S(1)} %slice.49.refs_0_), channel_id=1, source_target_pairs={{0,2},{1,3},{2,0},{3,1},{4,6},{5,7},{6,4},{7,5},{8,10},{9,11},{10,... | collective-permute-start | bytes 326408 | tf_op jit(solution)/shard_map/ppermute | solution.py:196
  21.0 0.7 copy-start.4
  21.7 12.7 %collective-permute-start.14 = (bf16[170,320]{1,0:T(8,128)(2,1)S(1)}, bf16[170,320]{1,0:T(8,128)(2,1)}, u32[]{:S(2)}, u32[]{:S(2)}) collective-permute-start(bf16[170,320]{1,0:T(8,128)(2,1)S(1)} %slice.49.refs_0_), channel_id=1, source_target_pairs={{0,1},{1,2},{2,3},{3,0},{4,5},{5,6},{6,7},{7,4},{8,9},{9,10},{10,1... | collective-permute-start | bytes 326408 | tf_op jit(solution)/shard_map/ppermute | solution.py:196
  32.0 1.0 %copy-start.10 = (bf16[2,680]{1,0:T(2,128)(2,1)S(1)}, bf16[2,680]{1,0:T(2,128)(2,1)}, u32[]{:S(2)}) copy-start(bf16[2,680]{1,0:T(2,128)(2,1)} %param.18) | copy-start | bytes 8164
  34.4 0.9 %copy-start.5 = (bf16[170,320]{1,0:T(8,128)(2,1)S(1)}, bf16[170,320]{1,0:T(8,128)(2,1)}, u32[]{:S(2)}) copy-start(bf16[170,320]{1,0:T(8,128)(2,1)} %copy-done.4) | copy-start | bytes 326404
  35.3 7.6 %copy-start.9 = (bf16[2,288,680]{2,1,0:T(8,128)(2,1)S(1)}, bf16[2,288,680]{2,1,0:T(8,128)(2,1)}, u32[]{:S(2)}) copy-start(bf16[2,288,680]{2,1,0:T(8,128)(2,1)} %param.19) | copy-start | bytes 2350084
  40.0 2.9 %copy-start.7 = (f32[1,170,680]{2,0,1:T(1,128)S(1)}, f32[1,170,680]{2,0,1:T(1,128)}, u32[]{:S(2)}) copy-start(f32[1,170,680]{2,0,1:T(1,128)} %param.21) | copy-start | bytes 1387204
  40.0 3.5 %copy-start.8 = (f32[1,170,680]{2,0,1:T(1,128)S(1)}, f32[1,170,680]{2,0,1:T(1,128)}, u32[]{:S(2)}) copy-start(f32[1,170,680]{2,0,1:T(1,128)} %param.22) | copy-start | bytes 1387204
  40.0 17.9 %collective-permute-start.20 = (bf16[170,320]{1,0:T(8,128)(2,1)S(1)}, bf16[170,320]{1,0:T(8,128)(2,1)S(1)}, u32[]{:S(2)}, u32[]{:S(2)}) collective-permute-start(bf16[170,320]{1,0:T(8,128)(2,1)S(1)} %get-tuple-element.73), channel_id=1, source_target_pairs={{0,3},{1,0},{2,1},{3,2},{4,7},{5,4},{6,5},{7,6},{8,11},{9,8},{10,9... | collective-permute-start | bytes 326408 | tf_op jit(solution)/shard_map/ppermute | solution.py:196
  40.1 18.4 %collective-permute-start.19 = (bf16[170,320]{1,0:T(8,128)(2,1)S(1)}, bf16[170,320]{1,0:T(8,128)(2,1)S(1)}, u32[]{:S(2)}, u32[]{:S(2)}) collective-permute-start(bf16[170,320]{1,0:T(8,128)(2,1)S(1)} %get-tuple-element.72), channel_id=1, source_target_pairs={{0,2},{1,3},{2,0},{3,1},{4,6},{5,7},{6,4},{7,5},{8,10},{9,11},{10,... | collective-permute-start | bytes 326408 | tf_op jit(solution)/shard_map/ppermute | solution.py:196
  42.8 15.7 %collective-permute-start.18 = (bf16[170,320]{1,0:T(8,128)(2,1)S(1)}, bf16[170,320]{1,0:T(8,128)(2,1)S(1)}, u32[]{:S(2)}, u32[]{:S(2)}) collective-permute-start(bf16[170,320]{1,0:T(8,128)(2,1)S(1)} %get-tuple-element.71), channel_id=1, source_target_pairs={{0,1},{1,2},{2,3},{3,0},{4,5},{5,6},{6,7},{7,4},{8,9},{9,10},{10,1... | collective-permute-start | bytes 326408 | tf_op jit(solution)/shard_map/ppermute | solution.py:196
  44.9 9.8 %copy-start.1 = (bf16[2,288,680]{2,1,0:T(8,128)(2,1)S(1)}, bf16[2,288,680]{2,1,0:T(8,128)(2,1)}, u32[]{:S(2)}) copy-start(bf16[2,288,680]{2,1,0:T(8,128)(2,1)} %x_ref.3) | copy-start | bytes 2350084
  45.0 0.7 copy-start.2
  45.6 0.9 %copy-start.3 = (bf16[170,360]{1,0:T(8,128)(2,1)S(1)}, bf16[170,360]{1,0:T(8,128)(2,1)}, u32[]{:S(2)}) copy-start(bf16[170,360]{1,0:T(8,128)(2,1)} %copy-done.2) | copy-start | bytes 367204
  50.9 15.7 %collective-permute-start.17 = (bf16[170,360]{1,0:T(8,128)(2,1)}, bf16[170,360]{1,0:T(8,128)(2,1)S(1)}, u32[]{:S(2)}, u32[]{:S(2)}) collective-permute-start(bf16[170,360]{1,0:T(8,128)(2,1)} %get-tuple-element.69), channel_id=1, source_target_pairs={{0,3},{1,0},{2,1},{3,2},{4,7},{5,4},{6,5},{7,6},{8,11},{9,8},{10,9... | collective-permute-start | bytes 367208 | tf_op jit(solution)/shard_map/ppermute | solution.py:196
  54.7 11.9 %collective-permute-start.16 = (bf16[170,360]{1,0:T(8,128)(2,1)}, bf16[170,360]{1,0:T(8,128)(2,1)S(1)}, u32[]{:S(2)}, u32[]{:S(2)}) collective-permute-start(bf16[170,360]{1,0:T(8,128)(2,1)} %get-tuple-element.68), channel_id=1, source_target_pairs={{0,2},{1,3},{2,0},{3,1},{4,6},{5,7},{6,4},{7,5},{8,10},{9,11},{10,... | collective-permute-start | bytes 367208 | tf_op jit(solution)/shard_map/ppermute | solution.py:196
  54.7 3.7 %copy-start.6 = (f32[1,170,680]{2,1,0:T(8,128)S(1)}, f32[1,170,680]{2,1,0:T(8,128)}, u32[]{:S(2)}) copy-start(f32[1,170,680]{2,1,0:T(8,128)} %get-tuple-element.87) | copy-start | bytes 1387204
  57.9 8.8 %collective-permute-start.15 = (bf16[170,360]{1,0:T(8,128)(2,1)}, bf16[170,360]{1,0:T(8,128)(2,1)S(1)}, u32[]{:S(2)}, u32[]{:S(2)}) collective-permute-start(bf16[170,360]{1,0:T(8,128)(2,1)} %get-tuple-element.67), channel_id=1, source_target_pairs={{0,1},{1,2},{2,3},{3,0},{4,5},{5,6},{6,7},{7,4},{8,9},{9,10},{10,1... | collective-permute-start | bytes 367208 | tf_op jit(solution)/shard_map/ppermute | solution.py:196
  58.5 8.2 %slice-start = ((f32[1,170,680]{2,0,1:T(1,128)}), f32[1,170,360]{2,0,1:T(1,128)S(1)}, s32[]{:S(2)}) async-start(f32[1,170,680]{2,0,1:T(1,128)} %param.21), calls=%async_computation | async-start | bytes 522240 | tf_op jit(solution)/shard_map/slice | solution.py:258
  58.5 8.2 %slice-start.1 = ((f32[1,170,680]{2,0,1:T(1,128)}), f32[1,170,360]{2,0,1:T(1,128)S(1)}, s32[]{:S(2)}) async-start(f32[1,170,680]{2,0,1:T(1,128)} %param.22), calls=%async_computation.1 | async-start | bytes 522240 | tf_op jit(solution)/shard_map/slice | solution.py:259
  58.8 6.9 %collective-permute-start.4 = (bf16[170,320]{1,0:T(8,128)(2,1)S(1)}, bf16[170,320]{1,0:T(8,128)(2,1)}, u32[]{:S(2)}, u32[]{:S(2)}) collective-permute-start(bf16[170,320]{1,0:T(8,128)(2,1)S(1)} %param.4), channel_id=1, source_target_pairs={{0,8},{4,12},{8,16},{12,20},{16,24},{20,28},{24,0},{28,4},{1,9},{5... | collective-permute-start | bytes 326408 | tf_op jit(solution)/shard_map/cond/branch_1_fun/ppermute | solution.py:196
  67.0 6.1 %collective-permute-start.1 = (bf16[170,360]{1,0:T(8,128)(2,1)S(1)}, bf16[170,360]{1,0:T(8,128)(2,1)}, u32[]{:S(2)}, u32[]{:S(2)}) collective-permute-start(bf16[170,360]{1,0:T(8,128)(2,1)S(1)} %param.1), channel_id=1, source_target_pairs={{0,8},{4,12},{8,16},{12,20},{16,24},{20,28},{24,0},{28,4},{1,9},{5... | collective-permute-start | bytes 367208 | tf_op jit(solution)/shard_map/cond/branch_1_fun/ppermute | solution.py:196

commit v2 on v1

v2 whole, which is shorter than its diff:
```python
import functools

import jax
import jax.numpy as jnp
from jax import lax
from jax.experimental import pallas as pl
from jax.experimental.pallas import tpu as pltpu
from jax.sharding import PartitionSpec as P

GSIZE = 40

NORM_EPS = 1e-05
BETA_ONE = 0.9
BETA_TWO = 0.999
LEARN_RATE = 0.002
ADAM_EPS = 1e-08

LANES = 128
TILE_ROWS = 16
VMEM_BYTES = 20 * 1024 * 1024


def padded(rows):
    return -(-rows // TILE_ROWS) * TILE_ROWS


class Packing:
    def __init__(self, rows, start, stop):
        self.rows, self.start, self.stop = rows, start, stop
        self.columns = stop - start
        self.deep = padded(rows)
        self.tiles, self.rest = divmod(self.columns, LANES)
        fold = LANES // self.rest if self.rest else 1
        self.fold_rows = padded(-(-self.deep // fold))
        self.folds = [
            (first, min(self.fold_rows, self.deep - first)) for first in range(0, self.deep, self.fold_rows)
        ]
        self.height = self.tiles * self.deep + (self.fold_rows if self.rest else 0)

    def write(self, ref, block):
        for tile in range(self.tiles):
            ref[tile * self.deep : (tile + 1) * self.deep, :] = block[
                :, tile * LANES : (tile + 1) * LANES
            ].astype(ref.dtype)
        if self.rest:
            left = block[:, self.tiles * LANES :]
            parts = []
            for first, count in self.folds:
                part = left[first : first + count]
                if count < self.fold_rows:
                    part = jnp.concatenate(
                        [part, jnp.zeros((self.fold_rows - count, self.rest), part.dtype)], axis=0
                    )
                parts.append(part)
            spare = LANES - self.rest * len(parts)
            if spare:
                parts.append(jnp.zeros((self.fold_rows, spare), left.dtype))
            ref[self.tiles * self.deep :, :] = jnp.concatenate(parts, axis=1).astype(ref.dtype)

    def read(self, ref):
        pieces = [
            ref[tile * self.deep : (tile + 1) * self.deep, :].astype(jnp.float32) for tile in range(self.tiles)
        ]
        if self.rest:
            left = ref[self.tiles * self.deep :, :].astype(jnp.float32)
            parts = [
                left[:count, i * self.rest : (i + 1) * self.rest] for i, (_, count) in enumerate(self.folds)
            ]
            pieces.append(jnp.concatenate(parts, axis=0) if len(parts) > 1 else parts[0])
        return jnp.concatenate(pieces, axis=1) if len(pieces) > 1 else pieces[0]

    def payload(self):
        return jax.ShapeDtypeStruct((self.height, LANES), jnp.bfloat16)

    def block(self):
        return jax.ShapeDtypeStruct((self.deep, self.columns), jnp.float32)


def group_sums(rows, same_group):
    high = rows.astype(jnp.bfloat16).astype(jnp.float32)
    rest = rows - high
    middle = rest.astype(jnp.bfloat16).astype(jnp.float32)
    count = rows.shape[0]
    stacked = jnp.concatenate([high, middle, rest - middle], axis=0).astype(jnp.bfloat16)
    sums = jnp.dot(stacked, same_group, preferred_element_type=jnp.float32)
    return sums[:count] + (sums[count : 2 * count] + sums[2 * count :])


def position_sums(parts):
    return jnp.concatenate([jnp.sum(part, axis=0, keepdims=True) for part in parts], axis=0)


def sigmoid(values):
    return 0.5 * jnp.tanh(0.5 * values) + 0.5


def silu_grad(values):
    gate = sigmoid(values)
    return gate * (1.0 + values * (1.0 - gate))


def cast_kernel(packs, push_ref, params_ref, *refs):
    out_refs, rows_ref = refs[:-1], refs[-1]
    rows = params_ref.shape[0]
    rows_ref[rows // 8 * 8 :, :] = jnp.zeros((rows_ref.shape[0] - rows // 8 * 8, rows_ref.shape[1]), jnp.float32)
    rows_ref[:rows, :] = params_ref[:, 0, :] / push_ref[0]
    for pack, out_ref in zip(packs, out_refs):
        pack.write(out_ref, rows_ref[:, pack.start : pack.stop])


def norm_in_kernel(shards, me_ref, x_ref, same_group_ref, act_ref, mean_ref, inverse_ref):
    samples, positions, channels = x_ref.shape
    rows = channels // shards
    deep = act_ref.shape[0] // shards
    entries = positions * GSIZE
    same_group = same_group_ref[...]
    parts = [x_ref[i].astype(jnp.float32) for i in range(samples)]
    mean = group_sums(position_sums(parts), same_group) / entries
    centered = [parts[i] - mean[i : i + 1] for i in range(samples)]
    variance = group_sums(position_sums([part * part for part in centered]), same_group) / entries
    inverse = lax.rsqrt(variance + NORM_EPS)
    mean_ref[...] = mean
    inverse_ref[...] = inverse
    normed = [centered[i] * inverse[i : i + 1] for i in range(samples)]
    act = jnp.concatenate([part * sigmoid(part) for part in normed], axis=0)
    turned = pltpu.roll(act.T, channels - me_ref[0] * rows, 0)
    act_ref[...] = jnp.zeros_like(act_ref)
    for slot in range(shards):
        act_ref[slot * deep : slot * deep + rows, :] = turned[slot * rows : (slot + 1) * rows].astype(jnp.bfloat16)


def mix_kernel(shards, pack, act_ref, shift_ref, out_grad_ref, same_group_ref, *refs):
    weight_refs, token_ref, refs = refs[:shards], refs[shards], refs[shards + 1 :]
    grad_hidden_ref, own_ref = refs[:2]
    send_refs, weight_ref = refs[2 : 1 + shards], refs[1 + shards]
    samples, positions, columns = out_grad_ref.shape
    entries = positions * GSIZE
    deep = pack.deep
    for slot, shard_ref in enumerate(weight_refs):
        weight_ref[slot * deep : (slot + 1) * deep, :] = pack.read(shard_ref).astype(jnp.bfloat16)
    same_group = same_group_ref[:columns, :columns]
    hidden = lax.dot_general(
        act_ref[...], weight_ref[...], (((0,), (0,)), ((), ())), preferred_element_type=jnp.float32
    )
    parts = [
        hidden[i * positions : (i + 1) * positions] + shift_ref[i : i + 1, :].astype(jnp.float32)
        for i in range(samples)
    ]
    mean = group_sums(position_sums(parts), same_group) / entries
    parts = [parts[i] - mean[i : i + 1] for i in range(samples)]
    variance = group_sums(position_sums([part * part for part in parts]), same_group) / entries
    inverse = lax.rsqrt(variance + NORM_EPS)
    normed = [parts[i] * inverse[i : i + 1] for i in range(samples)]
    grads = [out_grad_ref[i].astype(jnp.float32) * silu_grad(normed[i]) for i in range(samples)]
    means = group_sums(
        jnp.concatenate(
            [position_sums(grads), position_sums([g * n for g, n in zip(grads, normed)])], axis=0
        ),
        same_group,
    ) / entries
    for i in range(samples):
        first, second = means[i : i + 1], means[samples + i : samples + i + 1]
        grad_hidden_ref[i * positions : (i + 1) * positions, :] = (
            inverse[i : i + 1] * (grads[i] - first - normed[i] * second)
        ).astype(jnp.bfloat16)
    grad = jnp.dot(act_ref[...], grad_hidden_ref[...], preferred_element_type=jnp.float32)
    for slot, send_ref in enumerate(send_refs, 1):
        pack.write(send_ref, grad[slot * deep : (slot + 1) * deep])
    own_ref[...] = grad[:deep]


def input_grad_kernel(shards, packs, me_ref, x_ref, mean_ref, inverse_ref, same_group_ref, *refs):
    grad_refs, refs = refs[: len(packs)], refs[len(packs) :]
    weight_refs, out_ref, rows_ref = refs[:-2], refs[-2], refs[-1]
    samples, positions, channels = x_ref.shape
    entries = positions * GSIZE
    rows = channels // shards
    grad_act = 0.0
    for index, (pack, grad_ref) in enumerate(zip(packs, grad_refs)):
        for slot in range(shards):
            block = pack.read(weight_refs[index * shards + slot])
            rows_ref[slot * rows : (slot + 1) * rows, : pack.columns] = block[:rows]
        weight = pltpu.roll(rows_ref[:, : pack.columns], me_ref[0] * rows, 0).astype(jnp.bfloat16)
        grad_act += lax.dot_general(
            grad_ref[...], weight, (((1,), (1,)), ((), ())), preferred_element_type=jnp.float32
        )
    inverse = inverse_ref[...]
    normed = [
        (x_ref[i].astype(jnp.float32) - mean_ref[i : i + 1, :]) * inverse[i : i + 1] for i in range(samples)
    ]
    grads = [grad_act[i * positions : (i + 1) * positions] * silu_grad(normed[i]) for i in range(samples)]
    means = group_sums(
        jnp.concatenate(
            [position_sums(grads), position_sums([g * n for g, n in zip(grads, normed)])], axis=0
        ),
        same_group_ref[...],
    ) / entries
    for i in range(samples):
        first, second = means[i : i + 1], means[samples + i : samples + i + 1]
        out_ref[i] = (inverse[i : i + 1] * (grads[i] - first - normed[i] * second)).astype(jnp.bfloat16)


def adam_kernel(shards, pack, scales_ref, own_ref, *refs):
    other_refs, refs = refs[: shards - 1], refs[shards - 1 :]
    params_ref, first_ref, second_ref, token_ref, grad_ref, moved_ref, sent_ref = refs
    rows = pack.rows
    total = own_ref[...]
    for other_ref in other_refs:
        total = total + pack.read(other_ref)
    grad_ref[...] = total / shards
    grad = grad_ref[:rows, :]
    columns = slice(pack.start, pack.stop)
    first_new = BETA_ONE * first_ref[:, 0, columns] + (1.0 - BETA_ONE) * grad
    second_new = BETA_TWO * second_ref[:, 0, columns] + (1.0 - BETA_TWO) * grad * grad
    update = (scales_ref[0] * first_new) / (jnp.sqrt(second_new * scales_ref[1]) + ADAM_EPS)
    if rows < pack.deep:
        moved_ref[rows // 8 * 8 :, :] = jnp.zeros((pack.deep - rows // 8 * 8, pack.columns), jnp.float32)
    moved_ref[:rows, :] = params_ref[:, 0, columns] - update
    pack.write(sent_ref, moved_ref[...])


def moments_kernel(packs, first_ref, second_ref, *refs):
    grad_refs, (first_out, second_out) = refs[: len(packs)], refs[len(packs) :]
    rows = first_ref.shape[0]
    grad = jnp.concatenate([grad_ref[:rows, :] for grad_ref in grad_refs], axis=1)
    first_out[:, 0, :] = BETA_ONE * first_ref[:, 0, :] + (1.0 - BETA_ONE) * grad
    second_out[:, 0, :] = BETA_TWO * second_ref[:, 0, :] + (1.0 - BETA_TWO) * grad * grad


def average_kernel(packs, *refs):
    moved_refs, other_refs, out_ref = refs[: len(packs)], refs[len(packs) : -1], refs[-1]
    rows = out_ref.shape[0]
    pieces = [
        0.5 * (moved_ref[...] + pack.read(other_ref))
        for pack, moved_ref, other_ref in zip(packs, moved_refs, other_refs)
    ]
    out_ref[:, 0, :] = jnp.concatenate(pieces, axis=1)[:rows]


SCALARS = pl.BlockSpec(memory_space=pltpu.SMEM)
BLOCKS = pl.BlockSpec(memory_space=pltpu.VMEM)
TOKEN = pl.BlockSpec(memory_space=pl.ANY)


def call(kernel, name, outs, specs, operands, scratch=(), flops=0, elements=0):
    return pl.pallas_call(
        kernel,
        out_shape=outs,
        in_specs=specs,
        out_specs=jax.tree.map(lambda _: BLOCKS, outs),
        scratch_shapes=list(scratch),
        compiler_params=pltpu.CompilerParams(vmem_limit_bytes=VMEM_BYTES),
        cost_estimate=pl.CostEstimate(flops=flops, bytes_accessed=8 * elements, transcendentals=elements),
        name=name,
    )(*operands)


def moved_on(block, axis, distance):
    size = lax.axis_size(axis)
    return lax.ppermute(block, axis, [(i, (i + distance) % size) for i in range(size)])


def column_cuts(channels):
    half = (channels // GSIZE + 1) // 2 * GSIZE
    return [(0, half), (half, channels)]


def local(
    block_input, time_shift, out_grad, params, first_moment, second_moment, push_weight, step
):
    samples, positions, channels = block_input.shape
    tokens = samples * positions
    shards = lax.axis_size("dp")
    rows = params.shape[1]
    deep = padded(rows)
    me = lax.axis_index("dp").astype(jnp.int32).reshape(1)
    packs = [Packing(rows, start, stop) for start, stop in column_cuts(channels)]
    params, first_moment, second_moment = (
        jnp.transpose(array, (1, 0, 2)) for array in (params, first_moment, second_moment)
    )
    group_of = jnp.arange(channels, dtype=jnp.int32) // GSIZE
    same_group = (group_of[:, None] == group_of[None, :]).astype(jnp.bfloat16)

    shard_list = call(
        functools.partial(cast_kernel, packs),
        "cast",
        tuple(pack.payload() for pack in packs),
        [SCALARS, BLOCKS],
        (push_weight, params),
        scratch=[pltpu.VMEM((deep, channels), jnp.float32)],
        elements=rows * channels,
    )
    weights = [
        [piece] + [moved_on(piece, "dp", -slot) for slot in range(1, shards)] for piece in shard_list
    ]

    level_count = lax.axis_size("replica").bit_length() - 1
    distance_bits = step[0] % level_count
    step_count = (step[0] + 1).astype(jnp.float32)
    scales = jnp.stack(
        [LEARN_RATE / (1.0 - jnp.power(BETA_ONE, step_count)), 1.0 / (1.0 - jnp.power(BETA_TWO, step_count))]
    )

    activation, mean_in, inverse_in = call(
        functools.partial(norm_in_kernel, shards),
        "norm_in",
        (
            jax.ShapeDtypeStruct((shards * deep, tokens), jnp.bfloat16),
            jax.ShapeDtypeStruct((samples, channels), jnp.float32),
            jax.ShapeDtypeStruct((samples, channels), jnp.float32),
        ),
        [SCALARS, BLOCKS, BLOCKS],
        (me, block_input, same_group),
        elements=tokens * channels,
    )

    hidden_grads, owns, arrived = [], [], []
    token = mean_in
    for pack, pieces in zip(packs, weights):
        columns = slice(pack.start, pack.stop)
        grad_hidden, own, *sends = call(
            functools.partial(mix_kernel, shards, pack),
            "mix",
            (jax.ShapeDtypeStruct((tokens, pack.columns), jnp.bfloat16), pack.block())
            + (pack.payload(),) * (shards - 1),
            [BLOCKS] * (4 + shards) + [TOKEN],
            (activation, time_shift[:, columns], out_grad[:, :, columns], same_group, *pieces, token),
            scratch=[pltpu.VMEM((shards * deep, pack.columns), jnp.bfloat16)],
            flops=4 * tokens * channels * pack.columns,
            elements=tokens * pack.columns,
        )
        token = own
        hidden_grads.append(grad_hidden)
        owns.append(own)
        arrived.append([moved_on(send, "dp", slot) for slot, send in enumerate(sends, 1)])

    grad_input = call(
        functools.partial(input_grad_kernel, shards, packs),
        "input_grad",
        jax.ShapeDtypeStruct(block_input.shape, jnp.bfloat16),
        [SCALARS] + [BLOCKS] * (4 + len(packs) * (1 + shards)),
        (me, block_input, mean_in, inverse_in, same_group, *hidden_grads, *weights[0], *weights[1]),
        scratch=[pltpu.VMEM((channels, max(pack.columns for pack in packs)), jnp.float32)],
        flops=2 * tokens * channels * channels,
        elements=tokens * channels,
    )

    def adam(pack, own, others, token):
        return call(
            functools.partial(adam_kernel, shards, pack),
            "adam",
            (pack.block(), pack.block(), pack.payload()),
            [SCALARS] + [BLOCKS] * (3 + shards) + [TOKEN],
            (scales, own, *others, params, first_moment, second_moment, token),
            elements=rows * pack.columns,
        )

    def moments(*grads):
        return call(
            functools.partial(moments_kernel, packs),
            "moments",
            (jax.ShapeDtypeStruct(params.shape, jnp.float32),) * 2,
            [BLOCKS] * (2 + len(packs)),
            (first_moment, second_moment, *grads),
            elements=rows * channels,
        )

    def from_behind(finish, *operands):
        def branch(distance):
            return lambda *values: finish(lambda block: moved_on(block, "replica", distance), *values)

        return lax.switch(distance_bits, [branch(1 << power) for power in range(level_count)], *operands)

    grad_a, moved_a, sent_a = adam(packs[0], owns[0], arrived[0], token)
    other_a, other_weight = from_behind(
        lambda move, sent, weight: (move(sent), move(weight)), sent_a, push_weight.astype(jnp.bfloat16)
    )
    grad_b, moved_b, sent_b = adam(packs[1], owns[1], arrived[1], other_a)
    other_b, first_new, second_new = from_behind(
        lambda move, sent, *grads: (move(sent), *moments(*grads)), sent_b, grad_a, grad_b
    )
    averaged = call(
        functools.partial(average_kernel, packs),
        "average",
        jax.ShapeDtypeStruct(params.shape, jnp.float32),
        [BLOCKS] * (2 * len(packs)),
        (moved_a, moved_b, other_a, other_b),
        elements=rows * channels,
    )
    new_weight = 0.5 * (push_weight + other_weight.astype(jnp.float32))
    return (
        grad_input,
        *(jnp.transpose(array, (1, 0, 2)) for array in (averaged, first_new, second_new)),
        new_weight,
    )


def solution(mesh):
    placed = (
        P(("replica", "dp"), None, None),
        P(("replica", "dp"), None),
        P(("replica", "dp"), None, None),
        P("replica", "dp", None),
        P("replica", "dp", None),
        P("replica", "dp", None),
        P("replica"),
        P(),
    )
    return jax.shard_map(
        local,
        mesh=mesh,
        in_specs=placed,
        out_specs=(
            P(("replica", "dp"), None, None),
            P("replica", "dp", None),
            P("replica", "dp", None),
            P("replica", "dp", None),
            P("replica"),
        ),
        check_vma=False,
    )
```

time: 79.2 us -> 72.1 us (0.910)
  Pallas kernels: 13.5 us -> 21.7 us
  starting transfers between devices: 31.2 us -> 25 us
  other arithmetic: 5.02 us -> 0.32 us
  local copies, waits for them, and re-layouts: 10.8 us -> 7.8 us
  waiting for transfers between devices: 14.8 us -> 13.2 us
    pallas_call x4 -> x9, Pallas kernels: 13.5 us -> 21.7 us  [call(): pl.pallas_call(kernel, out_shape=outs, in_specs=specs, out_specs=jax.tree...]
    ppermute x15, starting transfers between devices: 31.2 us -> 25 us  [moved_on(): lax.ppermute(block, axis, [(i, (i + distance) % size) for i in range(size)])]
    unnamed x1 -> x0, other arithmetic: 1.9 us -> none
    mul x2 -> x0, other arithmetic: 1.88 us -> none  [local(): 0.5 * (moved + neighbour.astype(jnp.float32))]
    ppermute x15, waiting for transfers between devices: 14.8 us -> 13.2 us  [moved_on(): lax.ppermute(block, axis, [(i, (i + distance) % size) for i in range(size)])]
    unnamed x25 -> x58, local copies, waits for them, and re-layouts: 7.13 us -> 5.77 us
    pallas_call x1 -> x0, local copies, waits for them, and re-layouts: 0.96 us -> none  [norm_in(): pl.pallas_call(norm_in_kernel, out_shape=(jax.ShapeDtypeStruct((samples *...]
    slice x12 -> x4, local copies, waits for them, and re-layouts: 2.74 us -> 2.03 us  [the longest x2 1.27 us: local(): out_grad[:, :, columns]]
  transfers between devices with their start and end apart: 15 -> 15, of which waited for: 4 -> 3; matrix products, arithmetic and copies ran while one was open for 6% -> 3% of each run, Pallas kernels for 17% -> 26%
where the time goes in v2:
time: 72.1 us; the launch traced here: 72.3 us
  starting transfers between devices  25 us (35%)
  Pallas kernels  21.7 us (30%)
  waiting for transfers between devices  13.2 us (18%)
  local copies, waits for them, and re-layouts  7.8 us (11%)
  between operations  4.27 us (6%)
    ppermute x15, starting transfers between devices, moved_on(): lax.ppermute(block, axis, [(i, (i + distance) % size) for i in range(size)])  25 us
    pallas_call x9, Pallas kernels, call(): pl.pallas_call(kernel, out_shape=outs, in_specs=specs, out_specs=jax.tree...  21.7 us
    ppermute x15, waiting for transfers between devices, moved_on(): lax.ppermute(block, axis, [(i, (i + distance) % size) for i in range(size)])  13.2 us
    unnamed x58, local copies, waits for them, and re-layouts  5.77 us
  transfers between devices with their start and end apart: 15, of which 3 were waited for; matrix products, arithmetic and copies ran while one was open for 3% of the time, Pallas kernels for 26%

profile of v2, /device:TPU:0, one launch (start us, length us, event | category | flops | bytes accessed | tf_op | source)
XLA Modules:
  0.0 72.3 jit_solution(2703566544526674601)
XLA Ops:
  1.3 0.0 copy-start
  1.3 1.0 %copy-done = f32[1,170,680]{2,0,1:T(1,128)S(1)} copy-done((f32[1,170,680]{2,0,1:T(1,128)S(1)}, f32[1,170,680]{2,0,1:T(1,128)}, u32[]{:S(2)}) %copy-start) | copy-done | bytes 462424
  2.3 0.3 cast.1
  2.6 0.0 copy-start.6
  2.6 5.1 %collective-permute-start.9 = (bf16[528,128]{1,0:T(8,128)(2,1)S(1)}, bf16[528,128]{1,0:T(8,128)(2,1)S(1)}, u32[]{:S(2)}, u32[]{:S(2)}) collective-permute-start(bf16[528,128]{1,0:T(8,128)(2,1)S(1)} %get-tuple-element.111.refs_0_.refs_2_), channel_id=1, source_target_pairs={{0,3},{1,0},{2,1},{3,2},{4,7},{5,4},{6,5},{7,6},{8,11},{9,8},{10,9... | collective-permute-start | bytes 405512 | tf_op jit(solution)/shard_map/ppermute | solution.py:260
  7.7 1.0 %collective-permute-start.11 = (bf16[528,128]{1,0:T(8,128)(2,1)S(1)}, bf16[528,128]{1,0:T(8,128)(2,1)S(1)}, u32[]{:S(2)}, u32[]{:S(2)}) collective-permute-start(bf16[528,128]{1,0:T(8,128)(2,1)S(1)} %get-tuple-element.111.refs_0_.refs_2_), channel_id=1, source_target_pairs={{0,1},{1,2},{2,3},{3,0},{4,5},{5,6},{6,7},{7,4},{8,9},{9,10},{10,1... | collective-permute-start | bytes 405512 | tf_op jit(solution)/shard_map/ppermute | solution.py:260
  8.7 2.8 %collective-permute-start.12 = (bf16[448,128]{1,0:T(8,128)(2,1)S(1)}, bf16[448,128]{1,0:T(8,128)(2,1)}, u32[]{:S(2)}, u32[]{:S(2)}) collective-permute-start(bf16[448,128]{1,0:T(8,128)(2,1)S(1)} %get-tuple-element.113.refs_0_.refs_6_), channel_id=1, source_target_pairs={{0,3},{1,0},{2,1},{3,2},{4,7},{5,4},{6,5},{7,6},{8,11},{9,8},{10,9... | collective-permute-start | bytes 344072 | tf_op jit(solution)/shard_map/ppermute | solution.py:260
  11.5 1.1 %collective-permute-start.13 = (bf16[448,128]{1,0:T(8,128)(2,1)S(1)}, bf16[448,128]{1,0:T(8,128)(2,1)}, u32[]{:S(2)}, u32[]{:S(2)}) collective-permute-start(bf16[448,128]{1,0:T(8,128)(2,1)S(1)} %get-tuple-element.113.refs_0_.refs_6_), channel_id=1, source_target_pairs={{0,2},{1,3},{2,0},{3,1},{4,6},{5,7},{6,4},{7,5},{8,10},{9,11},{10,... | collective-permute-start | bytes 344072 | tf_op jit(solution)/shard_map/ppermute | solution.py:260
  12.7 0.7 slice.12.shift_ref
  13.4 1.1 %slice.13.out_grad_ref = bf16[2,288,360]{2,1,0:T(8,128)(2,1)S(1)} slice(bf16[2,288,680]{2,1,0:T(8,128)(2,1)} %param.16), slice={[0:2], [0:288], [0:360]} | slice | bytes 829440 | tf_op jit(solution)/shard_map/slice | solution.py:327
  14.4 0.2 compare_convert_fusion.same_group_ref
  14.7 2.0 %norm_in.1 = (bf16[704,576]{1,0:T(8,128)(2,1)S(1)}, f32[2,680]{1,0:T(2,128)S(1)}, f32[2,680]{1,0:T(2,128)S(1)}) custom-call(s32[1]{0:T(128)} %bitcast.me_ref, bf16[2,288,680]{2,1,0:T(8,128)(2,1)S(1)} %copy-done.2, bf16[680,680]{1,0:T(8,128)(2,1)S(1)} %compare_convert_fusion.same_group_ref), custom_call_target="tpu_custom_call" | custom-call | bytes 3133440 | tf_op jit(solution)/shard_map/norm_in/pallas_call | solution.py:246
  16.8 0.1 collective-permute-start.14
  16.8 8.1 %collective-permute-done.10.refs_2_.refs_4_ = bf16[528,128]{1,0:T(8,128)(2,1)S(1)} collective-permute-done((bf16[528,128]{1,0:T(8,128)(2,1)S(1)}, bf16[528,128]{1,0:T(8,128)(2,1)S(1)}, u32[]{:S(2)}, u32[]{:S(2)}) %collective-permute-start.10) | collective-permute-done | bytes 135200 | tf_op jit(solution)/shard_map/ppermute | solution.py:260
  24.9 0.0 copy-start.28
  24.9 0.0 copy-start.27
  24.9 3.4 %mix.2 = (bf16[576,360]{1,0:T(8,128)(2,1)S(1)}, f32[176,360]{1,0:T(8,128)S(1)}, bf16[528,128]{1,0:T(8,128)(2,1)}, bf16[528,128]{1,0:T(8,128)(2,1)S(1)}, bf16[528,128]{1,0:T(8,128)(2,1)S(1)}) custom-call(bf16[704,576]{1,0:T(8,128)(2,1)S(1)} %get-tuple-element.110.act_ref, bf16[2,360]{1,0:T(2,128)(2,1)S(1)} %slice.12.shift_ref, ...), custom_call_target="tpu_custom_call" | custom-call | flops 564019200 | bytes 1658880 | tf_op jit(solution)/shard_map/mix/pallas_call | solution.py:246
  28.4 0.0 copy-start.3
  28.4 0.7 copy-done.3
  29.1 0.8 %copy-done.17 = bf16[576,360]{1,0:T(8,128)(2,1)} copy-done((bf16[576,360]{1,0:T(8,128)(2,1)}, bf16[576,360]{1,0:T(8,128)(2,1)S(1)}, u32[]{:S(2)}) %copy-start.17) | copy-done | bytes 414744
  29.9 0.6 copy-done.21
  30.5 0.7 copy-done.22
  31.2 0.9 %collective-permute-start.15 = (bf16[528,128]{1,0:T(8,128)(2,1)}, bf16[528,128]{1,0:T(8,128)(2,1)}, u32[]{:S(2)}, u32[]{:S(2)}) collective-permute-start(bf16[528,128]{1,0:T(8,128)(2,1)} %get-tuple-element.116), channel_id=1, source_target_pairs={{0,1},{1,2},{2,3},{3,0},{4,5},{5,6},{6,7},{7,4},{8,9},{9,10},{10,1... | collective-permute-start | bytes 405512 | tf_op jit(solution)/shard_map/ppermute | solution.py:260
  32.1 0.1 slice.14.shift_ref
  32.1 0.2 slice.15.out_grad_ref
  33.2 2.0 %collective-permute-start.16 = (bf16[528,128]{1,0:T(8,128)(2,1)}, bf16[528,128]{1,0:T(8,128)(2,1)S(1)}, u32[]{:S(2)}, u32[]{:S(2)}) collective-permute-start(bf16[528,128]{1,0:T(8,128)(2,1)} %copy-done.22), channel_id=1, source_target_pairs={{0,2},{1,3},{2,0},{3,1},{4,6},{5,7},{6,4},{7,5},{8,10},{9,11},{10,... | collective-permute-start | bytes 405512 | tf_op jit(solution)/shard_map/ppermute | solution.py:260
  35.2 2.9 %collective-permute-start.17 = (bf16[528,128]{1,0:T(8,128)(2,1)}, bf16[528,128]{1,0:T(8,128)(2,1)S(1)}, u32[]{:S(2)}, u32[]{:S(2)}) collective-permute-start(bf16[528,128]{1,0:T(8,128)(2,1)} %copy-done.21), channel_id=1, source_target_pairs={{0,3},{1,0},{2,1},{3,2},{4,7},{5,4},{6,5},{7,6},{8,11},{9,8},{10,9... | collective-permute-start | bytes 405512 | tf_op jit(solution)/shard_map/ppermute | solution.py:260
  38.1 0.9 %copy-done.4 = f32[176,360]{1,0:T(8,128)S(1)} copy-done((f32[176,360]{1,0:T(8,128)S(1)}, f32[176,360]{1,0:T(8,128)}, u32[]{:S(2)}) %copy-start.4) | copy-done | bytes 253464
  39.1 0.9 %copy-done.15 = bf16[448,128]{1,0:T(8,128)(2,1)S(1)} copy-done((bf16[448,128]{1,0:T(8,128)(2,1)S(1)}, bf16[448,128]{1,0:T(8,128)(2,1)}, u32[]{:S(2)}) %copy-start.15) | copy-done | bytes 114712
  40.0 0.0 copy-start.18
  40.0 4.7 %mix.3 = (bf16[576,320]{1,0:T(8,128)(2,1)S(1)}, f32[176,320]{1,0:T(8,128)S(1)}, bf16[448,128]{1,0:T(8,128)(2,1)}, bf16[448,128]{1,0:T(8,128)(2,1)}, bf16[448,128]{1,0:T(8,128)(2,1)}) custom-call(bf16[704,576]{1,0:T(8,128)(2,1)S(1)} %get-tuple-element.110.act_ref, bf16[2,320]{1,0:T(2,128)(2,1)S(1)} %slice.14.shift_ref, ...), custom_call_target="tpu_custom_call" | custom-call | flops 501350400 | bytes 1474560 | tf_op jit(solution)/shard_map/mix/pallas_call | solution.py:246
  44.7 0.6 collective-permute-start.19
  45.3 3.2 %collective-permute-start.20 = (bf16[448,128]{1,0:T(8,128)(2,1)}, bf16[448,128]{1,0:T(8,128)(2,1)S(1)}, u32[]{:S(2)}, u32[]{:S(2)}) collective-permute-start(bf16[448,128]{1,0:T(8,128)(2,1)} %get-tuple-element.123), channel_id=1, source_target_pairs={{0,3},{1,0},{2,1},{3,2},{4,7},{5,4},{6,5},{7,6},{8,11},{9,8},{10,9... | collective-permute-start | bytes 344072 | tf_op jit(solution)/shard_map/ppermute | solution.py:260
  48.5 0.1 pad_maximum_fusion.scales_ref
  48.7 0.0 copy-start.23
  48.7 0.0 copy-start.25
  48.7 5.1 %input_grad.1 = bf16[2,288,680]{2,1,0:T(8,128)(2,1)} custom-call(s32[1]{0:T(128)} %bitcast.me_ref, bf16[2,288,680]{2,1,0:T(8,128)(2,1)S(1)} %copy-done.2, f32[2,680]{1,0:T(2,128)S(1)} %get-tuple-element.108.refs_4_.mean_ref, f32[2,680]{1,0:T(2,128)S(1)} %copy-done.20, bf16[680,680]{1,0:T(8,128)(2,1)S(1)} %compare_convert_fusion.same_group_ref, ...), custom_call_target="tpu_custom_call" | custom-call | flops 532684800 | bytes 3133440 | tf_op jit(solution)/shard_map/input_grad/pallas_call | solution.py:246
  53.9 1.6 %adam.2 = (f32[176,360]{1,0:T(8,128)S(1)}, f32[176,360]{1,0:T(8,128)S(1)}, bf16[528,128]{1,0:T(8,128)(2,1)S(1)}) custom-call(f32[2]{0:T(128)S(1)} %pad_maximum_fusion.scales_ref, f32[176,360]{1,0:T(8,128)S(1)} %copy-done.5, bf16[528,128]{1,0:T(8,128)(2,1)} %collective-permute-done.15.refs_0_, bf16[528,128]{1,0:T(8,128)(2,1)S(1)} %collective-permute-done.16.refs_1_, ...), custom_call_target="tpu_custom_call" | custom-call | bytes 489600 | tf_op jit(solution)/shard_map/adam/pallas_call | solution.py:246
  55.5 6.1 %conditional.12 = (bf16[528,128]{1,0:T(8,128)(2,1)}, bf16[1]{0:T(256)(128)(2,1)}) conditional(s32[]{:T(128)} %clamp.4, (bf16[528,128]{1,0:T(8,128)(2,1)S(1)}, bf16[1]{0:T(256)(128)(2,1)}) %tuple.46, (bf16[528,128]{1,0:T(8,128)(2,1)S(1)}, bf16[1]{0:T(256)(128)(2,1)}) %tuple.46, (bf16[528,128]{1,0:T(8,128)(2,1)S(1)}, ...), branch_computations={%region_0.1_spmd, %region_1.2_spmd, %region_2.3_spmd} | conditional | bytes 540776
  55.5 1.5 %collective-permute-start.2 = (bf16[528,128]{1,0:T(8,128)(2,1)S(1)}, bf16[528,128]{1,0:T(8,128)(2,1)}, u32[]{:S(2)}, u32[]{:S(2)}) collective-permute-start(bf16[528,128]{1,0:T(8,128)(2,1)S(1)} %get-tuple-element.52), channel_id=1, source_target_pairs={{0,8},{4,12},{8,16},{12,20},{16,24},{20,28},{24,0},{28,4},{1,9},{5... | collective-permute-start | bytes 405512 | tf_op jit(solution)/shard_map/cond/branch_1_fun/ppermute | solution.py:260
  57.1 2.8 %collective-permute-start.3 = (bf16[1]{0:T(256)(128)(2,1)}, bf16[1]{0:T(256)(128)(2,1)}, u32[]{:S(2)}, u32[]{:S(2)}) collective-permute-start(bf16[1]{0:T(256)(128)(2,1)} %get-tuple-element.53), channel_id=1, source_target_pairs={{0,8},{4,12},{8,16},{12,20},{16,24},{20,28},{24,0},{28,4},{1,9},{5... | collective-permute-start | bytes 14 | tf_op jit(solution)/shard_map/cond/branch_1_fun/ppermute | solution.py:260
  59.9 1.7 %collective-permute-done.3 = bf16[1]{0:T(256)(128)(2,1)} collective-permute-done((bf16[1]{0:T(256)(128)(2,1)}, bf16[1]{0:T(256)(128)(2,1)}, u32[]{:S(2)}, u32[]{:S(2)}) %collective-permute-start.3) | collective-permute-done | bytes 34 | tf_op jit(solution)/shard_map/cond/branch_1_fun/ppermute | solution.py:260
  61.6 1.0 %adam.3 = (f32[176,320]{1,0:T(8,128)S(1)}, f32[176,320]{1,0:T(8,128)S(1)}, bf16[448,128]{1,0:T(8,128)(2,1)S(1)}) custom-call(f32[2]{0:T(128)S(1)} %pad_maximum_fusion.scales_ref, f32[176,320]{1,0:T(8,128)S(1)} %get-tuple-element.119.refs_6_.own_ref, bf16[448,128]{1,0:T(8,128)(2,1)S(1)} %collective-permute-done.18.refs_0_, ...), custom_call_target="tpu_custom_call" | custom-call | bytes 435200 | tf_op jit(solution)/shard_map/adam/pallas_call | solution.py:246
  62.7 5.9 %conditional.5 = (bf16[448,128]{1,0:T(8,128)(2,1)}, f32[170,1,680]{2,1,0:T(1,128)}, f32[170,1,680]{2,1,0:T(1,128)}) conditional(s32[]{:T(128)} %clamp.4, (bf16[448,128]{1,0:T(8,128)(2,1)S(1)}, f32[170,1,680]{2,1,0:T(1,128)S(1)}, f32[170,1,680]{2,1,0:T(1,128)S(1)}, f32[176,360]{1,0:T(8,128)S(1)}, f32[176,320]{1,0:T(8,128)S(1)}) %tuple.65, ...), branch_computations={%region_3.4_spmd, %region_4.5_spmd, %region_5.6_spmd} | conditional | bytes 1383616 | solution.py:372
  62.7 0.9 %collective-permute-start.7 = (bf16[448,128]{1,0:T(8,128)(2,1)S(1)}, bf16[448,128]{1,0:T(8,128)(2,1)}, u32[]{:S(2)}, u32[]{:S(2)}) collective-permute-start(bf16[448,128]{1,0:T(8,128)(2,1)S(1)} %get-tuple-element.63), channel_id=1, source_target_pairs={{0,8},{4,12},{8,16},{12,20},{16,24},{20,28},{24,0},{28,4},{1,9},{5... | collective-permute-start | bytes 344072 | tf_op jit(solution)/shard_map/cond/branch_1_fun/ppermute | solution.py:260
  63.6 1.6 %moments.4 = (f32[170,1,680]{2,1,0:T(1,128)}, f32[170,1,680]{2,1,0:T(1,128)}) custom-call(f32[170,1,680]{2,1,0:T(1,128)S(1)} %get-tuple-element.64.first_ref, f32[170,1,680]{2,1,0:T(1,128)S(1)} %get-tuple-element.65.second_ref, f32[176,360]{1,0:T(8,128)S(1)} %get-tuple-element.66.refs_0_, f32[176,320]{1,0:T(8,128)S(1)} %get-tuple-element.67.refs_1_), custom_call_target="tpu_custom_call" | custom-call | bytes 924800 | tf_op jit(solution)/shard_map/cond/branch_1_fun/moments/pallas_call | solution.py:246
  65.2 3.4 %collective-permute-done.7 = bf16[448,128]{1,0:T(8,128)(2,1)} collective-permute-done((bf16[448,128]{1,0:T(8,128)(2,1)S(1)}, bf16[448,128]{1,0:T(8,128)(2,1)}, u32[]{:S(2)}, u32[]{:S(2)}) %collective-permute-start.7) | collective-permute-done | bytes 114720 | tf_op jit(solution)/shard_map/cond/branch_1_fun/ppermute | solution.py:260
  69.2 2.0 %average.1 = f32[170,1,680]{2,1,0:T(1,128)} custom-call(f32[176,360]{1,0:T(8,128)S(1)} %get-tuple-element.120.refs_0_, f32[176,320]{1,0:T(8,128)S(1)} %get-tuple-element.126.refs_1_, bf16[528,128]{1,0:T(8,128)(2,1)} %get-tuple-element.125.refs_6_.refs_2_, bf16[448,128]{1,0:T(8,128)(2,1)} %get-tuple-element.130.refs_3_), custom_call_target="tpu_custom_call" | custom-call | bytes 924800 | tf_op jit(solution)/shard_map/average/pallas_call | solution.py:246
  (58 shorter events, 0.1 us)
Async XLA Ops:
  1.3 1.0 %copy-start = (f32[1,170,680]{2,0,1:T(1,128)S(1)}, f32[1,170,680]{2,0,1:T(1,128)}, u32[]{:S(2)}) copy-start(f32[1,170,680]{2,0,1:T(1,128)} %param.17) | copy-start | bytes 1387204
  2.6 14.2 %copy-start.14 = (bf16[448,128]{1,0:T(8,128)(2,1)}, bf16[448,128]{1,0:T(8,128)(2,1)S(1)}, u32[]{:S(2)}) copy-start(bf16[448,128]{1,0:T(8,128)(2,1)S(1)} %get-tuple-element.113.refs_0_.refs_6_) | copy-start | bytes 344068
  2.6 22.3 %copy-start.6 = (bf16[528,128]{1,0:T(8,128)(2,1)}, bf16[528,128]{1,0:T(8,128)(2,1)S(1)}, u32[]{:S(2)}) copy-start(bf16[528,128]{1,0:T(8,128)(2,1)S(1)} %get-tuple-element.111.refs_0_.refs_2_) | copy-start | bytes 405508
  2.6 12.1 %copy-start.2 = (bf16[2,288,680]{2,1,0:T(8,128)(2,1)S(1)}, bf16[2,288,680]{2,1,0:T(8,128)(2,1)}, u32[]{:S(2)}) copy-start(bf16[2,288,680]{2,1,0:T(8,128)(2,1)} %x_ref.3) | copy-start | bytes 2350084
  2.6 14.1 %collective-permute-start.9 = (bf16[528,128]{1,0:T(8,128)(2,1)S(1)}, bf16[528,128]{1,0:T(8,128)(2,1)S(1)}, u32[]{:S(2)}, u32[]{:S(2)}) collective-permute-start(bf16[528,128]{1,0:T(8,128)(2,1)S(1)} %get-tuple-element.111.refs_0_.refs_2_), channel_id=1, source_target_pairs={{0,3},{1,0},{2,1},{3,2},{4,7},{5,4},{6,5},{7,6},{8,11},{9,8},{10,9... | collective-permute-start | bytes 405512 | tf_op jit(solution)/shard_map/ppermute | solution.py:260
  7.7 17.2 %collective-permute-start.10 = (bf16[528,128]{1,0:T(8,128)(2,1)S(1)}, bf16[528,128]{1,0:T(8,128)(2,1)S(1)}, u32[]{:S(2)}, u32[]{:S(2)}) collective-permute-start(bf16[528,128]{1,0:T(8,128)(2,1)S(1)} %get-tuple-element.111.refs_0_.refs_2_), channel_id=1, source_target_pairs={{0,2},{1,3},{2,0},{3,1},{4,6},{5,7},{6,4},{7,5},{8,10},{9,11},{10,... | collective-permute-start | bytes 405512 | tf_op jit(solution)/shard_map/ppermute | solution.py:260
  7.7 17.2 %collective-permute-start.11 = (bf16[528,128]{1,0:T(8,128)(2,1)S(1)}, bf16[528,128]{1,0:T(8,128)(2,1)S(1)}, u32[]{:S(2)}, u32[]{:S(2)}) collective-permute-start(bf16[528,128]{1,0:T(8,128)(2,1)S(1)} %get-tuple-element.111.refs_0_.refs_2_), channel_id=1, source_target_pairs={{0,1},{1,2},{2,3},{3,0},{4,5},{5,6},{6,7},{7,4},{8,9},{9,10},{10,1... | collective-permute-start | bytes 405512 | tf_op jit(solution)/shard_map/ppermute | solution.py:260
  8.7 26.4 %collective-permute-start.12 = (bf16[448,128]{1,0:T(8,128)(2,1)S(1)}, bf16[448,128]{1,0:T(8,128)(2,1)}, u32[]{:S(2)}, u32[]{:S(2)}) collective-permute-start(bf16[448,128]{1,0:T(8,128)(2,1)S(1)} %get-tuple-element.113.refs_0_.refs_6_), channel_id=1, source_target_pairs={{0,3},{1,0},{2,1},{3,2},{4,7},{5,4},{6,5},{7,6},{8,11},{9,8},{10,9... | collective-permute-start | bytes 344072 | tf_op jit(solution)/shard_map/ppermute | solution.py:260
  11.5 26.6 %collective-permute-start.13 = (bf16[448,128]{1,0:T(8,128)(2,1)S(1)}, bf16[448,128]{1,0:T(8,128)(2,1)}, u32[]{:S(2)}, u32[]{:S(2)}) collective-permute-start(bf16[448,128]{1,0:T(8,128)(2,1)S(1)} %get-tuple-element.113.refs_0_.refs_6_), channel_id=1, source_target_pairs={{0,2},{1,3},{2,0},{3,1},{4,6},{5,7},{6,4},{7,5},{8,10},{9,11},{10,... | collective-permute-start | bytes 344072 | tf_op jit(solution)/shard_map/ppermute | solution.py:260
  16.7 11.7 %copy-start.19 = (f32[2,680]{1,0:T(2,128)}, f32[2,680]{1,0:T(2,128)S(1)}, u32[]{:S(2)}) copy-start(f32[2,680]{1,0:T(2,128)S(1)} %get-tuple-element.109.inverse_ref) | copy-start | bytes 16324
  16.8 11.6 %copy-start.8 = (bf16[528,128]{1,0:T(8,128)(2,1)}, bf16[528,128]{1,0:T(8,128)(2,1)S(1)}, u32[]{:S(2)}) copy-start(bf16[528,128]{1,0:T(8,128)(2,1)S(1)} %collective-permute-done.9.refs_1_.refs_3_) | copy-start | bytes 405508
  16.8 21.3 %collective-permute-start.14 = (bf16[448,128]{1,0:T(8,128)(2,1)S(1)}, bf16[448,128]{1,0:T(8,128)(2,1)}, u32[]{:S(2)}, u32[]{:S(2)}) collective-permute-start(bf16[448,128]{1,0:T(8,128)(2,1)S(1)} %get-tuple-element.113.refs_0_.refs_6_), channel_id=1, source_target_pairs={{0,1},{1,2},{2,3},{3,0},{4,5},{5,6},{6,7},{7,4},{8,9},{9,10},{10,1... | collective-permute-start | bytes 344072 | tf_op jit(solution)/shard_map/ppermute | solution.py:260
  24.9 3.5 %copy-start.10 = (bf16[528,128]{1,0:T(8,128)(2,1)}, bf16[528,128]{1,0:T(8,128)(2,1)S(1)}, u32[]{:S(2)}) copy-start(bf16[528,128]{1,0:T(8,128)(2,1)S(1)} %collective-permute-done.10.refs_2_.refs_4_) | copy-start | bytes 405508
  24.9 3.5 %copy-start.12 = (bf16[528,128]{1,0:T(8,128)(2,1)}, bf16[528,128]{1,0:T(8,128)(2,1)S(1)}, u32[]{:S(2)}) copy-start(bf16[528,128]{1,0:T(8,128)(2,1)S(1)} %collective-permute-done.11.refs_3_.refs_5_) | copy-start | bytes 405508
  24.9 7.1 %copy-start.28 = (bf16[2,680]{1,0:T(2,128)(2,1)S(1)}, bf16[2,680]{1,0:T(2,128)(2,1)}, u32[]{:S(2)}) copy-start(bf16[2,680]{1,0:T(2,128)(2,1)} %param.15) | copy-start | bytes 8164
  24.9 7.2 %copy-start.27 = (bf16[2,288,680]{2,1,0:T(8,128)(2,1)S(1)}, bf16[2,288,680]{2,1,0:T(8,128)(2,1)}, u32[]{:S(2)}) copy-start(bf16[2,288,680]{2,1,0:T(8,128)(2,1)} %param.16) | copy-start | bytes 2350084
  28.4 0.7 copy-start.3
  29.1 0.8 %copy-start.17 = (bf16[576,360]{1,0:T(8,128)(2,1)}, bf16[576,360]{1,0:T(8,128)(2,1)S(1)}, u32[]{:S(2)}) copy-start(bf16[576,360]{1,0:T(8,128)(2,1)S(1)} %get-tuple-element.112.refs_0_) | copy-start | bytes 1244164
  29.9 0.7 copy-start.21
  30.5 0.7 copy-start.22
  31.2 14.1 %collective-permute-start.15 = (bf16[528,128]{1,0:T(8,128)(2,1)}, bf16[528,128]{1,0:T(8,128)(2,1)}, u32[]{:S(2)}, u32[]{:S(2)}) collective-permute-start(bf16[528,128]{1,0:T(8,128)(2,1)} %get-tuple-element.116), channel_id=1, source_target_pairs={{0,1},{1,2},{2,3},{3,0},{4,5},{5,6},{6,7},{7,4},{8,9},{9,10},{10,1... | collective-permute-start | bytes 405512 | tf_op jit(solution)/shard_map/ppermute | solution.py:260
  33.2 20.6 %collective-permute-start.16 = (bf16[528,128]{1,0:T(8,128)(2,1)}, bf16[528,128]{1,0:T(8,128)(2,1)S(1)}, u32[]{:S(2)}, u32[]{:S(2)}) collective-permute-start(bf16[528,128]{1,0:T(8,128)(2,1)} %copy-done.22), channel_id=1, source_target_pairs={{0,2},{1,3},{2,0},{3,1},{4,6},{5,7},{6,4},{7,5},{8,10},{9,11},{10,... | collective-permute-start | bytes 405512 | tf_op jit(solution)/shard_map/ppermute | solution.py:260
  35.2 18.7 %collective-permute-start.17 = (bf16[528,128]{1,0:T(8,128)(2,1)}, bf16[528,128]{1,0:T(8,128)(2,1)S(1)}, u32[]{:S(2)}, u32[]{:S(2)}) collective-permute-start(bf16[528,128]{1,0:T(8,128)(2,1)} %copy-done.21), channel_id=1, source_target_pairs={{0,3},{1,0},{2,1},{3,2},{4,7},{5,4},{6,5},{7,6},{8,11},{9,8},{10,9... | collective-permute-start | bytes 405512 | tf_op jit(solution)/shard_map/ppermute | solution.py:260
  38.1 1.0 %copy-start.4 = (f32[176,360]{1,0:T(8,128)S(1)}, f32[176,360]{1,0:T(8,128)}, u32[]{:S(2)}) copy-start(f32[176,360]{1,0:T(8,128)} %copy-done.3) | copy-start | bytes 760324
  39.1 0.9 %copy-start.15 = (bf16[448,128]{1,0:T(8,128)(2,1)S(1)}, bf16[448,128]{1,0:T(8,128)(2,1)}, u32[]{:S(2)}) copy-start(bf16[448,128]{1,0:T(8,128)(2,1)} %copy-done.14) | copy-start | bytes 344068
  40.0 8.6 %copy-start.7 = (bf16[528,128]{1,0:T(8,128)(2,1)S(1)}, bf16[528,128]{1,0:T(8,128)(2,1)}, u32[]{:S(2)}) copy-start(bf16[528,128]{1,0:T(8,128)(2,1)} %copy-done.6) | copy-start | bytes 405508
  40.0 8.6 %copy-start.9 = (bf16[528,128]{1,0:T(8,128)(2,1)S(1)}, bf16[528,128]{1,0:T(8,128)(2,1)}, u32[]{:S(2)}) copy-start(bf16[528,128]{1,0:T(8,128)(2,1)} %copy-done.8) | copy-start | bytes 405508
  40.0 8.6 %copy-start.11 = (bf16[528,128]{1,0:T(8,128)(2,1)S(1)}, bf16[528,128]{1,0:T(8,128)(2,1)}, u32[]{:S(2)}) copy-start(bf16[528,128]{1,0:T(8,128)(2,1)} %copy-done.10) | copy-start | bytes 405508
  40.0 8.6 %copy-start.13 = (bf16[528,128]{1,0:T(8,128)(2,1)S(1)}, bf16[528,128]{1,0:T(8,128)(2,1)}, u32[]{:S(2)}) copy-start(bf16[528,128]{1,0:T(8,128)(2,1)} %copy-done.12) | copy-start | bytes 405508
  40.0 8.6 %copy-start.16 = (bf16[448,128]{1,0:T(8,128)(2,1)S(1)}, bf16[448,128]{1,0:T(8,128)(2,1)}, u32[]{:S(2)}) copy-start(bf16[448,128]{1,0:T(8,128)(2,1)} %copy-done.14) | copy-start | bytes 344068
  40.0 8.6 %copy-start.18 = (bf16[576,360]{1,0:T(8,128)(2,1)S(1)}, bf16[576,360]{1,0:T(8,128)(2,1)}, u32[]{:S(2)}) copy-start(bf16[576,360]{1,0:T(8,128)(2,1)} %copy-done.17) | copy-start | bytes 1244164
  40.0 8.6 %copy-start.20 = (f32[2,680]{1,0:T(2,128)S(1)}, f32[2,680]{1,0:T(2,128)}, u32[]{:S(2)}) copy-start(f32[2,680]{1,0:T(2,128)} %copy-done.19) | copy-start | bytes 16324
  44.7 16.9 %collective-permute-start.18 = (bf16[448,128]{1,0:T(8,128)(2,1)}, bf16[448,128]{1,0:T(8,128)(2,1)S(1)}, u32[]{:S(2)}, u32[]{:S(2)}) collective-permute-start(bf16[448,128]{1,0:T(8,128)(2,1)} %get-tuple-element.121), channel_id=1, source_target_pairs={{0,1},{1,2},{2,3},{3,0},{4,5},{5,6},{6,7},{7,4},{8,9},{9,10},{10,1... | collective-permute-start | bytes 344072 | tf_op jit(solution)/shard_map/ppermute | solution.py:260
  44.7 16.9 %collective-permute-start.19 = (bf16[448,128]{1,0:T(8,128)(2,1)}, bf16[448,128]{1,0:T(8,128)(2,1)S(1)}, u32[]{:S(2)}, u32[]{:S(2)}) collective-permute-start(bf16[448,128]{1,0:T(8,128)(2,1)} %get-tuple-element.122), channel_id=1, source_target_pairs={{0,2},{1,3},{2,0},{3,1},{4,6},{5,7},{6,4},{7,5},{8,10},{9,11},{10,... | collective-permute-start | bytes 344072 | tf_op jit(solution)/shard_map/ppermute | solution.py:260
  45.3 16.3 %collective-permute-start.20 = (bf16[448,128]{1,0:T(8,128)(2,1)}, bf16[448,128]{1,0:T(8,128)(2,1)S(1)}, u32[]{:S(2)}, u32[]{:S(2)}) collective-permute-start(bf16[448,128]{1,0:T(8,128)(2,1)} %get-tuple-element.123), channel_id=1, source_target_pairs={{0,3},{1,0},{2,1},{3,2},{4,7},{5,4},{6,5},{7,6},{8,11},{9,8},{10,9... | collective-permute-start | bytes 344072 | tf_op jit(solution)/shard_map/ppermute | solution.py:260
  48.6 5.2 %copy-start.1 = (f32[1,170,680]{2,0,1:T(1,128)S(1)}, f32[1,170,680]{2,0,1:T(1,128)}, u32[]{:S(2)}) copy-start(f32[1,170,680]{2,0,1:T(1,128)} %param.17) | copy-start | bytes 1387204
  48.7 5.2 %copy-start.5 = (f32[176,360]{1,0:T(8,128)S(1)}, f32[176,360]{1,0:T(8,128)}, u32[]{:S(2)}) copy-start(f32[176,360]{1,0:T(8,128)} %copy-done.3) | copy-start | bytes 760324
  48.7 5.2 %copy-start.23 = (f32[1,170,680]{2,0,1:T(1,128)S(1)}, f32[1,170,680]{2,0,1:T(1,128)}, u32[]{:S(2)}) copy-start(f32[1,170,680]{2,0,1:T(1,128)} %param.18) | copy-start | bytes 1387204
  48.7 5.2 %copy-start.25 = (f32[1,170,680]{2,0,1:T(1,128)S(1)}, f32[1,170,680]{2,0,1:T(1,128)}, u32[]{:S(2)}) copy-start(f32[1,170,680]{2,0,1:T(1,128)} %param.19) | copy-start | bytes 1387204
  53.9 7.7 %copy-start.24 = (f32[1,170,680]{2,0,1:T(1,128)S(1)}, f32[1,170,680]{2,0,1:T(1,128)}, u32[]{:S(2)}) copy-start(f32[1,170,680]{2,0,1:T(1,128)} %param.18) | copy-start | bytes 1387204
  53.9 7.7 %copy-start.26 = (f32[1,170,680]{2,0,1:T(1,128)S(1)}, f32[1,170,680]{2,0,1:T(1,128)}, u32[]{:S(2)}) copy-start(f32[1,170,680]{2,0,1:T(1,128)} %param.19) | copy-start | bytes 1387204
  55.5 6.1 %collective-permute-start.2 = (bf16[528,128]{1,0:T(8,128)(2,1)S(1)}, bf16[528,128]{1,0:T(8,128)(2,1)}, u32[]{:S(2)}, u32[]{:S(2)}) collective-permute-start(bf16[528,128]{1,0:T(8,128)(2,1)S(1)} %get-tuple-element.52), channel_id=1, source_target_pairs={{0,8},{4,12},{8,16},{12,20},{16,24},{20,28},{24,0},{28,4},{1,9},{5... | collective-permute-start | bytes 405512 | tf_op jit(solution)/shard_map/cond/branch_1_fun/ppermute | solution.py:260
  57.1 4.5 %collective-permute-start.3 = (bf16[1]{0:T(256)(128)(2,1)}, bf16[1]{0:T(256)(128)(2,1)}, u32[]{:S(2)}, u32[]{:S(2)}) collective-permute-start(bf16[1]{0:T(256)(128)(2,1)} %get-tuple-element.53), channel_id=1, source_target_pairs={{0,8},{4,12},{8,16},{12,20},{16,24},{20,28},{24,0},{28,4},{1,9},{5... | collective-permute-start | bytes 14 | tf_op jit(solution)/shard_map/cond/branch_1_fun/ppermute | solution.py:260
  62.7 5.8 %collective-permute-start.7 = (bf16[448,128]{1,0:T(8,128)(2,1)S(1)}, bf16[448,128]{1,0:T(8,128)(2,1)}, u32[]{:S(2)}, u32[]{:S(2)}) collective-permute-start(bf16[448,128]{1,0:T(8,128)(2,1)S(1)} %get-tuple-element.63), channel_id=1, source_target_pairs={{0,8},{4,12},{8,16},{12,20},{16,24},{20,28},{24,0},{28,4},{1,9},{5... | collective-permute-start | bytes 344072 | tf_op jit(solution)/shard_map/cond/branch_1_fun/ppermute | solution.py:260

commit v3 on v2

--- a/solution.py
+++ b/solution.py
@@ -17,7 +17,7 @@
 
 LANES = 128
 TILE_ROWS = 16
-VMEM_BYTES = 20 * 1024 * 1024
+VMEM_BYTES = 16 * 1024 * 1024
 
 
 def padded(rows):
@@ -69,6 +69,18 @@
             pieces.append(jnp.concatenate(parts, axis=0) if len(parts) > 1 else parts[0])
         return jnp.concatenate(pieces, axis=1) if len(pieces) > 1 else pieces[0]
 
+    def unpack(self, ref, out_ref, first_row):
+        for tile in range(self.tiles):
+            out_ref[first_row : first_row + self.deep, tile * LANES : (tile + 1) * LANES] = ref[
+                tile * self.deep : (tile + 1) * self.deep, :
+            ]
+        if self.rest:
+            left = ref[self.tiles * self.deep :, :]
+            for i, (first, count) in enumerate(self.folds):
+                out_ref[first_row + first : first_row + first + count, self.tiles * LANES :] = left[
+                    :count, i * self.rest : (i + 1) * self.rest
+                ]
+
     def payload(self):
         return jax.ShapeDtypeStruct((self.height, LANES), jnp.bfloat16)
 
@@ -86,6 +98,16 @@
     return sums[:count] + (sums[count : 2 * count] + sums[2 * count :])
 
 
+def table_sums(packs, rows, same_group):
+    return jnp.concatenate(
+        [
+            group_sums(rows[:, pack.start : pack.stop], same_group[: pack.columns, : pack.columns])
+            for pack in packs
+        ],
+        axis=1,
+    )
+
+
 def position_sums(parts):
     return jnp.concatenate([jnp.sum(part, axis=0, keepdims=True) for part in parts], axis=0)
 
@@ -108,16 +130,25 @@
         pack.write(out_ref, rows_ref[:, pack.start : pack.stop])
 
 
-def norm_in_kernel(shards, me_ref, x_ref, same_group_ref, act_ref, mean_ref, inverse_ref):
+def norm_in_kernel(shards, packs, me_ref, scales_ref, x_ref, shift_ref, out_grad_ref, *refs):
+    act_ref, mean_ref, inverse_ref, same_group_ref = refs[:4]
+    shift_refs, out_grad_refs = refs[4 : 4 + len(packs)], refs[4 + len(packs) :]
     samples, positions, channels = x_ref.shape
+    for pack, shift_out, out_grad_out in zip(packs, shift_refs, out_grad_refs):
+        shift_out[...] = shift_ref[...].astype(jnp.float32)[:, pack.start : pack.stop]
+        for i in range(samples):
+            out_grad_out[i] = out_grad_ref[i][:, pack.start : pack.stop]
+    group_of_row = lax.broadcasted_iota(jnp.int32, same_group_ref.shape, 0) // GSIZE
+    group_of_column = lax.broadcasted_iota(jnp.int32, same_group_ref.shape, 1) // GSIZE
+    same_group_ref[...] = (group_of_row == group_of_column).astype(jnp.float32).astype(jnp.bfloat16)
     rows = channels // shards
     deep = act_ref.shape[0] // shards
     entries = positions * GSIZE
     same_group = same_group_ref[...]
     parts = [x_ref[i].astype(jnp.float32) for i in range(samples)]
-    mean = group_sums(position_sums(parts), same_group) / entries
+    mean = table_sums(packs, position_sums(parts), same_group) / entries
     centered = [parts[i] - mean[i : i + 1] for i in range(samples)]
-    variance = group_sums(position_sums([part * part for part in centered]), same_group) / entries
+    variance = table_sums(packs, position_sums([part * part for part in centered]), same_group) / entries
     inverse = lax.rsqrt(variance + NORM_EPS)
     mean_ref[...] = mean
     inverse_ref[...] = inverse
@@ -132,18 +163,18 @@
 def mix_kernel(shards, pack, act_ref, shift_ref, out_grad_ref, same_group_ref, *refs):
     weight_refs, token_ref, refs = refs[:shards], refs[shards], refs[shards + 1 :]
     grad_hidden_ref, own_ref = refs[:2]
-    send_refs, weight_ref = refs[2 : 1 + shards], refs[1 + shards]
+    send_refs, (weight_ref, kept_ref, sem) = refs[2 : 1 + shards], refs[1 + shards :]
     samples, positions, columns = out_grad_ref.shape
     entries = positions * GSIZE
     deep = pack.deep
     for slot, shard_ref in enumerate(weight_refs):
-        weight_ref[slot * deep : (slot + 1) * deep, :] = pack.read(shard_ref).astype(jnp.bfloat16)
+        pack.unpack(shard_ref, weight_ref, slot * deep)
     same_group = same_group_ref[:columns, :columns]
     hidden = lax.dot_general(
         act_ref[...], weight_ref[...], (((0,), (0,)), ((), ())), preferred_element_type=jnp.float32
     )
     parts = [
-        hidden[i * positions : (i + 1) * positions] + shift_ref[i : i + 1, :].astype(jnp.float32)
+        hidden[i * positions : (i + 1) * positions] + shift_ref[i : i + 1, :]
         for i in range(samples)
     ]
     mean = group_sums(position_sums(parts), same_group) / entries
@@ -160,13 +191,16 @@
     ) / entries
     for i in range(samples):
         first, second = means[i : i + 1], means[samples + i : samples + i + 1]
-        grad_hidden_ref[i * positions : (i + 1) * positions, :] = (
+        kept_ref[i * positions : (i + 1) * positions, :] = (
             inverse[i : i + 1] * (grads[i] - first - normed[i] * second)
         ).astype(jnp.bfloat16)
-    grad = jnp.dot(act_ref[...], grad_hidden_ref[...], preferred_element_type=jnp.float32)
+    copy = pltpu.make_async_copy(kept_ref, grad_hidden_ref, sem)
+    copy.start()
+    grad = jnp.dot(act_ref[...], kept_ref[...], preferred_element_type=jnp.float32)
     for slot, send_ref in enumerate(send_refs, 1):
         pack.write(send_ref, grad[slot * deep : (slot + 1) * deep])
     own_ref[...] = grad[:deep]
+    copy.wait()
 
 
 def input_grad_kernel(shards, packs, me_ref, x_ref, mean_ref, inverse_ref, same_group_ref, *refs):
@@ -189,7 +223,8 @@
         (x_ref[i].astype(jnp.float32) - mean_ref[i : i + 1, :]) * inverse[i : i + 1] for i in range(samples)
     ]
     grads = [grad_act[i * positions : (i + 1) * positions] * silu_grad(normed[i]) for i in range(samples)]
-    means = group_sums(
+    means = table_sums(
+        packs,
         jnp.concatenate(
             [position_sums(grads), position_sums([g * n for g, n in zip(grads, normed)])], axis=0
         ),
@@ -228,26 +263,31 @@
 
 
 def average_kernel(packs, *refs):
-    moved_refs, other_refs, out_ref = refs[: len(packs)], refs[len(packs) : -1], refs[-1]
+    moved_refs, other_refs = refs[: len(packs)], refs[len(packs) : -3]
+    out_ref, rows_ref, sem = refs[-3:]
     rows = out_ref.shape[0]
     pieces = [
         0.5 * (moved_ref[...] + pack.read(other_ref))
         for pack, moved_ref, other_ref in zip(packs, moved_refs, other_refs)
     ]
-    out_ref[:, 0, :] = jnp.concatenate(pieces, axis=1)[:rows]
+    rows_ref[:, 0, :] = jnp.concatenate(pieces, axis=1)[:rows]
+    copy = pltpu.make_async_copy(rows_ref, out_ref, sem)
+    copy.start()
+    copy.wait()
 
 
 SCALARS = pl.BlockSpec(memory_space=pltpu.SMEM)
 BLOCKS = pl.BlockSpec(memory_space=pltpu.VMEM)
 TOKEN = pl.BlockSpec(memory_space=pl.ANY)
-
-
-def call(kernel, name, outs, specs, operands, scratch=(), flops=0, elements=0):
+IN_HBM = pl.BlockSpec(memory_space=pltpu.HBM)
+
+
+def call(kernel, name, outs, specs, operands, scratch=(), out_specs=None, flops=0, elements=0):
     return pl.pallas_call(
         kernel,
         out_shape=outs,
         in_specs=specs,
-        out_specs=jax.tree.map(lambda _: BLOCKS, outs),
+        out_specs=out_specs or jax.tree.map(lambda _: BLOCKS, outs),
         scratch_shapes=list(scratch),
         compiler_params=pltpu.CompilerParams(vmem_limit_bytes=VMEM_BYTES),
         cost_estimate=pl.CostEstimate(flops=flops, bytes_accessed=8 * elements, transcendentals=elements),
@@ -278,9 +318,6 @@
     params, first_moment, second_moment = (
         jnp.transpose(array, (1, 0, 2)) for array in (params, first_moment, second_moment)
     )
-    group_of = jnp.arange(channels, dtype=jnp.int32) // GSIZE
-    same_group = (group_of[:, None] == group_of[None, :]).astype(jnp.bfloat16)
-
     shard_list = call(
         functools.partial(cast_kernel, packs),
         "cast",
@@ -301,31 +338,39 @@
         [LEARN_RATE / (1.0 - jnp.power(BETA_ONE, step_count)), 1.0 / (1.0 - jnp.power(BETA_TWO, step_count))]
     )
 
-    activation, mean_in, inverse_in = call(
-        functools.partial(norm_in_kernel, shards),
+    activation, mean_in, inverse_in, same_group, *pieces = call(
+        functools.partial(norm_in_kernel, shards, packs),
         "norm_in",
         (
             jax.ShapeDtypeStruct((shards * deep, tokens), jnp.bfloat16),
             jax.ShapeDtypeStruct((samples, channels), jnp.float32),
             jax.ShapeDtypeStruct((samples, channels), jnp.float32),
+            jax.ShapeDtypeStruct((max(pack.columns for pack in packs),) * 2, jnp.bfloat16),
+            *(jax.ShapeDtypeStruct((samples, pack.columns), jnp.float32) for pack in packs),
+            *(jax.ShapeDtypeStruct((samples, positions, pack.columns), jnp.bfloat16) for pack in packs),
         ),
-        [SCALARS, BLOCKS, BLOCKS],
-        (me, block_input, same_group),
+        [SCALARS, SCALARS, BLOCKS, BLOCKS, BLOCKS],
+        (me, scales, block_input, time_shift, out_grad),
         elements=tokens * channels,
     )
 
     hidden_grads, owns, arrived = [], [], []
     token = mean_in
-    for pack, pieces in zip(packs, weights):
-        columns = slice(pack.start, pack.stop)
+    shifts, out_grads = pieces[: len(packs)], pieces[len(packs) :]
+    for pack, shard_list, shift, out_grad_piece in zip(packs, weights, shifts, out_grads):
         grad_hidden, own, *sends = call(
             functools.partial(mix_kernel, shards, pack),
             "mix",
-            (jax.ShapeDtypeStruct((tokens, pack.columns), jnp.bfloat16), pack.block())
+            (pltpu.HBM((tokens, pack.columns), jnp.bfloat16), pack.block())
             + (pack.payload(),) * (shards - 1),
             [BLOCKS] * (4 + shards) + [TOKEN],
-            (activation, time_shift[:, columns], out_grad[:, :, columns], same_group, *pieces, token),
-            scratch=[pltpu.VMEM((shards * deep, pack.columns), jnp.bfloat16)],
+            (activation, shift, out_grad_piece, same_group, *shard_list, token),
+            scratch=[
+                pltpu.VMEM((shards * deep, pack.columns), jnp.bfloat16),
+                pltpu.VMEM((tokens, pack.columns), jnp.bfloat16),
+                pltpu.SemaphoreType.DMA,
+            ],
+            out_specs=(IN_HBM,) + (BLOCKS,) * shards,
             flops=4 * tokens * channels * pack.columns,
             elements=tokens * pack.columns,
         )
@@ -365,6 +410,18 @@
             elements=rows * channels,
         )
 
+    def average(*blocks):
+        return call(
+            functools.partial(average_kernel, packs),
+            "average",
+            pltpu.HBM(params.shape, jnp.float32),
+            [BLOCKS] * (2 * len(packs)),
+            blocks,
+            scratch=[pltpu.VMEM(params.shape, jnp.float32), pltpu.SemaphoreType.DMA],
+            out_specs=IN_HBM,
+            elements=rows * channels,
+        )
+
     def from_behind(finish, *operands):
         def branch(distance):
             return lambda *values: finish(lambda block: moved_on(block, "replica", distance), *values)
@@ -376,17 +433,13 @@
         lambda move, sent, weight: (move(sent), move(weight)), sent_a, push_weight.astype(jnp.bfloat16)
     )
     grad_b, moved_b, sent_b = adam(packs[1], owns[1], arrived[1], other_a)
-    other_b, first_new, second_new = from_behind(
-        lambda move, sent, *grads: (move(sent), *moments(*grads)), sent_b, grad_a, grad_b
-    )
-    averaged = call(
-        functools.partial(average_kernel, packs),
-        "average",
-        jax.ShapeDtypeStruct(params.shape, jnp.float32),
-        [BLOCKS] * (2 * len(packs)),
-        (moved_a, moved_b, other_a, other_b),
-        elements=rows * channels,
-    )
+
+    def finish(move, sent, *values):
+        grads, moved, other_first = values[:2], values[2:4], values[4]
+        other = move(sent)
+        return (*moments(*grads), average(*moved, other_first, other))
+
+    first_new, second_new, averaged = from_behind(finish, sent_b, grad_a, grad_b, moved_a, moved_b, other_a)
     new_weight = 0.5 * (push_weight + other_weight.astype(jnp.float32))
     return (
         grad_input,

time: 72.1 us -> 64.8 us (0.90); the launches traced: 72.3 us -> 64.1 us
  waiting for transfers between devices: 13.2 us -> 2.73 us
  starting transfers between devices: 25 us -> 29.3 us
  local copies, waits for them, and re-layouts: 7.8 us -> 5.99 us
    ppermute x15, waiting for transfers between devices: 13.2 us -> 2.73 us  [moved_on(): lax.ppermute(block, axis, [(i, (i + distance) % size) for i in range(size)])]
    ppermute x15, starting transfers between devices: 25 us -> 29.3 us  [moved_on(): lax.ppermute(block, axis, [(i, (i + distance) % size) for i in range(size)])]
    slice x4 -> x0, local copies, waits for them, and re-layouts: 2.03 us -> none  [the longest x2 1.27 us: local(): out_grad[:, :, columns]]
    unnamed x58 -> x24, local copies, waits for them, and re-layouts: 5.77 us -> 5.99 us
  transfers between devices with their start and end apart: 15 -> 15, of which waited for: 3 -> 2; matrix products, arithmetic and copies ran while one was open for 3% -> 0% of each run, Pallas kernels for 26% -> 28%
where the time goes in v3:
time: 64.8 us; the launch traced here: 64.1 us
  starting transfers between devices  29.3 us (45%)
  Pallas kernels  21.9 us (34%)
  local copies, waits for them, and re-layouts  5.99 us (9%)
  between operations  4.08 us (6%)
  waiting for transfers between devices  2.73 us (4%)
    ppermute x15, starting transfers between devices, moved_on(): lax.ppermute(block, axis, [(i, (i + distance) % size) for i in range(size)])  29.3 us
    pallas_call x9, Pallas kernels, call(): pl.pallas_call(kernel, out_shape=outs, in_specs=specs, out_specs=out_spec...  21.9 us
    unnamed x24, local copies, waits for them, and re-layouts  5.99 us
    ppermute x15, waiting for transfers between devices, moved_on(): lax.ppermute(block, axis, [(i, (i + distance) % size) for i in range(size)])  2.73 us
  transfers between devices with their start and end apart: 15, of which 2 were waited for; matrix products, arithmetic and copies ran while one was open for 0% of the time, Pallas kernels for 28%

profile of v3, /device:TPU:0, one launch (start us, length us, event | category | flops | bytes accessed | tf_op | source)
XLA Modules:
  0.0 64.1 jit_solution(17016477942457997710)
XLA Ops:
  1.3 0.0 copy-start
  1.3 1.0 %copy-done = f32[1,170,680]{2,0,1:T(1,128)S(1)} copy-done((f32[1,170,680]{2,0,1:T(1,128)S(1)}, f32[1,170,680]{2,0,1:T(1,128)}, u32[]{:S(2)}) %copy-start) | copy-done | bytes 462424
  2.3 0.3 cast.1
  2.6 3.1 %collective-permute-start.11 = (bf16[528,128]{1,0:T(8,128)(2,1)S(1)}, bf16[528,128]{1,0:T(8,128)(2,1)S(1)}, u32[]{:S(2)}, u32[]{:S(2)}) collective-permute-start(bf16[528,128]{1,0:T(8,128)(2,1)S(1)} %get-tuple-element.147.refs_0_.refs_2_), channel_id=1, source_target_pairs={{0,1},{1,2},{2,3},{3,0},{4,5},{5,6},{6,7},{7,4},{8,9},{9,10},{10,1... | collective-permute-start | bytes 405512 | tf_op jit(solution)/shard_map/ppermute | solution.py:300
  5.7 2.6 %collective-permute-start.10 = (bf16[528,128]{1,0:T(8,128)(2,1)S(1)}, bf16[528,128]{1,0:T(8,128)(2,1)S(1)}, u32[]{:S(2)}, u32[]{:S(2)}) collective-permute-start(bf16[528,128]{1,0:T(8,128)(2,1)S(1)} %get-tuple-element.147.refs_0_.refs_2_), channel_id=1, source_target_pairs={{0,2},{1,3},{2,0},{3,1},{4,6},{5,7},{6,4},{7,5},{8,10},{9,11},{10,... | collective-permute-start | bytes 405512 | tf_op jit(solution)/shard_map/ppermute | solution.py:300
  8.2 1.3 %collective-permute-start.9 = (bf16[528,128]{1,0:T(8,128)(2,1)S(1)}, bf16[528,128]{1,0:T(8,128)(2,1)S(1)}, u32[]{:S(2)}, u32[]{:S(2)}) collective-permute-start(bf16[528,128]{1,0:T(8,128)(2,1)S(1)} %get-tuple-element.147.refs_0_.refs_2_), channel_id=1, source_target_pairs={{0,3},{1,0},{2,1},{3,2},{4,7},{5,4},{6,5},{7,6},{8,11},{9,8},{10,9... | collective-permute-start | bytes 405512 | tf_op jit(solution)/shard_map/ppermute | solution.py:300
  9.6 0.7 %collective-permute-start.14 = (bf16[448,128]{1,0:T(8,128)(2,1)S(1)}, bf16[448,128]{1,0:T(8,128)(2,1)S(1)}, u32[]{:S(2)}, u32[]{:S(2)}) collective-permute-start(bf16[448,128]{1,0:T(8,128)(2,1)S(1)} %get-tuple-element.151.refs_0_.refs_6_), channel_id=1, source_target_pairs={{0,1},{1,2},{2,3},{3,0},{4,5},{5,6},{6,7},{7,4},{8,9},{9,10},{10,1... | collective-permute-start | bytes 344072 | tf_op jit(solution)/shard_map/ppermute | solution.py:300
  10.3 0.3 collective-permute-start.13
  11.4 0.0 copy-start.7
  11.4 0.1 pad_maximum_fusion.scales_ref
  11.5 0.6 copy-done.7
  12.1 1.2 %copy-done.2 = bf16[2,288,680]{2,1,0:T(8,128)(2,1)S(1)} copy-done((bf16[2,288,680]{2,1,0:T(8,128)(2,1)S(1)}, bf16[2,288,680]{2,1,0:T(8,128)(2,1)}, u32[]{:S(2)}) %copy-start.2) | copy-done | bytes 783384
  13.2 1.2 %copy-done.4 = bf16[2,288,680]{2,1,0:T(8,128)(2,1)S(1)} copy-done((bf16[2,288,680]{2,1,0:T(8,128)(2,1)S(1)}, bf16[2,288,680]{2,1,0:T(8,128)(2,1)}, u32[]{:S(2)}) %copy-start.4) | copy-done | bytes 783384
  14.4 2.9 %norm_in.1 = (bf16[704,576]{1,0:T(8,128)(2,1)S(1)}, f32[2,680]{1,0:T(2,128)S(1)}, f32[2,680]{1,0:T(2,128)S(1)}, bf16[360,360]{1,0:T(8,128)(2,1)S(1)}, f32[2,360]...) custom-call(s32[1]{0:T(128)} %bitcast.3.me_ref, ...), custom_call_target="tpu_custom_call" | custom-call | bytes 3133440 | tf_op jit(solution)/shard_map/norm_in/pallas_call | solution.py:286
  17.3 0.0 collective-permute-done.11.refs_3_.refs_5_
  17.3 2.9 %collective-permute-start.12 = (bf16[448,128]{1,0:T(8,128)(2,1)S(1)}, bf16[448,128]{1,0:T(8,128)(2,1)S(1)}, u32[]{:S(2)}, u32[]{:S(2)}) collective-permute-start(bf16[448,128]{1,0:T(8,128)(2,1)S(1)} %get-tuple-element.151.refs_0_.refs_6_), channel_id=1, source_target_pairs={{0,3},{1,0},{2,1},{3,2},{4,7},{5,4},{6,5},{7,6},{8,11},{9,8},{10,9... | collective-permute-start | bytes 344072 | tf_op jit(solution)/shard_map/ppermute | solution.py:300
  20.2 3.6 %mix.2 = (bf16[576,360]{1,0:T(8,128)(2,1)}, f32[176,360]{1,0:T(8,128)S(1)}, bf16[528,128]{1,0:T(8,128)(2,1)S(1)}, bf16[528,128]{1,0:T(8,128)(2,1)}, bf16[528,128]{1,0:T(8,128)(2,1)}) custom-call(bf16[704,576]{1,0:T(8,128)(2,1)S(1)} %get-tuple-element.144.act_ref, f32[2,360]{1,0:T(2,128)S(1)} %get-tuple-element.145.shift_ref, ...), custom_call_target="tpu_custom_call" | custom-call | flops 564019200 | bytes 1658880 | tf_op jit(solution)/shard_map/mix/pallas_call | solution.py:286
  23.9 5.4 %collective-permute-start.15 = (bf16[528,128]{1,0:T(8,128)(2,1)S(1)}, bf16[528,128]{1,0:T(8,128)(2,1)S(1)}, u32[]{:S(2)}, u32[]{:S(2)}) collective-permute-start(bf16[528,128]{1,0:T(8,128)(2,1)S(1)} %get-tuple-element.154), channel_id=1, source_target_pairs={{0,1},{1,2},{2,3},{3,0},{4,5},{5,6},{6,7},{7,4},{8,9},{9,10},{10,1... | collective-permute-start | bytes 405512 | tf_op jit(solution)/shard_map/ppermute | solution.py:300
  29.2 2.7 %collective-permute-start.16 = (bf16[528,128]{1,0:T(8,128)(2,1)}, bf16[528,128]{1,0:T(8,128)(2,1)S(1)}, u32[]{:S(2)}, u32[]{:S(2)}) collective-permute-start(bf16[528,128]{1,0:T(8,128)(2,1)} %get-tuple-element.155), channel_id=1, source_target_pairs={{0,2},{1,3},{2,0},{3,1},{4,6},{5,7},{6,4},{7,5},{8,10},{9,11},{10,... | collective-permute-start | bytes 405512 | tf_op jit(solution)/shard_map/ppermute | solution.py:300
  32.0 0.0 collective-permute-done.14.refs_3_.refs_9_
  32.0 0.0 collective-permute-start.17
  32.0 0.0 collective-permute-done.13.refs_2_.refs_8_
  32.0 0.0 copy-start.3
  32.0 4.3 %mix.3 = (bf16[576,320]{1,0:T(8,128)(2,1)}, f32[176,320]{1,0:T(8,128)S(1)}, bf16[448,128]{1,0:T(8,128)(2,1)}, bf16[448,128]{1,0:T(8,128)(2,1)}, bf16[448,128]{1,0:T(8,128)(2,1)}) custom-call(bf16[704,576]{1,0:T(8,128)(2,1)S(1)} %get-tuple-element.144.act_ref, f32[2,320]{1,0:T(2,128)S(1)} %get-tuple-element.149.shift_ref, ...), custom_call_target="tpu_custom_call" | custom-call | flops 501350400 | bytes 1474560 | tf_op jit(solution)/shard_map/mix/pallas_call | solution.py:286
  36.3 2.1 %collective-permute-start.18 = (bf16[448,128]{1,0:T(8,128)(2,1)}, bf16[448,128]{1,0:T(8,128)(2,1)}, u32[]{:S(2)}, u32[]{:S(2)}) collective-permute-start(bf16[448,128]{1,0:T(8,128)(2,1)} %get-tuple-element.159), channel_id=1, source_target_pairs={{0,1},{1,2},{2,3},{3,0},{4,5},{5,6},{6,7},{7,4},{8,9},{9,10},{10,1... | collective-permute-start | bytes 344072 | tf_op jit(solution)/shard_map/ppermute | solution.py:300
  38.4 0.2 collective-permute-start.19
  38.6 0.0 collective-permute-done.15.refs_0_
  38.6 2.2 %collective-permute-start.20 = (bf16[448,128]{1,0:T(8,128)(2,1)}, bf16[448,128]{1,0:T(8,128)(2,1)}, u32[]{:S(2)}, u32[]{:S(2)}) collective-permute-start(bf16[448,128]{1,0:T(8,128)(2,1)} %get-tuple-element.161), channel_id=1, source_target_pairs={{0,3},{1,0},{2,1},{3,2},{4,7},{5,4},{6,5},{7,6},{8,11},{9,8},{10,9... | collective-permute-start | bytes 344072 | tf_op jit(solution)/shard_map/ppermute | solution.py:300
  40.8 1.0 %copy-done.5 = bf16[576,360]{1,0:T(8,128)(2,1)S(1)} copy-done((bf16[576,360]{1,0:T(8,128)(2,1)S(1)}, bf16[576,360]{1,0:T(8,128)(2,1)}, u32[]{:S(2)}) %copy-start.5) | copy-done | bytes 414744
  41.8 1.0 %copy-done.6 = bf16[576,320]{1,0:T(8,128)(2,1)S(1)} copy-done((bf16[576,320]{1,0:T(8,128)(2,1)S(1)}, bf16[576,320]{1,0:T(8,128)(2,1)}, u32[]{:S(2)}) %copy-start.6) | copy-done | bytes 368664
  42.9 4.2 %input_grad.1 = bf16[2,288,680]{2,1,0:T(8,128)(2,1)} custom-call(s32[1]{0:T(128)} %bitcast.3.me_ref, bf16[2,288,680]{2,1,0:T(8,128)(2,1)S(1)} %copy-done.3, f32[2,680]{1,0:T(2,128)S(1)} %get-tuple-element.141.refs_4_.mean_ref, f32[2,680]{1,0:T(2,128)S(1)} %get-tuple-element.142.inverse_ref, bf16[360,360]{1,0:T(8,128)(2,1)S(1)} %get-tuple-element.143.same_group_ref, ...), custom_call_target="tpu_custom_call" | custom-call | flops 532684800 | bytes 3133440 | tf_op jit(solution)/shard_map/input_grad/pallas_call | solution.py:286
  47.0 0.0 collective-permute-done.16.refs_1_
  47.0 0.0 collective-permute-done.17.refs_2_
  47.1 0.0 copy-start.9
  47.1 0.0 copy-start.11
  47.1 1.6 %adam.2 = (f32[176,360]{1,0:T(8,128)S(1)}, f32[176,360]{1,0:T(8,128)S(1)}, bf16[528,128]{1,0:T(8,128)(2,1)S(1)}) custom-call(f32[2]{0:T(128)S(1)} %pad_maximum_fusion.scales_ref, f32[176,360]{1,0:T(8,128)S(1)} %get-tuple-element.152.refs_4_.own_ref, bf16[528,128]{1,0:T(8,128)(2,1)S(1)} %collective-permute-done.15.refs_0_, ...), custom_call_target="tpu_custom_call" | custom-call | bytes 489600 | tf_op jit(solution)/shard_map/adam/pallas_call | solution.py:286
  48.7 5.2 %conditional.12 = (bf16[528,128]{1,0:T(8,128)(2,1)}, bf16[1]{0:T(256)(128)(2,1)}) conditional(s32[]{:T(128)} %clamp.4, (bf16[528,128]{1,0:T(8,128)(2,1)S(1)}, bf16[1]{0:T(256)(128)(2,1)}) %tuple.49, (bf16[528,128]{1,0:T(8,128)(2,1)S(1)}, bf16[1]{0:T(256)(128)(2,1)}) %tuple.49, (bf16[528,128]{1,0:T(8,128)(2,1)S(1)}, ...), branch_computations={%region_0.1_spmd, %region_1.2_spmd, %region_2.3_spmd} | conditional | bytes 540776
  48.7 1.6 %collective-permute-start.4 = (bf16[528,128]{1,0:T(8,128)(2,1)S(1)}, bf16[528,128]{1,0:T(8,128)(2,1)}, u32[]{:S(2)}, u32[]{:S(2)}) collective-permute-start(bf16[528,128]{1,0:T(8,128)(2,1)S(1)} %get-tuple-element.73), channel_id=1, source_target_pairs={{0,16},{4,20},{8,24},{12,28},{16,0},{20,4},{24,8},{28,12},{1,17},{... | collective-permute-start | bytes 405512 | tf_op jit(solution)/shard_map/cond/branch_2_fun/ppermute | solution.py:300
  50.3 2.6 %collective-permute-start.5 = (bf16[1]{0:T(256)(128)(2,1)}, bf16[1]{0:T(256)(128)(2,1)}, u32[]{:S(2)}, u32[]{:S(2)}) collective-permute-start(bf16[1]{0:T(256)(128)(2,1)} %get-tuple-element.74), channel_id=1, source_target_pairs={{0,16},{4,20},{8,24},{12,28},{16,0},{20,4},{24,8},{28,12},{1,17},{... | collective-permute-start | bytes 14 | tf_op jit(solution)/shard_map/cond/branch_2_fun/ppermute | solution.py:300
  52.9 1.0 %collective-permute-done.5 = bf16[1]{0:T(256)(128)(2,1)} collective-permute-done((bf16[1]{0:T(256)(128)(2,1)}, bf16[1]{0:T(256)(128)(2,1)}, u32[]{:S(2)}, u32[]{:S(2)}) %collective-permute-start.5) | collective-permute-done | bytes 34 | tf_op jit(solution)/shard_map/cond/branch_2_fun/ppermute | solution.py:300
  53.9 0.0 collective-permute-done.4
  54.6 0.0 collective-permute-done.18.refs_0_
  54.6 1.5 %adam.3 = (f32[176,320]{1,0:T(8,128)S(1)}, f32[176,320]{1,0:T(8,128)S(1)}, bf16[448,128]{1,0:T(8,128)(2,1)S(1)}) custom-call(f32[2]{0:T(128)S(1)} %pad_maximum_fusion.scales_ref, f32[176,320]{1,0:T(8,128)S(1)} %get-tuple-element.157.refs_6_.own_ref, bf16[448,128]{1,0:T(8,128)(2,1)} %collective-permute-done.18.refs_0_, ...), custom_call_target="tpu_custom_call" | custom-call | bytes 435200 | tf_op jit(solution)/shard_map/adam/pallas_call | solution.py:286
  56.2 6.8 %conditional.5 = (f32[170,1,680]{2,1,0:T(1,128)}, f32[170,1,680]{2,1,0:T(1,128)}, f32[1,170,680]{2,0,1:T(1,128)}) conditional(s32[]{:T(128)} %clamp.4, (f32[170,1,680]{2,1,0:T(1,128)S(1)}, f32[170,1,680]{2,1,0:T(1,128)S(1)}, f32[176,360]{1,0:T(8,128)S(1)}, f32[176,320]{1,0:T(8,128)S(1)}, bf16[448,128]{1,0:T(8,128)(2,1)S(1)}, ...), branch_computations={%region_3.4_spmd, %region_4.5_spmd, %region_5.6_spmd} | conditional | bytes 2308416 | solution.py:429
  56.2 1.6 %collective-permute-start.8 = (bf16[448,128]{1,0:T(8,128)(2,1)S(1)}, bf16[448,128]{1,0:T(8,128)(2,1)S(1)}, u32[]{:S(2)}, u32[]{:S(2)}) collective-permute-start(bf16[448,128]{1,0:T(8,128)(2,1)S(1)} %get-tuple-element.104), channel_id=1, source_target_pairs={{0,16},{4,20},{8,24},{12,28},{16,0},{20,4},{24,8},{28,12},{1,17},{... | collective-permute-start | bytes 344072 | tf_op jit(solution)/shard_map/cond/branch_2_fun/ppermute | solution.py:300
  57.8 1.6 %moments.5 = (f32[170,1,680]{2,1,0:T(1,128)}, f32[170,1,680]{2,1,0:T(1,128)}) custom-call(f32[170,1,680]{2,1,0:T(1,128)S(1)} %get-tuple-element.95.first_ref, f32[170,1,680]{2,1,0:T(1,128)S(1)} %get-tuple-element.96.second_ref, f32[176,360]{1,0:T(8,128)S(1)} %get-tuple-element.97.refs_0_, f32[176,320]{1,0:T(8,128)S(1)} %get-tuple-element.98.refs_1_), custom_call_target="tpu_custom_call" | custom-call | bytes 924800 | tf_op jit(solution)/shard_map/cond/branch_2_fun/moments/pallas_call | solution.py:286
  59.4 1.7 %collective-permute-done.8.refs_3_ = bf16[448,128]{1,0:T(8,128)(2,1)S(1)} collective-permute-done((bf16[448,128]{1,0:T(8,128)(2,1)S(1)}, bf16[448,128]{1,0:T(8,128)(2,1)S(1)}, u32[]{:S(2)}, u32[]{:S(2)}) %collective-permute-start.8) | collective-permute-done | bytes 114720 | tf_op jit(solution)/shard_map/cond/branch_2_fun/ppermute | solution.py:300
  61.1 1.9 %average.5 = f32[170,1,680]{2,1,0:T(1,128)} custom-call(f32[176,360]{1,0:T(8,128)S(1)} %get-tuple-element.101.refs_0_, f32[176,320]{1,0:T(8,128)S(1)} %get-tuple-element.102.refs_1_, bf16[528,128]{1,0:T(8,128)(2,1)} %get-tuple-element.103.refs_2_, bf16[448,128]{1,0:T(8,128)(2,1)S(1)} %collective-permute-done.8.refs_3_), custom_call_target="tpu_custom_call" | custom-call | bytes 924800 | tf_op jit(solution)/shard_map/cond/branch_2_fun/average/pallas_call | solution.py:286
  (18 shorter events, 0.0 us)
Async XLA Ops:
  1.3 1.0 %copy-start = (f32[1,170,680]{2,0,1:T(1,128)S(1)}, f32[1,170,680]{2,0,1:T(1,128)}, u32[]{:S(2)}) copy-start(f32[1,170,680]{2,0,1:T(1,128)} %param.17) | copy-start | bytes 1387204
  2.6 14.7 %collective-permute-start.11 = (bf16[528,128]{1,0:T(8,128)(2,1)S(1)}, bf16[528,128]{1,0:T(8,128)(2,1)S(1)}, u32[]{:S(2)}, u32[]{:S(2)}) collective-permute-start(bf16[528,128]{1,0:T(8,128)(2,1)S(1)} %get-tuple-element.147.refs_0_.refs_2_), channel_id=1, source_target_pairs={{0,1},{1,2},{2,3},{3,0},{4,5},{5,6},{6,7},{7,4},{8,9},{9,10},{10,1... | collective-permute-start | bytes 405512 | tf_op jit(solution)/shard_map/ppermute | solution.py:300
  5.7 14.5 %collective-permute-start.10 = (bf16[528,128]{1,0:T(8,128)(2,1)S(1)}, bf16[528,128]{1,0:T(8,128)(2,1)S(1)}, u32[]{:S(2)}, u32[]{:S(2)}) collective-permute-start(bf16[528,128]{1,0:T(8,128)(2,1)S(1)} %get-tuple-element.147.refs_0_.refs_2_), channel_id=1, source_target_pairs={{0,2},{1,3},{2,0},{3,1},{4,6},{5,7},{6,4},{7,5},{8,10},{9,11},{10,... | collective-permute-start | bytes 405512 | tf_op jit(solution)/shard_map/ppermute | solution.py:300
  8.2 11.9 %collective-permute-start.9 = (bf16[528,128]{1,0:T(8,128)(2,1)S(1)}, bf16[528,128]{1,0:T(8,128)(2,1)S(1)}, u32[]{:S(2)}, u32[]{:S(2)}) collective-permute-start(bf16[528,128]{1,0:T(8,128)(2,1)S(1)} %get-tuple-element.147.refs_0_.refs_2_), channel_id=1, source_target_pairs={{0,3},{1,0},{2,1},{3,2},{4,7},{5,4},{6,5},{7,6},{8,11},{9,8},{10,9... | collective-permute-start | bytes 405512 | tf_op jit(solution)/shard_map/ppermute | solution.py:300
  9.6 22.4 %collective-permute-start.14 = (bf16[448,128]{1,0:T(8,128)(2,1)S(1)}, bf16[448,128]{1,0:T(8,128)(2,1)S(1)}, u32[]{:S(2)}, u32[]{:S(2)}) collective-permute-start(bf16[448,128]{1,0:T(8,128)(2,1)S(1)} %get-tuple-element.151.refs_0_.refs_6_), channel_id=1, source_target_pairs={{0,1},{1,2},{2,3},{3,0},{4,5},{5,6},{6,7},{7,4},{8,9},{9,10},{10,1... | collective-permute-start | bytes 344072 | tf_op jit(solution)/shard_map/ppermute | solution.py:300
  10.3 21.7 %collective-permute-start.13 = (bf16[448,128]{1,0:T(8,128)(2,1)S(1)}, bf16[448,128]{1,0:T(8,128)(2,1)S(1)}, u32[]{:S(2)}, u32[]{:S(2)}) collective-permute-start(bf16[448,128]{1,0:T(8,128)(2,1)S(1)} %get-tuple-element.151.refs_0_.refs_6_), channel_id=1, source_target_pairs={{0,2},{1,3},{2,0},{3,1},{4,6},{5,7},{6,4},{7,5},{8,10},{9,11},{10,... | collective-permute-start | bytes 344072 | tf_op jit(solution)/shard_map/ppermute | solution.py:300
  11.4 0.7 %copy-start.7 = (bf16[2,680]{1,0:T(2,128)(2,1)S(1)}, bf16[2,680]{1,0:T(2,128)(2,1)}, u32[]{:S(2)}) copy-start(bf16[2,680]{1,0:T(2,128)(2,1)} %shift_ref.1) | copy-start | bytes 8164
  12.1 1.2 %copy-start.2 = (bf16[2,288,680]{2,1,0:T(8,128)(2,1)S(1)}, bf16[2,288,680]{2,1,0:T(8,128)(2,1)}, u32[]{:S(2)}) copy-start(bf16[2,288,680]{2,1,0:T(8,128)(2,1)} %x_ref.3) | copy-start | bytes 2350084
  13.2 1.2 %copy-start.4 = (bf16[2,288,680]{2,1,0:T(8,128)(2,1)S(1)}, bf16[2,288,680]{2,1,0:T(8,128)(2,1)}, u32[]{:S(2)}) copy-start(bf16[2,288,680]{2,1,0:T(8,128)(2,1)} %out_grad_ref.1) | copy-start | bytes 2350084
  17.3 14.7 %collective-permute-start.12 = (bf16[448,128]{1,0:T(8,128)(2,1)S(1)}, bf16[448,128]{1,0:T(8,128)(2,1)S(1)}, u32[]{:S(2)}, u32[]{:S(2)}) collective-permute-start(bf16[448,128]{1,0:T(8,128)(2,1)S(1)} %get-tuple-element.151.refs_0_.refs_6_), channel_id=1, source_target_pairs={{0,3},{1,0},{2,1},{3,2},{4,7},{5,4},{6,5},{7,6},{8,11},{9,8},{10,9... | collective-permute-start | bytes 344072 | tf_op jit(solution)/shard_map/ppermute | solution.py:300
  23.9 14.7 %collective-permute-start.15 = (bf16[528,128]{1,0:T(8,128)(2,1)S(1)}, bf16[528,128]{1,0:T(8,128)(2,1)S(1)}, u32[]{:S(2)}, u32[]{:S(2)}) collective-permute-start(bf16[528,128]{1,0:T(8,128)(2,1)S(1)} %get-tuple-element.154), channel_id=1, source_target_pairs={{0,1},{1,2},{2,3},{3,0},{4,5},{5,6},{6,7},{7,4},{8,9},{9,10},{10,1... | collective-permute-start | bytes 405512 | tf_op jit(solution)/shard_map/ppermute | solution.py:300
  29.2 17.8 %collective-permute-start.16 = (bf16[528,128]{1,0:T(8,128)(2,1)}, bf16[528,128]{1,0:T(8,128)(2,1)S(1)}, u32[]{:S(2)}, u32[]{:S(2)}) collective-permute-start(bf16[528,128]{1,0:T(8,128)(2,1)} %get-tuple-element.155), channel_id=1, source_target_pairs={{0,2},{1,3},{2,0},{3,1},{4,6},{5,7},{6,4},{7,5},{8,10},{9,11},{10,... | collective-permute-start | bytes 405512 | tf_op jit(solution)/shard_map/ppermute | solution.py:300
  32.0 15.1 %collective-permute-start.17 = (bf16[528,128]{1,0:T(8,128)(2,1)}, bf16[528,128]{1,0:T(8,128)(2,1)}, u32[]{:S(2)}, u32[]{:S(2)}) collective-permute-start(bf16[528,128]{1,0:T(8,128)(2,1)} %get-tuple-element.156), channel_id=1, source_target_pairs={{0,3},{1,0},{2,1},{3,2},{4,7},{5,4},{6,5},{7,6},{8,11},{9,8},{10,9... | collective-permute-start | bytes 405512 | tf_op jit(solution)/shard_map/ppermute | solution.py:300
  32.0 8.8 %copy-start.3 = (bf16[2,288,680]{2,1,0:T(8,128)(2,1)S(1)}, bf16[2,288,680]{2,1,0:T(8,128)(2,1)}, u32[]{:S(2)}) copy-start(bf16[2,288,680]{2,1,0:T(8,128)(2,1)} %x_ref.3) | copy-start | bytes 2350084
  36.3 18.3 %collective-permute-start.18 = (bf16[448,128]{1,0:T(8,128)(2,1)}, bf16[448,128]{1,0:T(8,128)(2,1)}, u32[]{:S(2)}, u32[]{:S(2)}) collective-permute-start(bf16[448,128]{1,0:T(8,128)(2,1)} %get-tuple-element.159), channel_id=1, source_target_pairs={{0,1},{1,2},{2,3},{3,0},{4,5},{5,6},{6,7},{7,4},{8,9},{9,10},{10,1... | collective-permute-start | bytes 344072 | tf_op jit(solution)/shard_map/ppermute | solution.py:300
  38.4 16.2 %collective-permute-start.19 = (bf16[448,128]{1,0:T(8,128)(2,1)}, bf16[448,128]{1,0:T(8,128)(2,1)}, u32[]{:S(2)}, u32[]{:S(2)}) collective-permute-start(bf16[448,128]{1,0:T(8,128)(2,1)} %get-tuple-element.160), channel_id=1, source_target_pairs={{0,2},{1,3},{2,0},{3,1},{4,6},{5,7},{6,4},{7,5},{8,10},{9,11},{10,... | collective-permute-start | bytes 344072 | tf_op jit(solution)/shard_map/ppermute | solution.py:300
  38.6 16.0 %collective-permute-start.20 = (bf16[448,128]{1,0:T(8,128)(2,1)}, bf16[448,128]{1,0:T(8,128)(2,1)}, u32[]{:S(2)}, u32[]{:S(2)}) collective-permute-start(bf16[448,128]{1,0:T(8,128)(2,1)} %get-tuple-element.161), channel_id=1, source_target_pairs={{0,3},{1,0},{2,1},{3,2},{4,7},{5,4},{6,5},{7,6},{8,11},{9,8},{10,9... | collective-permute-start | bytes 344072 | tf_op jit(solution)/shard_map/ppermute | solution.py:300
  40.8 1.0 %copy-start.5 = (bf16[576,360]{1,0:T(8,128)(2,1)S(1)}, bf16[576,360]{1,0:T(8,128)(2,1)}, u32[]{:S(2)}) copy-start(bf16[576,360]{1,0:T(8,128)(2,1)} %get-tuple-element.148.refs_0_) | copy-start | bytes 1244164
  41.8 1.0 %copy-start.6 = (bf16[576,320]{1,0:T(8,128)(2,1)S(1)}, bf16[576,320]{1,0:T(8,128)(2,1)}, u32[]{:S(2)}) copy-start(bf16[576,320]{1,0:T(8,128)(2,1)} %get-tuple-element.153.refs_1_) | copy-start | bytes 1105924
  42.8 4.2 %copy-start.1 = (f32[1,170,680]{2,0,1:T(1,128)S(1)}, f32[1,170,680]{2,0,1:T(1,128)}, u32[]{:S(2)}) copy-start(f32[1,170,680]{2,0,1:T(1,128)} %param.17) | copy-start | bytes 1387204
  42.8 4.2 %copy-start.8 = (f32[1,170,680]{2,0,1:T(1,128)S(1)}, f32[1,170,680]{2,0,1:T(1,128)}, u32[]{:S(2)}) copy-start(f32[1,170,680]{2,0,1:T(1,128)} %param.18) | copy-start | bytes 1387204
  42.9 4.2 %copy-start.10 = (f32[1,170,680]{2,0,1:T(1,128)S(1)}, f32[1,170,680]{2,0,1:T(1,128)}, u32[]{:S(2)}) copy-start(f32[1,170,680]{2,0,1:T(1,128)} %param.19) | copy-start | bytes 1387204
  47.1 7.5 %copy-start.9 = (f32[1,170,680]{2,0,1:T(1,128)S(1)}, f32[1,170,680]{2,0,1:T(1,128)}, u32[]{:S(2)}) copy-start(f32[1,170,680]{2,0,1:T(1,128)} %param.18) | copy-start | bytes 1387204
  47.1 7.5 %copy-start.11 = (f32[1,170,680]{2,0,1:T(1,128)S(1)}, f32[1,170,680]{2,0,1:T(1,128)}, u32[]{:S(2)}) copy-start(f32[1,170,680]{2,0,1:T(1,128)} %param.19) | copy-start | bytes 1387204
  48.7 5.2 %collective-permute-start.4 = (bf16[528,128]{1,0:T(8,128)(2,1)S(1)}, bf16[528,128]{1,0:T(8,128)(2,1)}, u32[]{:S(2)}, u32[]{:S(2)}) collective-permute-start(bf16[528,128]{1,0:T(8,128)(2,1)S(1)} %get-tuple-element.73), channel_id=1, source_target_pairs={{0,16},{4,20},{8,24},{12,28},{16,0},{20,4},{24,8},{28,12},{1,17},{... | collective-permute-start | bytes 405512 | tf_op jit(solution)/shard_map/cond/branch_2_fun/ppermute | solution.py:300
  50.3 3.6 %collective-permute-start.5 = (bf16[1]{0:T(256)(128)(2,1)}, bf16[1]{0:T(256)(128)(2,1)}, u32[]{:S(2)}, u32[]{:S(2)}) collective-permute-start(bf16[1]{0:T(256)(128)(2,1)} %get-tuple-element.74), channel_id=1, source_target_pairs={{0,16},{4,20},{8,24},{12,28},{16,0},{20,4},{24,8},{28,12},{1,17},{... | collective-permute-start | bytes 14 | tf_op jit(solution)/shard_map/cond/branch_2_fun/ppermute | solution.py:300
  56.2 4.9 %collective-permute-start.8 = (bf16[448,128]{1,0:T(8,128)(2,1)S(1)}, bf16[448,128]{1,0:T(8,128)(2,1)S(1)}, u32[]{:S(2)}, u32[]{:S(2)}) collective-permute-start(bf16[448,128]{1,0:T(8,128)(2,1)S(1)} %get-tuple-element.104), channel_id=1, source_target_pairs={{0,16},{4,20},{8,24},{12,28},{16,0},{20,4},{24,8},{28,12},{1,17},{... | collective-permute-start | bytes 344072 | tf_op jit(solution)/shard_map/cond/branch_2_fun/ppermute | solution.py:300

commit v4 on v3

--- a/solution.py
+++ b/solution.py
@@ -160,15 +160,26 @@
         act_ref[slot * deep : slot * deep + rows, :] = turned[slot * rows : (slot + 1) * rows].astype(jnp.bfloat16)
 
 
-def mix_kernel(shards, pack, act_ref, shift_ref, out_grad_ref, same_group_ref, *refs):
-    weight_refs, token_ref, refs = refs[:shards], refs[shards], refs[shards + 1 :]
+def for_each_slot(shards, me, refs, use):
+    for slot in range(shards):
+        if len(refs) == shards or slot not in (1, shards - 1):
+            use(slot, refs[slot])
+            continue
+        edge = shards - 1 if slot == 1 else 0
+        pl.when(me == edge)(functools.partial(use, slot, refs[shards]))
+        pl.when(me != edge)(functools.partial(use, slot, refs[slot]))
+
+
+def mix_kernel(shards, held, pack, me_ref, act_ref, shift_ref, out_grad_ref, same_group_ref, *refs):
+    weight_refs, token_ref, refs = refs[:held], refs[held], refs[held + 1 :]
     grad_hidden_ref, own_ref = refs[:2]
     send_refs, (weight_ref, kept_ref, sem) = refs[2 : 1 + shards], refs[1 + shards :]
     samples, positions, columns = out_grad_ref.shape
     entries = positions * GSIZE
     deep = pack.deep
-    for slot, shard_ref in enumerate(weight_refs):
-        pack.unpack(shard_ref, weight_ref, slot * deep)
+    for_each_slot(
+        shards, me_ref[0], weight_refs, lambda slot, ref: pack.unpack(ref, weight_ref, slot * deep)
+    )
     same_group = same_group_ref[:columns, :columns]
     hidden = lax.dot_general(
         act_ref[...], weight_ref[...], (((0,), (0,)), ((), ())), preferred_element_type=jnp.float32
@@ -203,7 +214,7 @@
     copy.wait()
 
 
-def input_grad_kernel(shards, packs, me_ref, x_ref, mean_ref, inverse_ref, same_group_ref, *refs):
+def input_grad_kernel(shards, held, packs, me_ref, x_ref, mean_ref, inverse_ref, same_group_ref, *refs):
     grad_refs, refs = refs[: len(packs)], refs[len(packs) :]
     weight_refs, out_ref, rows_ref = refs[:-2], refs[-2], refs[-1]
     samples, positions, channels = x_ref.shape
@@ -211,9 +222,11 @@
     rows = channels // shards
     grad_act = 0.0
     for index, (pack, grad_ref) in enumerate(zip(packs, grad_refs)):
-        for slot in range(shards):
-            block = pack.read(weight_refs[index * shards + slot])
-            rows_ref[slot * rows : (slot + 1) * rows, : pack.columns] = block[:rows]
+
+        def place(slot, ref, pack=pack):
+            rows_ref[slot * rows : (slot + 1) * rows, : pack.columns] = pack.read(ref)[:rows]
+
+        for_each_slot(shards, me_ref[0], weight_refs[index * held : (index + 1) * held], place)
         weight = pltpu.roll(rows_ref[:, : pack.columns], me_ref[0] * rows, 0).astype(jnp.bfloat16)
         grad_act += lax.dot_general(
             grad_ref[...], weight, (((1,), (1,)), ((), ())), preferred_element_type=jnp.float32
@@ -300,6 +313,16 @@
     return lax.ppermute(block, axis, [(i, (i + distance) % size) for i in range(size)])
 
 
+def gathered(piece, shards):
+    if shards != 4:
+        return [piece] + [moved_on(piece, "dp", -slot) for slot in range(1, shards)]
+    two = moved_on(piece, "dp", -2)
+    above = lax.ppermute(piece, "dp", [(i + 1, i) for i in range(shards - 1)])
+    below = lax.ppermute(piece, "dp", [(i, i + 1) for i in range(shards - 1)])
+    far = lax.ppermute(two, "dp", [(1, 0), (shards - 2, shards - 1)])
+    return [piece, above, two, below, far]
+
+
 def column_cuts(channels):
     half = (channels // GSIZE + 1) // 2 * GSIZE
     return [(0, half), (half, channels)]
@@ -327,9 +350,8 @@
         scratch=[pltpu.VMEM((deep, channels), jnp.float32)],
         elements=rows * channels,
     )
-    weights = [
-        [piece] + [moved_on(piece, "dp", -slot) for slot in range(1, shards)] for piece in shard_list
-    ]
+    weights = [gathered(piece, shards) for piece in shard_list]
+    held = len(weights[0])
 
     level_count = lax.axis_size("replica").bit_length() - 1
     distance_bits = step[0] % level_count
@@ -359,12 +381,12 @@
     shifts, out_grads = pieces[: len(packs)], pieces[len(packs) :]
     for pack, shard_list, shift, out_grad_piece in zip(packs, weights, shifts, out_grads):
         grad_hidden, own, *sends = call(
-            functools.partial(mix_kernel, shards, pack),
+            functools.partial(mix_kernel, shards, held, pack),
             "mix",
             (pltpu.HBM((tokens, pack.columns), jnp.bfloat16), pack.block())
             + (pack.payload(),) * (shards - 1),
-            [BLOCKS] * (4 + shards) + [TOKEN],
-            (activation, shift, out_grad_piece, same_group, *shard_list, token),
+            [SCALARS] + [BLOCKS] * (4 + held) + [TOKEN],
+            (me, activation, shift, out_grad_piece, same_group, *shard_list, token),
             scratch=[
                 pltpu.VMEM((shards * deep, pack.columns), jnp.bfloat16),
                 pltpu.VMEM((tokens, pack.columns), jnp.bfloat16),
@@ -380,10 +402,10 @@
         arrived.append([moved_on(send, "dp", slot) for slot, send in enumerate(sends, 1)])
 
     grad_input = call(
-        functools.partial(input_grad_kernel, shards, packs),
+        functools.partial(input_grad_kernel, shards, held, packs),
         "input_grad",
         jax.ShapeDtypeStruct(block_input.shape, jnp.bfloat16),
-        [SCALARS] + [BLOCKS] * (4 + len(packs) * (1 + shards)),
+        [SCALARS] + [BLOCKS] * (4 + len(packs) * (1 + held)),
         (me, block_input, mean_in, inverse_in, same_group, *hidden_grads, *weights[0], *weights[1]),
         scratch=[pltpu.VMEM((channels, max(pack.columns for pack in packs)), jnp.float32)],
         flops=2 * tokens * channels * channels,

time: 64.8 us -> 75.4 us (1.16)
  waiting for transfers between devices: 2.73 us -> 8.15 us
  starting transfers between devices: 29.3 us -> 33.1 us
  Pallas kernels: 21.9 us -> 22.8 us
    ppermute x0 -> x6, starting transfers between devices: none -> 9.92 us  [the longest x2 4.76 us: gathered(): below = lax.ppermute(piece, 'dp', [(i, i + 1) for i in range(shards - 1)])]
    ppermute x15 -> x11, starting transfers between devices: 29.3 us -> 23.2 us  [moved_on(): lax.ppermute(block, axis, [(i, (i + distance) % size) for i in range(size)])]
    ppermute x15 -> x11, waiting for transfers between devices: 2.73 us -> 8.13 us  [moved_on(): lax.ppermute(block, axis, [(i, (i + distance) % size) for i in range(size)])]
    pallas_call x9, Pallas kernels: 21.9 us -> 22.8 us  [call(): pl.pallas_call(kernel, out_shape=outs, in_specs=specs, out_specs=out_spec...]
    unnamed x24 -> x28, local copies, waits for them, and re-layouts: 5.99 us -> 6.64 us
  transfers between devices with their start and end apart: 15 -> 17, of which waited for: 2 -> 3; matrix products, arithmetic and copies ran while one was open for 0% -> 0% of each run, Pallas kernels for 28% -> 26%
where the time goes in v4:
time: 75.4 us; the launch traced here: 74.8 us
  starting transfers between devices  33.1 us (44%)
  Pallas kernels  22.8 us (30%)
  waiting for transfers between devices  8.15 us (11%)
  local copies, waits for them, and re-layouts  6.64 us (9%)
  between operations  4.03 us (5%)
    ppermute x11, starting transfers between devices, moved_on(): lax.ppermute(block, axis, [(i, (i + distance) % size) for i in range(size)])  23.2 us
    pallas_call x9, Pallas kernels, call(): pl.pallas_call(kernel, out_shape=outs, in_specs=specs, out_specs=out_spec...  22.8 us
    ppermute x11, waiting for transfers between devices, moved_on(): lax.ppermute(block, axis, [(i, (i + distance) % size) for i in range(size)])  8.13 us
    unnamed x28, local copies, waits for them, and re-layouts  6.64 us
    ppermute x2, starting transfers between devices, gathered(): below = lax.ppermute(piece, 'dp', [(i, i + 1) for i in range(shards - 1)])  4.76 us
    ppermute x2, starting transfers between devices, gathered(): above = lax.ppermute(piece, 'dp', [(i + 1, i) for i in range(shards - 1)])  2.58 us
    ppermute x2, starting transfers between devices, gathered(): far = lax.ppermute(two, 'dp', [(1, 0), (shards - 2, shards - 1)])  2.57 us
  transfers between devices with their start and end apart: 17, of which 3 were waited for; matrix products, arithmetic and copies ran while one was open for 0% of the time, Pallas kernels for 26%

profile of v4, /device:TPU:0, one launch (start us, length us, event | category | flops | bytes accessed | tf_op | source)
XLA Modules:
  0.0 74.8 jit_solution(2901673016443838779)
XLA Ops:
  1.3 0.0 copy-start
  1.3 1.0 %copy-done = f32[1,170,680]{2,0,1:T(1,128)S(1)} copy-done((f32[1,170,680]{2,0,1:T(1,128)S(1)}, f32[1,170,680]{2,0,1:T(1,128)}, u32[]{:S(2)}) %copy-start) | copy-done | bytes 462424
  2.3 0.3 cast.1
  2.6 4.1 %collective-permute-start.10 = (bf16[528,128]{1,0:T(8,128)(2,1)S(1)}, bf16[528,128]{1,0:T(8,128)(2,1)S(1)}, u32[]{:S(2)}, u32[]{:S(2)}) collective-permute-start(bf16[528,128]{1,0:T(8,128)(2,1)S(1)} %get-tuple-element.147.refs_0_.refs_2_), channel_id=1, source_target_pairs={{0,2},{1,3},{2,0},{3,1},{4,6},{5,7},{6,4},{7,5},{8,10},{9,11},{10,... | collective-permute-start | bytes 405512 | tf_op jit(solution)/shard_map/ppermute | solution.py:313
  6.7 3.5 %collective-permute-start.11 = (bf16[528,128]{1,0:T(8,128)(2,1)S(1)}, bf16[528,128]{1,0:T(8,128)(2,1)S(1)}, u32[]{:S(2)}, u32[]{:S(2)}) collective-permute-start(bf16[528,128]{1,0:T(8,128)(2,1)S(1)} %get-tuple-element.147.refs_0_.refs_2_), channel_id=1, source_target_pairs={{0,1},{1,2},{2,3},{4,5},{5,6},{6,7},{8,9},{9,10},{10,11},{12,13},{... | collective-permute-start | bytes 405512 | tf_op jit(solution)/shard_map/ppermute | solution.py:321
  10.2 1.3 %collective-permute-start.9 = (bf16[528,128]{1,0:T(8,128)(2,1)S(1)}, bf16[528,128]{1,0:T(8,128)(2,1)S(1)}, u32[]{:S(2)}, u32[]{:S(2)}) collective-permute-start(bf16[528,128]{1,0:T(8,128)(2,1)S(1)} %get-tuple-element.147.refs_0_.refs_2_), channel_id=1, source_target_pairs={{1,0},{2,1},{3,2},{5,4},{6,5},{7,6},{9,8},{10,9},{11,10},{13,12},{... | collective-permute-start | bytes 405512 | tf_op jit(solution)/shard_map/ppermute | solution.py:320
  11.5 1.7 %collective-permute-done.10.refs_2_.refs_4_ = bf16[528,128]{1,0:T(8,128)(2,1)S(1)} collective-permute-done((bf16[528,128]{1,0:T(8,128)(2,1)S(1)}, bf16[528,128]{1,0:T(8,128)(2,1)S(1)}, u32[]{:S(2)}, u32[]{:S(2)}) %collective-permute-start.10) | collective-permute-done | bytes 135200 | tf_op jit(solution)/shard_map/ppermute | solution.py:313
  13.2 1.3 %collective-permute-start.12 = (bf16[528,128]{1,0:T(8,128)(2,1)S(1)}, bf16[528,128]{1,0:T(8,128)(2,1)S(1)}, u32[]{:S(2)}, u32[]{:S(2)}) collective-permute-start(bf16[528,128]{1,0:T(8,128)(2,1)S(1)} %collective-permute-done.10.refs_2_.refs_4_), channel_id=1, source_target_pairs={{1,0},{2,3},{5,4},{6,7},{9,8},{10,11},{13,12},{14,15},{17,16},{18,... | collective-permute-start | bytes 405512 | tf_op jit(solution)/shard_map/ppermute | solution.py:322
  14.5 4.9 %collective-permute-start.14 = (bf16[448,128]{1,0:T(8,128)(2,1)S(1)}, bf16[448,128]{1,0:T(8,128)(2,1)S(1)}, u32[]{:S(2)}, u32[]{:S(2)}) collective-permute-start(bf16[448,128]{1,0:T(8,128)(2,1)S(1)} %get-tuple-element.151.refs_0_.refs_7_), channel_id=1, source_target_pairs={{0,2},{1,3},{2,0},{3,1},{4,6},{5,7},{6,4},{7,5},{8,10},{9,11},{10,... | collective-permute-start | bytes 344072 | tf_op jit(solution)/shard_map/ppermute | solution.py:313
  19.4 1.3 %collective-permute-start.15 = (bf16[448,128]{1,0:T(8,128)(2,1)S(1)}, bf16[448,128]{1,0:T(8,128)(2,1)S(1)}, u32[]{:S(2)}, u32[]{:S(2)}) collective-permute-start(bf16[448,128]{1,0:T(8,128)(2,1)S(1)} %get-tuple-element.151.refs_0_.refs_7_), channel_id=1, source_target_pairs={{0,1},{1,2},{2,3},{4,5},{5,6},{6,7},{8,9},{9,10},{10,11},{12,13},{... | collective-permute-start | bytes 344072 | tf_op jit(solution)/shard_map/ppermute | solution.py:321
  21.4 0.0 copy-start.9
  21.5 0.1 pad_maximum_fusion.scales_ref
  21.6 0.6 copy-done.9
  22.1 1.2 %copy-done.2 = bf16[2,288,680]{2,1,0:T(8,128)(2,1)S(1)} copy-done((bf16[2,288,680]{2,1,0:T(8,128)(2,1)S(1)}, bf16[2,288,680]{2,1,0:T(8,128)(2,1)}, u32[]{:S(2)}) %copy-start.2) | copy-done | bytes 783384
  23.3 1.2 %copy-done.4 = bf16[2,288,680]{2,1,0:T(8,128)(2,1)S(1)} copy-done((bf16[2,288,680]{2,1,0:T(8,128)(2,1)S(1)}, bf16[2,288,680]{2,1,0:T(8,128)(2,1)}, u32[]{:S(2)}) %copy-start.4) | copy-done | bytes 783384
  24.5 2.9 %norm_in.1 = (bf16[704,576]{1,0:T(8,128)(2,1)S(1)}, f32[2,680]{1,0:T(2,128)S(1)}, f32[2,680]{1,0:T(2,128)S(1)}, bf16[360,360]{1,0:T(8,128)(2,1)S(1)}, f32[2,360]...) custom-call(s32[1]{0:T(128)} %bitcast.3.me_ref, ...), custom_call_target="tpu_custom_call" | custom-call | bytes 3133440 | tf_op jit(solution)/shard_map/norm_in/pallas_call | solution.py:299
  27.4 0.0 collective-permute-done.14.refs_2_.refs_9_
  27.4 1.3 %collective-permute-start.13 = (bf16[448,128]{1,0:T(8,128)(2,1)S(1)}, bf16[448,128]{1,0:T(8,128)(2,1)S(1)}, u32[]{:S(2)}, u32[]{:S(2)}) collective-permute-start(bf16[448,128]{1,0:T(8,128)(2,1)S(1)} %get-tuple-element.151.refs_0_.refs_7_), channel_id=1, source_target_pairs={{1,0},{2,1},{3,2},{5,4},{6,5},{7,6},{9,8},{10,9},{11,10},{13,12},{... | collective-permute-start | bytes 344072 | tf_op jit(solution)/shard_map/ppermute | solution.py:320
  28.7 1.3 %collective-permute-start.16 = (bf16[448,128]{1,0:T(8,128)(2,1)S(1)}, bf16[448,128]{1,0:T(8,128)(2,1)S(1)}, u32[]{:S(2)}, u32[]{:S(2)}) collective-permute-start(bf16[448,128]{1,0:T(8,128)(2,1)S(1)} %collective-permute-done.14.refs_2_.refs_9_), channel_id=1, source_target_pairs={{1,0},{2,3},{5,4},{6,7},{9,8},{10,11},{13,12},{14,15},{17,16},{18,... | collective-permute-start | bytes 344072 | tf_op jit(solution)/shard_map/ppermute | solution.py:322
  30.0 0.0 collective-permute-done.12.refs_4_.refs_6_
  30.0 3.7 %mix.2 = (bf16[576,360]{1,0:T(8,128)(2,1)}, f32[176,360]{1,0:T(8,128)S(1)}, bf16[528,128]{1,0:T(8,128)(2,1)S(1)}, bf16[528,128]{1,0:T(8,128)(2,1)}, bf16[528,128]{1,0:T(8,128)(2,1)}) custom-call(s32[1]{0:T(128)} %bitcast.3.me_ref, bf16[704,576]{1,0:T(8,128)(2,1)S(1)} %get-tuple-element.144.act_ref, f32[2,360]{1,0:T(2,128)S(1)} %get-tuple-element.145.shift_ref, ...), custom_call_target="tpu_custom_call" | custom-call | flops 564019200 | bytes 1658880 | tf_op jit(solution)/shard_map/mix/pallas_call | solution.py:299
  33.7 2.7 %collective-permute-start.17 = (bf16[528,128]{1,0:T(8,128)(2,1)S(1)}, bf16[528,128]{1,0:T(8,128)(2,1)S(1)}, u32[]{:S(2)}, u32[]{:S(2)}) collective-permute-start(bf16[528,128]{1,0:T(8,128)(2,1)S(1)} %get-tuple-element.154), channel_id=1, source_target_pairs={{0,1},{1,2},{2,3},{3,0},{4,5},{5,6},{6,7},{7,4},{8,9},{9,10},{10,1... | collective-permute-start | bytes 405512 | tf_op jit(solution)/shard_map/ppermute | solution.py:313
  36.4 2.0 %collective-permute-start.18 = (bf16[528,128]{1,0:T(8,128)(2,1)}, bf16[528,128]{1,0:T(8,128)(2,1)}, u32[]{:S(2)}, u32[]{:S(2)}) collective-permute-start(bf16[528,128]{1,0:T(8,128)(2,1)} %get-tuple-element.155), channel_id=1, source_target_pairs={{0,2},{1,3},{2,0},{3,1},{4,6},{5,7},{6,4},{7,5},{8,10},{9,11},{10,... | collective-permute-start | bytes 405512 | tf_op jit(solution)/shard_map/ppermute | solution.py:313
  38.5 2.8 %collective-permute-start.19 = (bf16[528,128]{1,0:T(8,128)(2,1)}, bf16[528,128]{1,0:T(8,128)(2,1)}, u32[]{:S(2)}, u32[]{:S(2)}) collective-permute-start(bf16[528,128]{1,0:T(8,128)(2,1)} %get-tuple-element.156), channel_id=1, source_target_pairs={{0,3},{1,0},{2,1},{3,2},{4,7},{5,4},{6,5},{7,6},{8,11},{9,8},{10,9... | collective-permute-start | bytes 405512 | tf_op jit(solution)/shard_map/ppermute | solution.py:313
  41.3 0.0 collective-permute-done.13.refs_1_.refs_8_
  41.3 4.5 %mix.3 = (bf16[576,320]{1,0:T(8,128)(2,1)}, f32[176,320]{1,0:T(8,128)S(1)}, bf16[448,128]{1,0:T(8,128)(2,1)}, bf16[448,128]{1,0:T(8,128)(2,1)}, bf16[448,128]{1,0:T(8,128)(2,1)}) custom-call(s32[1]{0:T(128)} %bitcast.3.me_ref, bf16[704,576]{1,0:T(8,128)(2,1)S(1)} %get-tuple-element.144.act_ref, f32[2,320]{1,0:T(2,128)S(1)} %get-tuple-element.149.shift_ref, ...), custom_call_target="tpu_custom_call" | custom-call | flops 501350400 | bytes 1474560 | tf_op jit(solution)/shard_map/mix/pallas_call | solution.py:299
  45.8 0.1 collective-permute-start.20
  45.9 0.6 collective-permute-start.21
  46.4 0.0 collective-permute-done.17.refs_0_
  46.5 0.7 copy-done.7
  47.1 3.2 %collective-permute-start.22 = (bf16[448,128]{1,0:T(8,128)(2,1)}, bf16[448,128]{1,0:T(8,128)(2,1)}, u32[]{:S(2)}, u32[]{:S(2)}) collective-permute-start(bf16[448,128]{1,0:T(8,128)(2,1)} %get-tuple-element.161), channel_id=1, source_target_pairs={{0,3},{1,0},{2,1},{3,2},{4,7},{5,4},{6,5},{7,6},{8,11},{9,8},{10,9... | collective-permute-start | bytes 344072 | tf_op jit(solution)/shard_map/ppermute | solution.py:313
  50.4 1.0 %copy-done.5 = bf16[576,360]{1,0:T(8,128)(2,1)S(1)} copy-done((bf16[576,360]{1,0:T(8,128)(2,1)S(1)}, bf16[576,360]{1,0:T(8,128)(2,1)}, u32[]{:S(2)}) %copy-start.5) | copy-done | bytes 414744
  51.4 1.0 %copy-done.6 = bf16[576,320]{1,0:T(8,128)(2,1)S(1)} copy-done((bf16[576,320]{1,0:T(8,128)(2,1)S(1)}, bf16[576,320]{1,0:T(8,128)(2,1)}, u32[]{:S(2)}) %copy-start.6) | copy-done | bytes 368664
  52.4 4.8 %input_grad.1 = bf16[2,288,680]{2,1,0:T(8,128)(2,1)} custom-call(s32[1]{0:T(128)} %bitcast.3.me_ref, bf16[2,288,680]{2,1,0:T(8,128)(2,1)S(1)} %copy-done.3, f32[2,680]{1,0:T(2,128)S(1)} %get-tuple-element.141.refs_5_.mean_ref, f32[2,680]{1,0:T(2,128)S(1)} %get-tuple-element.142.inverse_ref, bf16[360,360]{1,0:T(8,128)(2,1)S(1)} %get-tuple-element.143.same_group_ref, ...), custom_call_target="tpu_custom_call" | custom-call | flops 532684800 | bytes 3133440 | tf_op jit(solution)/shard_map/input_grad/pallas_call | solution.py:299
  57.2 0.0 collective-permute-done.18.refs_1_
  57.2 0.0 copy-start.11
  57.2 0.0 copy-start.13
  57.3 1.7 %adam.2 = (f32[176,360]{1,0:T(8,128)S(1)}, f32[176,360]{1,0:T(8,128)S(1)}, bf16[528,128]{1,0:T(8,128)(2,1)S(1)}) custom-call(f32[2]{0:T(128)S(1)} %pad_maximum_fusion.scales_ref, f32[176,360]{1,0:T(8,128)S(1)} %get-tuple-element.152.refs_5_.own_ref, bf16[528,128]{1,0:T(8,128)(2,1)S(1)} %copy-done.8, bf16[528,128]{1,0:T(8,128)(2,1)} %collective-permute-done.18.refs_1_, ...), custom_call_target="tpu_custom_call" | custom-call | bytes 489600 | tf_op jit(solution)/shard_map/adam/pallas_call | solution.py:299
  58.9 5.6 %conditional.12 = (bf16[528,128]{1,0:T(8,128)(2,1)}, bf16[1]{0:T(256)(128)(2,1)}) conditional(s32[]{:T(128)} %clamp.4, (bf16[528,128]{1,0:T(8,128)(2,1)S(1)}, bf16[1]{0:T(256)(128)(2,1)}) %tuple.49, (bf16[528,128]{1,0:T(8,128)(2,1)S(1)}, bf16[1]{0:T(256)(128)(2,1)}) %tuple.49, (bf16[528,128]{1,0:T(8,128)(2,1)S(1)}, ...), branch_computations={%region_0.1_spmd, %region_1.2_spmd, %region_2.3_spmd} | conditional | bytes 540776
  58.9 0.1 collective-permute-start
  59.0 2.6 %collective-permute-start.1 = (bf16[1]{0:T(256)(128)(2,1)}, bf16[1]{0:T(256)(128)(2,1)}, u32[]{:S(2)}, u32[]{:S(2)}) collective-permute-start(bf16[1]{0:T(256)(128)(2,1)} %get-tuple-element.70), channel_id=1, source_target_pairs={{0,4},{4,8},{8,12},{12,16},{16,20},{20,24},{24,28},{28,0},{1,5},{5... | collective-permute-start | bytes 14 | tf_op jit(solution)/shard_map/cond/branch_0_fun/ppermute | solution.py:313
  61.6 2.9 %collective-permute-done.1 = bf16[1]{0:T(256)(128)(2,1)} collective-permute-done((bf16[1]{0:T(256)(128)(2,1)}, bf16[1]{0:T(256)(128)(2,1)}, u32[]{:S(2)}, u32[]{:S(2)}) %collective-permute-start.1) | collective-permute-done | bytes 34 | tf_op jit(solution)/shard_map/cond/branch_0_fun/ppermute | solution.py:313
  65.1 1.5 %adam.3 = (f32[176,320]{1,0:T(8,128)S(1)}, f32[176,320]{1,0:T(8,128)S(1)}, bf16[448,128]{1,0:T(8,128)(2,1)S(1)}) custom-call(f32[2]{0:T(128)S(1)} %pad_maximum_fusion.scales_ref, f32[176,320]{1,0:T(8,128)S(1)} %get-tuple-element.157.refs_6_.own_ref, bf16[448,128]{1,0:T(8,128)(2,1)} %collective-permute-done.20.refs_0_, ...), custom_call_target="tpu_custom_call" | custom-call | bytes 435200 | tf_op jit(solution)/shard_map/adam/pallas_call | solution.py:299
  66.6 7.1 %conditional.5 = (f32[170,1,680]{2,1,0:T(1,128)}, f32[170,1,680]{2,1,0:T(1,128)}, f32[1,170,680]{2,0,1:T(1,128)}) conditional(s32[]{:T(128)} %clamp.4, (f32[170,1,680]{2,1,0:T(1,128)S(1)}, f32[170,1,680]{2,1,0:T(1,128)S(1)}, f32[176,360]{1,0:T(8,128)S(1)}, f32[176,320]{1,0:T(8,128)S(1)}, bf16[448,128]{1,0:T(8,128)(2,1)S(1)}, ...), branch_computations={%region_3.4_spmd, %region_4.5_spmd, %region_5.6_spmd} | conditional | bytes 2308416 | solution.py:451
  66.6 0.1 collective-permute-start.6
  66.7 1.6 %moments.3 = (f32[170,1,680]{2,1,0:T(1,128)}, f32[170,1,680]{2,1,0:T(1,128)}) custom-call(f32[170,1,680]{2,1,0:T(1,128)S(1)} %get-tuple-element.75.first_ref, f32[170,1,680]{2,1,0:T(1,128)S(1)} %get-tuple-element.76.second_ref, f32[176,360]{1,0:T(8,128)S(1)} %get-tuple-element.77.refs_0_, f32[176,320]{1,0:T(8,128)S(1)} %get-tuple-element.78.refs_1_), custom_call_target="tpu_custom_call" | custom-call | bytes 924800 | tf_op jit(solution)/shard_map/cond/branch_0_fun/moments/pallas_call | solution.py:299
  68.3 3.5 %collective-permute-done.6.refs_3_ = bf16[448,128]{1,0:T(8,128)(2,1)S(1)} collective-permute-done((bf16[448,128]{1,0:T(8,128)(2,1)S(1)}, bf16[448,128]{1,0:T(8,128)(2,1)S(1)}, u32[]{:S(2)}, u32[]{:S(2)}) %collective-permute-start.6) | collective-permute-done | bytes 114720 | tf_op jit(solution)/shard_map/cond/branch_0_fun/ppermute | solution.py:313
  71.8 1.9 %average.3 = f32[170,1,680]{2,1,0:T(1,128)} custom-call(f32[176,360]{1,0:T(8,128)S(1)} %get-tuple-element.81.refs_0_, f32[176,320]{1,0:T(8,128)S(1)} %get-tuple-element.82.refs_1_, bf16[528,128]{1,0:T(8,128)(2,1)} %get-tuple-element.83.refs_2_, bf16[448,128]{1,0:T(8,128)(2,1)S(1)} %collective-permute-done.6.refs_3_), custom_call_target="tpu_custom_call" | custom-call | bytes 924800 | tf_op jit(solution)/shard_map/cond/branch_0_fun/average/pallas_call | solution.py:299
  (26 shorter events, 0.1 us)
Async XLA Ops:
  1.3 1.0 %copy-start = (f32[1,170,680]{2,0,1:T(1,128)S(1)}, f32[1,170,680]{2,0,1:T(1,128)}, u32[]{:S(2)}) copy-start(f32[1,170,680]{2,0,1:T(1,128)} %param.17) | copy-start | bytes 1387204
  2.6 10.6 %collective-permute-start.10 = (bf16[528,128]{1,0:T(8,128)(2,1)S(1)}, bf16[528,128]{1,0:T(8,128)(2,1)S(1)}, u32[]{:S(2)}, u32[]{:S(2)}) collective-permute-start(bf16[528,128]{1,0:T(8,128)(2,1)S(1)} %get-tuple-element.147.refs_0_.refs_2_), channel_id=1, source_target_pairs={{0,2},{1,3},{2,0},{3,1},{4,6},{5,7},{6,4},{7,5},{8,10},{9,11},{10,... | collective-permute-start | bytes 405512 | tf_op jit(solution)/shard_map/ppermute | solution.py:313
  6.7 22.0 %collective-permute-start.11 = (bf16[528,128]{1,0:T(8,128)(2,1)S(1)}, bf16[528,128]{1,0:T(8,128)(2,1)S(1)}, u32[]{:S(2)}, u32[]{:S(2)}) collective-permute-start(bf16[528,128]{1,0:T(8,128)(2,1)S(1)} %get-tuple-element.147.refs_0_.refs_2_), channel_id=1, source_target_pairs={{0,1},{1,2},{2,3},{4,5},{5,6},{6,7},{8,9},{9,10},{10,11},{12,13},{... | collective-permute-start | bytes 405512 | tf_op jit(solution)/shard_map/ppermute | solution.py:321
  10.2 19.8 %collective-permute-start.9 = (bf16[528,128]{1,0:T(8,128)(2,1)S(1)}, bf16[528,128]{1,0:T(8,128)(2,1)S(1)}, u32[]{:S(2)}, u32[]{:S(2)}) collective-permute-start(bf16[528,128]{1,0:T(8,128)(2,1)S(1)} %get-tuple-element.147.refs_0_.refs_2_), channel_id=1, source_target_pairs={{1,0},{2,1},{3,2},{5,4},{6,5},{7,6},{9,8},{10,9},{11,10},{13,12},{... | collective-permute-start | bytes 405512 | tf_op jit(solution)/shard_map/ppermute | solution.py:320
  13.2 16.8 %collective-permute-start.12 = (bf16[528,128]{1,0:T(8,128)(2,1)S(1)}, bf16[528,128]{1,0:T(8,128)(2,1)S(1)}, u32[]{:S(2)}, u32[]{:S(2)}) collective-permute-start(bf16[528,128]{1,0:T(8,128)(2,1)S(1)} %collective-permute-done.10.refs_2_.refs_4_), channel_id=1, source_target_pairs={{1,0},{2,3},{5,4},{6,7},{9,8},{10,11},{13,12},{14,15},{17,16},{18,... | collective-permute-start | bytes 405512 | tf_op jit(solution)/shard_map/ppermute | solution.py:322
  14.5 12.9 %collective-permute-start.14 = (bf16[448,128]{1,0:T(8,128)(2,1)S(1)}, bf16[448,128]{1,0:T(8,128)(2,1)S(1)}, u32[]{:S(2)}, u32[]{:S(2)}) collective-permute-start(bf16[448,128]{1,0:T(8,128)(2,1)S(1)} %get-tuple-element.151.refs_0_.refs_7_), channel_id=1, source_target_pairs={{0,2},{1,3},{2,0},{3,1},{4,6},{5,7},{6,4},{7,5},{8,10},{9,11},{10,... | collective-permute-start | bytes 344072 | tf_op jit(solution)/shard_map/ppermute | solution.py:313
  19.4 19.1 %collective-permute-start.15 = (bf16[448,128]{1,0:T(8,128)(2,1)S(1)}, bf16[448,128]{1,0:T(8,128)(2,1)S(1)}, u32[]{:S(2)}, u32[]{:S(2)}) collective-permute-start(bf16[448,128]{1,0:T(8,128)(2,1)S(1)} %get-tuple-element.151.refs_0_.refs_7_), channel_id=1, source_target_pairs={{0,1},{1,2},{2,3},{4,5},{5,6},{6,7},{8,9},{9,10},{10,11},{12,13},{... | collective-permute-start | bytes 344072 | tf_op jit(solution)/shard_map/ppermute | solution.py:321
  21.4 0.7 copy-start.9
  22.1 1.2 %copy-start.2 = (bf16[2,288,680]{2,1,0:T(8,128)(2,1)S(1)}, bf16[2,288,680]{2,1,0:T(8,128)(2,1)}, u32[]{:S(2)}) copy-start(bf16[2,288,680]{2,1,0:T(8,128)(2,1)} %x_ref.3) | copy-start | bytes 2350084
  23.3 1.2 %copy-start.4 = (bf16[2,288,680]{2,1,0:T(8,128)(2,1)S(1)}, bf16[2,288,680]{2,1,0:T(8,128)(2,1)}, u32[]{:S(2)}) copy-start(bf16[2,288,680]{2,1,0:T(8,128)(2,1)} %out_grad_ref.1) | copy-start | bytes 2350084
  27.4 13.9 %collective-permute-start.13 = (bf16[448,128]{1,0:T(8,128)(2,1)S(1)}, bf16[448,128]{1,0:T(8,128)(2,1)S(1)}, u32[]{:S(2)}, u32[]{:S(2)}) collective-permute-start(bf16[448,128]{1,0:T(8,128)(2,1)S(1)} %get-tuple-element.151.refs_0_.refs_7_), channel_id=1, source_target_pairs={{1,0},{2,1},{3,2},{5,4},{6,5},{7,6},{9,8},{10,9},{11,10},{13,12},{... | collective-permute-start | bytes 344072 | tf_op jit(solution)/shard_map/ppermute | solution.py:320
  28.7 12.6 %collective-permute-start.16 = (bf16[448,128]{1,0:T(8,128)(2,1)S(1)}, bf16[448,128]{1,0:T(8,128)(2,1)S(1)}, u32[]{:S(2)}, u32[]{:S(2)}) collective-permute-start(bf16[448,128]{1,0:T(8,128)(2,1)S(1)} %collective-permute-done.14.refs_2_.refs_9_), channel_id=1, source_target_pairs={{1,0},{2,3},{5,4},{6,7},{9,8},{10,11},{13,12},{14,15},{17,16},{18,... | collective-permute-start | bytes 344072 | tf_op jit(solution)/shard_map/ppermute | solution.py:322
  33.7 12.7 %collective-permute-start.17 = (bf16[528,128]{1,0:T(8,128)(2,1)S(1)}, bf16[528,128]{1,0:T(8,128)(2,1)S(1)}, u32[]{:S(2)}, u32[]{:S(2)}) collective-permute-start(bf16[528,128]{1,0:T(8,128)(2,1)S(1)} %get-tuple-element.154), channel_id=1, source_target_pairs={{0,1},{1,2},{2,3},{3,0},{4,5},{5,6},{6,7},{7,4},{8,9},{9,10},{10,1... | collective-permute-start | bytes 405512 | tf_op jit(solution)/shard_map/ppermute | solution.py:313
  36.4 20.8 %collective-permute-start.18 = (bf16[528,128]{1,0:T(8,128)(2,1)}, bf16[528,128]{1,0:T(8,128)(2,1)}, u32[]{:S(2)}, u32[]{:S(2)}) collective-permute-start(bf16[528,128]{1,0:T(8,128)(2,1)} %get-tuple-element.155), channel_id=1, source_target_pairs={{0,2},{1,3},{2,0},{3,1},{4,6},{5,7},{6,4},{7,5},{8,10},{9,11},{10,... | collective-permute-start | bytes 405512 | tf_op jit(solution)/shard_map/ppermute | solution.py:313
  38.5 18.7 %collective-permute-start.19 = (bf16[528,128]{1,0:T(8,128)(2,1)}, bf16[528,128]{1,0:T(8,128)(2,1)}, u32[]{:S(2)}, u32[]{:S(2)}) collective-permute-start(bf16[528,128]{1,0:T(8,128)(2,1)} %get-tuple-element.156), channel_id=1, source_target_pairs={{0,3},{1,0},{2,1},{3,2},{4,7},{5,4},{6,5},{7,6},{8,11},{9,8},{10,9... | collective-permute-start | bytes 405512 | tf_op jit(solution)/shard_map/ppermute | solution.py:313
  41.3 9.0 %copy-start.3 = (bf16[2,288,680]{2,1,0:T(8,128)(2,1)S(1)}, bf16[2,288,680]{2,1,0:T(8,128)(2,1)}, u32[]{:S(2)}) copy-start(bf16[2,288,680]{2,1,0:T(8,128)(2,1)} %x_ref.3) | copy-start | bytes 2350084
  45.8 19.3 %collective-permute-start.20 = (bf16[448,128]{1,0:T(8,128)(2,1)}, bf16[448,128]{1,0:T(8,128)(2,1)}, u32[]{:S(2)}, u32[]{:S(2)}) collective-permute-start(bf16[448,128]{1,0:T(8,128)(2,1)} %get-tuple-element.159), channel_id=1, source_target_pairs={{0,1},{1,2},{2,3},{3,0},{4,5},{5,6},{6,7},{7,4},{8,9},{9,10},{10,1... | collective-permute-start | bytes 344072 | tf_op jit(solution)/shard_map/ppermute | solution.py:313
  45.9 19.2 %collective-permute-start.21 = (bf16[448,128]{1,0:T(8,128)(2,1)}, bf16[448,128]{1,0:T(8,128)(2,1)}, u32[]{:S(2)}, u32[]{:S(2)}) collective-permute-start(bf16[448,128]{1,0:T(8,128)(2,1)} %get-tuple-element.160), channel_id=1, source_target_pairs={{0,2},{1,3},{2,0},{3,1},{4,6},{5,7},{6,4},{7,5},{8,10},{9,11},{10,... | collective-permute-start | bytes 344072 | tf_op jit(solution)/shard_map/ppermute | solution.py:313
  46.5 0.7 copy-start.7
  47.1 18.0 %collective-permute-start.22 = (bf16[448,128]{1,0:T(8,128)(2,1)}, bf16[448,128]{1,0:T(8,128)(2,1)}, u32[]{:S(2)}, u32[]{:S(2)}) collective-permute-start(bf16[448,128]{1,0:T(8,128)(2,1)} %get-tuple-element.161), channel_id=1, source_target_pairs={{0,3},{1,0},{2,1},{3,2},{4,7},{5,4},{6,5},{7,6},{8,11},{9,8},{10,9... | collective-permute-start | bytes 344072 | tf_op jit(solution)/shard_map/ppermute | solution.py:313
  50.3 1.0 %copy-start.5 = (bf16[576,360]{1,0:T(8,128)(2,1)S(1)}, bf16[576,360]{1,0:T(8,128)(2,1)}, u32[]{:S(2)}) copy-start(bf16[576,360]{1,0:T(8,128)(2,1)} %get-tuple-element.148.refs_0_) | copy-start | bytes 1244164
  51.4 1.0 %copy-start.6 = (bf16[576,320]{1,0:T(8,128)(2,1)S(1)}, bf16[576,320]{1,0:T(8,128)(2,1)}, u32[]{:S(2)}) copy-start(bf16[576,320]{1,0:T(8,128)(2,1)} %get-tuple-element.153.refs_1_) | copy-start | bytes 1105924
  52.4 4.8 %copy-start.1 = (f32[1,170,680]{2,0,1:T(1,128)S(1)}, f32[1,170,680]{2,0,1:T(1,128)}, u32[]{:S(2)}) copy-start(f32[1,170,680]{2,0,1:T(1,128)} %param.17) | copy-start | bytes 1387204
  52.4 4.8 %copy-start.8 = (bf16[528,128]{1,0:T(8,128)(2,1)S(1)}, bf16[528,128]{1,0:T(8,128)(2,1)}, u32[]{:S(2)}) copy-start(bf16[528,128]{1,0:T(8,128)(2,1)} %copy-done.7) | copy-start | bytes 405508
  52.4 4.8 %copy-start.10 = (f32[1,170,680]{2,0,1:T(1,128)S(1)}, f32[1,170,680]{2,0,1:T(1,128)}, u32[]{:S(2)}) copy-start(f32[1,170,680]{2,0,1:T(1,128)} %param.18) | copy-start | bytes 1387204
  52.4 4.8 %copy-start.12 = (f32[1,170,680]{2,0,1:T(1,128)S(1)}, f32[1,170,680]{2,0,1:T(1,128)}, u32[]{:S(2)}) copy-start(f32[1,170,680]{2,0,1:T(1,128)} %param.19) | copy-start | bytes 1387204
  57.2 7.9 %copy-start.11 = (f32[1,170,680]{2,0,1:T(1,128)S(1)}, f32[1,170,680]{2,0,1:T(1,128)}, u32[]{:S(2)}) copy-start(f32[1,170,680]{2,0,1:T(1,128)} %param.18) | copy-start | bytes 1387204
  57.2 7.9 %copy-start.13 = (f32[1,170,680]{2,0,1:T(1,128)S(1)}, f32[1,170,680]{2,0,1:T(1,128)}, u32[]{:S(2)}) copy-start(f32[1,170,680]{2,0,1:T(1,128)} %param.19) | copy-start | bytes 1387204
  58.9 5.6 %collective-permute-start = (bf16[528,128]{1,0:T(8,128)(2,1)S(1)}, bf16[528,128]{1,0:T(8,128)(2,1)}, u32[]{:S(2)}, u32[]{:S(2)}) collective-permute-start(bf16[528,128]{1,0:T(8,128)(2,1)S(1)} %get-tuple-element.69), channel_id=1, source_target_pairs={{0,4},{4,8},{8,12},{12,16},{16,20},{20,24},{24,28},{28,0},{1,5},{5... | collective-permute-start | bytes 405512 | tf_op jit(solution)/shard_map/cond/branch_0_fun/ppermute | solution.py:313
  59.0 5.5 %collective-permute-start.1 = (bf16[1]{0:T(256)(128)(2,1)}, bf16[1]{0:T(256)(128)(2,1)}, u32[]{:S(2)}, u32[]{:S(2)}) collective-permute-start(bf16[1]{0:T(256)(128)(2,1)} %get-tuple-element.70), channel_id=1, source_target_pairs={{0,4},{4,8},{8,12},{12,16},{16,20},{20,24},{24,28},{28,0},{1,5},{5... | collective-permute-start | bytes 14 | tf_op jit(solution)/shard_map/cond/branch_0_fun/ppermute | solution.py:313
  66.6 5.2 %collective-permute-start.6 = (bf16[448,128]{1,0:T(8,128)(2,1)S(1)}, bf16[448,128]{1,0:T(8,128)(2,1)S(1)}, u32[]{:S(2)}, u32[]{:S(2)}) collective-permute-start(bf16[448,128]{1,0:T(8,128)(2,1)S(1)} %get-tuple-element.84), channel_id=1, source_target_pairs={{0,4},{4,8},{8,12},{12,16},{16,20},{20,24},{24,28},{28,0},{1,5},{5... | collective-permute-start | bytes 344072 | tf_op jit(solution)/shard_map/cond/branch_0_fun/ppermute | solution.py:313

commit v5 on v3

--- a/solution.py
+++ b/solution.py
@@ -24,11 +24,15 @@
     return -(-rows // TILE_ROWS) * TILE_ROWS
 
 
+def packed_rows(rows):
+    return padded(rows + 1)
+
+
 class Packing:
     def __init__(self, rows, start, stop):
         self.rows, self.start, self.stop = rows, start, stop
         self.columns = stop - start
-        self.deep = padded(rows)
+        self.deep = packed_rows(rows)
         self.tiles, self.rest = divmod(self.columns, LANES)
         fold = LANES // self.rest if self.rest else 1
         self.fold_rows = padded(-(-self.deep // fold))
@@ -162,13 +166,15 @@
 
 def mix_kernel(shards, pack, act_ref, shift_ref, out_grad_ref, same_group_ref, *refs):
     weight_refs, token_ref, refs = refs[:shards], refs[shards], refs[shards + 1 :]
-    grad_hidden_ref, own_ref = refs[:2]
-    send_refs, (weight_ref, kept_ref, sem) = refs[2 : 1 + shards], refs[1 + shards :]
+    grad_hidden_ref, weight_out_ref, own_ref = refs[:3]
+    send_refs, (weight_ref, kept_ref, sems) = refs[3 : 2 + shards], refs[2 + shards :]
     samples, positions, columns = out_grad_ref.shape
     entries = positions * GSIZE
     deep = pack.deep
     for slot, shard_ref in enumerate(weight_refs):
         pack.unpack(shard_ref, weight_ref, slot * deep)
+    weight_copy = pltpu.make_async_copy(weight_ref, weight_out_ref, sems.at[0])
+    weight_copy.start()
     same_group = same_group_ref[:columns, :columns]
     hidden = lax.dot_general(
         act_ref[...], weight_ref[...], (((0,), (0,)), ((), ())), preferred_element_type=jnp.float32
@@ -194,30 +200,47 @@
         kept_ref[i * positions : (i + 1) * positions, :] = (
             inverse[i : i + 1] * (grads[i] - first - normed[i] * second)
         ).astype(jnp.bfloat16)
-    copy = pltpu.make_async_copy(kept_ref, grad_hidden_ref, sem)
+    copy = pltpu.make_async_copy(kept_ref, grad_hidden_ref, sems.at[1])
     copy.start()
     grad = jnp.dot(act_ref[...], kept_ref[...], preferred_element_type=jnp.float32)
     for slot, send_ref in enumerate(send_refs, 1):
         pack.write(send_ref, grad[slot * deep : (slot + 1) * deep])
     own_ref[...] = grad[:deep]
+    weight_copy.wait()
     copy.wait()
 
 
-def input_grad_kernel(shards, packs, me_ref, x_ref, mean_ref, inverse_ref, same_group_ref, *refs):
-    grad_refs, refs = refs[: len(packs)], refs[len(packs) :]
-    weight_refs, out_ref, rows_ref = refs[:-2], refs[-2], refs[-1]
+def input_grad_kernel(shards, packs, me_ref, mean_ref, inverse_ref, same_group_ref, x_hbm, *refs):
+    count = len(packs)
+    grad_hbms, weight_hbms, out_ref = refs[:count], refs[count : 2 * count], refs[2 * count]
+    rows_ref, x_ref, sems = refs[2 * count + 1 : 2 * count + 4]
+    grad_refs, weight_refs = refs[2 * count + 4 : 3 * count + 4], refs[3 * count + 4 :]
+    copies = [
+        pltpu.make_async_copy(source, target, sems.at[i])
+        for i, (source, target) in enumerate(
+            zip((*weight_hbms, *grad_hbms, x_hbm), (*weight_refs, *grad_refs, x_ref))
+        )
+    ]
+    for copy in copies:
+        copy.start()
     samples, positions, channels = x_ref.shape
     entries = positions * GSIZE
     rows = channels // shards
+    weights = []
+    for index, (pack, weight_ref) in enumerate(zip(packs, weight_refs)):
+        copies[index].wait()
+        for slot in range(shards):
+            rows_ref[slot * rows : (slot + 1) * rows, : pack.columns] = weight_ref[
+                slot * pack.deep : (slot + 1) * pack.deep, :
+            ].astype(jnp.float32)[:rows]
+        weights.append(pltpu.roll(rows_ref[:, : pack.columns], me_ref[0] * rows, 0).astype(jnp.bfloat16))
     grad_act = 0.0
-    for index, (pack, grad_ref) in enumerate(zip(packs, grad_refs)):
-        for slot in range(shards):
-            block = pack.read(weight_refs[index * shards + slot])
-            rows_ref[slot * rows : (slot + 1) * rows, : pack.columns] = block[:rows]
-        weight = pltpu.roll(rows_ref[:, : pack.columns], me_ref[0] * rows, 0).astype(jnp.bfloat16)
+    for index, (grad_ref, weight) in enumerate(zip(grad_refs, weights)):
+        copies[count + index].wait()
         grad_act += lax.dot_general(
             grad_ref[...], weight, (((1,), (1,)), ((), ())), preferred_element_type=jnp.float32
         )
+    copies[-1].wait()
     inverse = inverse_ref[...]
     normed = [
         (x_ref[i].astype(jnp.float32) - mean_ref[i : i + 1, :]) * inverse[i : i + 1] for i in range(samples)
@@ -235,23 +258,59 @@
         out_ref[i] = (inverse[i : i + 1] * (grads[i] - first - normed[i] * second)).astype(jnp.bfloat16)
 
 
-def adam_kernel(shards, pack, scales_ref, own_ref, *refs):
-    other_refs, refs = refs[: shards - 1], refs[shards - 1 :]
-    params_ref, first_ref, second_ref, token_ref, grad_ref, moved_ref, sent_ref = refs
+def adam_step(shards, pack, scales_ref, own_ref, other_refs, blocks, grad_ref, moved_ref):
     rows = pack.rows
     total = own_ref[...]
     for other_ref in other_refs:
         total = total + pack.read(other_ref)
     grad_ref[...] = total / shards
     grad = grad_ref[:rows, :]
-    columns = slice(pack.start, pack.stop)
-    first_new = BETA_ONE * first_ref[:, 0, columns] + (1.0 - BETA_ONE) * grad
-    second_new = BETA_TWO * second_ref[:, 0, columns] + (1.0 - BETA_TWO) * grad * grad
+    params, first, second = blocks()
+    first_new = BETA_ONE * first + (1.0 - BETA_ONE) * grad
+    second_new = BETA_TWO * second + (1.0 - BETA_TWO) * grad * grad
     update = (scales_ref[0] * first_new) / (jnp.sqrt(second_new * scales_ref[1]) + ADAM_EPS)
-    if rows < pack.deep:
-        moved_ref[rows // 8 * 8 :, :] = jnp.zeros((pack.deep - rows // 8 * 8, pack.columns), jnp.float32)
-    moved_ref[:rows, :] = params_ref[:, 0, columns] - update
+    moved_ref[rows // 8 * 8 :, :] = jnp.zeros((pack.deep - rows // 8 * 8, pack.columns), jnp.float32)
+    moved_ref[:rows, :] = params - update
+
+
+def first_adam_kernel(shards, packs, scales_ref, push_ref, own_ref, *refs):
+    pack, later = packs
+    other_refs, refs = refs[: shards - 1], refs[shards - 1 :]
+    hbm_refs, token_ref, (grad_ref, moved_ref, sent_ref), later_refs = refs[:3], refs[3], refs[4:7], refs[7:10]
+    row_refs, sems = refs[10:13], refs[13]
+    copies = [
+        pltpu.make_async_copy(source, target, sems.at[i])
+        for i, (source, target) in enumerate(zip(hbm_refs, row_refs))
+    ]
+    for copy in copies:
+        copy.start()
+
+    def blocks():
+        for copy in copies:
+            copy.wait()
+        return [row_ref[:, 0, pack.start : pack.stop] for row_ref in row_refs]
+
+    adam_step(shards, pack, scales_ref, own_ref, other_refs, blocks, grad_ref, moved_ref)
+    moved = moved_ref[...]
+    spare = lax.broadcasted_iota(jnp.int32, moved.shape, 0) == pack.rows
+    pack.write(sent_ref, jnp.where(spare, push_ref[0], moved))
+    for row_ref, later_ref in zip(row_refs, later_refs):
+        later_ref[...] = row_ref[:, 0, later.start : later.stop]
+
+
+def second_adam_kernel(shards, pack, scales_ref, own_ref, *refs):
+    other_refs, refs = refs[: shards - 1], refs[shards - 1 :]
+    block_refs, token_ref, (grad_ref, moved_ref, sent_ref) = refs[:3], refs[3], refs[4:]
+    adam_step(
+        shards, pack, scales_ref, own_ref, other_refs, lambda: [ref[...] for ref in block_refs], grad_ref, moved_ref
+    )
     pack.write(sent_ref, moved_ref[...])
+
+
+def half_average_kernel(pack, push_ref, moved_ref, other_ref, mean_ref, push_out_ref):
+    other = pack.read(other_ref)
+    mean_ref[...] = 0.5 * (moved_ref[...] + other)
+    push_out_ref[0:1, :] = 0.5 * (push_ref[0] + other[pack.rows : pack.rows + 1, :LANES])
 
 
 def moments_kernel(packs, first_ref, second_ref, *refs):
@@ -262,15 +321,10 @@
     second_out[:, 0, :] = BETA_TWO * second_ref[:, 0, :] + (1.0 - BETA_TWO) * grad * grad
 
 
-def average_kernel(packs, *refs):
-    moved_refs, other_refs = refs[: len(packs)], refs[len(packs) : -3]
-    out_ref, rows_ref, sem = refs[-3:]
+def average_kernel(pack, mean_ref, moved_ref, other_ref, out_ref, rows_ref, sem):
     rows = out_ref.shape[0]
-    pieces = [
-        0.5 * (moved_ref[...] + pack.read(other_ref))
-        for pack, moved_ref, other_ref in zip(packs, moved_refs, other_refs)
-    ]
-    rows_ref[:, 0, :] = jnp.concatenate(pieces, axis=1)[:rows]
+    later = 0.5 * (moved_ref[...] + pack.read(other_ref))
+    rows_ref[:, 0, :] = jnp.concatenate([mean_ref[...], later], axis=1)[:rows]
     copy = pltpu.make_async_copy(rows_ref, out_ref, sem)
     copy.start()
     copy.wait()
@@ -295,6 +349,10 @@
     )(*operands)
 
 
+def stay(array):
+    return pltpu.with_memory_space_constraint(array, pltpu.HBM)
+
+
 def moved_on(block, axis, distance):
     size = lax.axis_size(axis)
     return lax.ppermute(block, axis, [(i, (i + distance) % size) for i in range(size)])
@@ -312,7 +370,7 @@
     tokens = samples * positions
     shards = lax.axis_size("dp")
     rows = params.shape[1]
-    deep = padded(rows)
+    deep = packed_rows(rows)
     me = lax.axis_index("dp").astype(jnp.int32).reshape(1)
     packs = [Packing(rows, start, stop) for start, stop in column_cuts(channels)]
     params, first_moment, second_moment = (
@@ -354,28 +412,33 @@
         elements=tokens * channels,
     )
 
-    hidden_grads, owns, arrived = [], [], []
+    hidden_grads, full_weights, owns, arrived = [], [], [], []
     token = mean_in
     shifts, out_grads = pieces[: len(packs)], pieces[len(packs) :]
     for pack, shard_list, shift, out_grad_piece in zip(packs, weights, shifts, out_grads):
-        grad_hidden, own, *sends = call(
+        grad_hidden, full_weight, own, *sends = call(
             functools.partial(mix_kernel, shards, pack),
             "mix",
-            (pltpu.HBM((tokens, pack.columns), jnp.bfloat16), pack.block())
+            (
+                pltpu.HBM((tokens, pack.columns), jnp.bfloat16),
+                pltpu.HBM((shards * deep, pack.columns), jnp.bfloat16),
+                pack.block(),
+            )
             + (pack.payload(),) * (shards - 1),
             [BLOCKS] * (4 + shards) + [TOKEN],
             (activation, shift, out_grad_piece, same_group, *shard_list, token),
             scratch=[
                 pltpu.VMEM((shards * deep, pack.columns), jnp.bfloat16),
                 pltpu.VMEM((tokens, pack.columns), jnp.bfloat16),
-                pltpu.SemaphoreType.DMA,
+                pltpu.SemaphoreType.DMA((2,)),
             ],
-            out_specs=(IN_HBM,) + (BLOCKS,) * shards,
+            out_specs=(IN_HBM,) * 2 + (BLOCKS,) * shards,
             flops=4 * tokens * channels * pack.columns,
             elements=tokens * pack.columns,
         )
         token = own
         hidden_grads.append(grad_hidden)
+        full_weights.append(full_weight)
         owns.append(own)
         arrived.append([moved_on(send, "dp", slot) for slot, send in enumerate(sends, 1)])
 
@@ -383,22 +446,18 @@
         functools.partial(input_grad_kernel, shards, packs),
         "input_grad",
         jax.ShapeDtypeStruct(block_input.shape, jnp.bfloat16),
-        [SCALARS] + [BLOCKS] * (4 + len(packs) * (1 + shards)),
-        (me, block_input, mean_in, inverse_in, same_group, *hidden_grads, *weights[0], *weights[1]),
-        scratch=[pltpu.VMEM((channels, max(pack.columns for pack in packs)), jnp.float32)],
+        [SCALARS] + [BLOCKS] * 3 + [IN_HBM] * (1 + 2 * len(packs)),
+        (me, mean_in, inverse_in, same_group, *map(stay, (block_input, *hidden_grads, *full_weights))),
+        scratch=[
+            pltpu.VMEM((channels, max(pack.columns for pack in packs)), jnp.float32),
+            pltpu.VMEM(block_input.shape, jnp.bfloat16),
+            pltpu.SemaphoreType.DMA((1 + 2 * len(packs),)),
+            *(pltpu.VMEM((tokens, pack.columns), jnp.bfloat16) for pack in packs),
+            *(pltpu.VMEM((shards * deep, pack.columns), jnp.bfloat16) for pack in packs),
+        ],
         flops=2 * tokens * channels * channels,
         elements=tokens * channels,
     )
-
-    def adam(pack, own, others, token):
-        return call(
-            functools.partial(adam_kernel, shards, pack),
-            "adam",
-            (pack.block(), pack.block(), pack.payload()),
-            [SCALARS] + [BLOCKS] * (3 + shards) + [TOKEN],
-            (scales, own, *others, params, first_moment, second_moment, token),
-            elements=rows * pack.columns,
-        )
 
     def moments(*grads):
         return call(
@@ -410,37 +469,60 @@
             elements=rows * channels,
         )
 
-    def average(*blocks):
+    def from_behind(finish, *operands):
+        def branch(distance):
+            return lambda *values: finish(lambda block: moved_on(block, "replica", distance), *values)
+
+        return lax.switch(distance_bits, [branch(1 << power) for power in range(level_count)], *operands)
+
+    early, late = packs
+    rows_kept = jax.ShapeDtypeStruct((rows, late.columns), jnp.float32)
+    grad_a, moved_a, sent_a, *late_blocks = call(
+        functools.partial(first_adam_kernel, shards, packs),
+        "adam",
+        (early.block(), early.block(), early.payload()) + (rows_kept,) * 3,
+        [SCALARS] * 2 + [BLOCKS] * shards + [IN_HBM] * 3 + [TOKEN],
+        (scales, push_weight, owns[0], *arrived[0], stay(params), stay(first_moment), stay(second_moment), token),
+        scratch=[pltpu.VMEM(params.shape, jnp.float32)] * 3 + [pltpu.SemaphoreType.DMA((3,))],
+        elements=rows * channels,
+    )
+
+    def finish_early(move, sent, moved):
         return call(
-            functools.partial(average_kernel, packs),
+            functools.partial(half_average_kernel, early),
+            "half_average",
+            (early.block(), jax.ShapeDtypeStruct((8, LANES), jnp.float32)),
+            [SCALARS] + [BLOCKS] * 2,
+            (push_weight, moved, move(sent)),
+            elements=rows * early.columns,
+        )
+
+    mean_a, weight_tile = from_behind(finish_early, sent_a, moved_a)
+    grad_b, moved_b, sent_b = call(
+        functools.partial(second_adam_kernel, shards, late),
+        "adam",
+        (late.block(), late.block(), late.payload()),
+        [SCALARS] + [BLOCKS] * (3 + shards) + [TOKEN],
+        (scales, owns[1], *arrived[1], *late_blocks, mean_a),
+        elements=rows * late.columns,
+    )
+
+    def finish_late(move, sent, grad_a, grad_b, mean_a, moved_b):
+        other = move(sent)
+        averaged = call(
+            functools.partial(average_kernel, late),
             "average",
             pltpu.HBM(params.shape, jnp.float32),
-            [BLOCKS] * (2 * len(packs)),
-            blocks,
+            [BLOCKS] * 3,
+            (mean_a, moved_b, other),
             scratch=[pltpu.VMEM(params.shape, jnp.float32), pltpu.SemaphoreType.DMA],
             out_specs=IN_HBM,
             elements=rows * channels,
         )
-
-    def from_behind(finish, *operands):
-        def branch(distance):
-            return lambda *values: finish(lambda block: moved_on(block, "replica", distance), *values)
-
-        return lax.switch(distance_bits, [branch(1 << power) for power in range(level_count)], *operands)
-
-    grad_a, moved_a, sent_a = adam(packs[0], owns[0], arrived[0], token)
-    other_a, other_weight = from_behind(
-        lambda move, sent, weight: (move(sent), move(weight)), sent_a, push_weight.astype(jnp.bfloat16)
-    )
-    grad_b, moved_b, sent_b = adam(packs[1], owns[1], arrived[1], other_a)
-
-    def finish(move, sent, *values):
-        grads, moved, other_first = values[:2], values[2:4], values[4]
-        other = move(sent)
-        return (*moments(*grads), average(*moved, other_first, other))
-
-    first_new, second_new, averaged = from_behind(finish, sent_b, grad_a, grad_b, moved_a, moved_b, other_a)
-    new_weight = 0.5 * (push_weight + other_weight.astype(jnp.float32))
+        return (*moments(grad_a, grad_b), averaged)
+
+    first_new, second_new, averaged = from_behind(finish_late, sent_b, grad_a, grad_b, mean_a, moved_b)
+    new_weight = weight_tile[0, :1]
     return (
         grad_input,
         *(jnp.transpose(array, (1, 0, 2)) for array in (averaged, first_new, second_new)),

time: 64.8 us -> 61.7 us (0.952)
  starting transfers between devices: 29.3 us -> 26.6 us
  waiting for transfers between devices: 2.73 us -> 5.22 us
  between operations: 4.08 us -> 2.39 us
  local copies, waits for them, and re-layouts: 5.99 us -> 4.7 us
    ppermute x15 -> x14, starting transfers between devices: 29.3 us -> 26.6 us  [moved_on(): lax.ppermute(block, axis, [(i, (i + distance) % size) for i in range(size)])]
    ppermute x15 -> x14, waiting for transfers between devices: 2.73 us -> 5.22 us  [moved_on(): lax.ppermute(block, axis, [(i, (i + distance) % size) for i in range(size)])]
    unnamed x24 -> x12, local copies, waits for them, and re-layouts: 5.99 us -> 4.18 us
    pallas_call x9 -> x10, Pallas kernels: 21.9 us -> 22.3 us  [call(): pl.pallas_call(kernel, out_shape=outs, in_specs=specs, out_specs=out_spec...]
  transfers between devices with their start and end apart: 15 -> 14, of which waited for: 2 -> 2; matrix products, arithmetic and copies ran while one was open for 0% -> 1% of each run, Pallas kernels for 28% -> 33%
where the time goes in v5:
time: 61.7 us; the launch traced here: 61.3 us
  starting transfers between devices  26.6 us (43%)
  Pallas kernels  22.3 us (36%)
  waiting for transfers between devices  5.22 us (8%)
  local copies, waits for them, and re-layouts  4.7 us (8%)
  between operations  2.39 us (4%)
    ppermute x14, starting transfers between devices, moved_on(): lax.ppermute(block, axis, [(i, (i + distance) % size) for i in range(size)])  26.6 us
    pallas_call x10, Pallas kernels, call(): pl.pallas_call(kernel, out_shape=outs, in_specs=specs, out_specs=out_spec...  22.3 us
    ppermute x14, waiting for transfers between devices, moved_on(): lax.ppermute(block, axis, [(i, (i + distance) % size) for i in range(size)])  5.22 us
    unnamed x12, local copies, waits for them, and re-layouts  4.18 us
  transfers between devices with their start and end apart: 14, of which 2 were waited for; matrix products, arithmetic and copies ran while one was open for 1% of the time, Pallas kernels for 33%

profile of v5, /device:TPU:0, one launch (start us, length us, event | category | flops | bytes accessed | tf_op | source)
XLA Modules:
  0.0 61.3 jit_solution(6408005366671612395)
XLA Ops:
  1.3 0.0 copy-start.1
  1.3 1.0 %copy-done.1 = f32[1,170,680]{2,0,1:T(1,128)S(1)} copy-done((f32[1,170,680]{2,0,1:T(1,128)S(1)}, f32[1,170,680]{2,0,1:T(1,128)}, u32[]{:S(2)}) %copy-start.1) | copy-done | bytes 462424
  2.3 0.3 cast.1
  2.6 3.1 %collective-permute-start.8 = (bf16[528,128]{1,0:T(8,128)(2,1)S(1)}, bf16[528,128]{1,0:T(8,128)(2,1)S(1)}, u32[]{:S(2)}, u32[]{:S(2)}) collective-permute-start(bf16[528,128]{1,0:T(8,128)(2,1)S(1)} %get-tuple-element.157.refs_0_), channel_id=1, source_target_pairs={{0,1},{1,2},{2,3},{3,0},{4,5},{5,6},{6,7},{7,4},{8,9},{9,10},{10,1... | collective-permute-start | bytes 405512 | tf_op jit(solution)/shard_map/ppermute | solution.py:358
  5.7 2.6 %collective-permute-start.7 = (bf16[528,128]{1,0:T(8,128)(2,1)S(1)}, bf16[528,128]{1,0:T(8,128)(2,1)S(1)}, u32[]{:S(2)}, u32[]{:S(2)}) collective-permute-start(bf16[528,128]{1,0:T(8,128)(2,1)S(1)} %get-tuple-element.157.refs_0_), channel_id=1, source_target_pairs={{0,2},{1,3},{2,0},{3,1},{4,6},{5,7},{6,4},{7,5},{8,10},{9,11},{10,... | collective-permute-start | bytes 405512 | tf_op jit(solution)/shard_map/ppermute | solution.py:358
  8.3 1.3 %collective-permute-start.6 = (bf16[528,128]{1,0:T(8,128)(2,1)S(1)}, bf16[528,128]{1,0:T(8,128)(2,1)S(1)}, u32[]{:S(2)}, u32[]{:S(2)}) collective-permute-start(bf16[528,128]{1,0:T(8,128)(2,1)S(1)} %get-tuple-element.157.refs_0_), channel_id=1, source_target_pairs={{0,3},{1,0},{2,1},{3,2},{4,7},{5,4},{6,5},{7,6},{8,11},{9,8},{10,9... | collective-permute-start | bytes 405512 | tf_op jit(solution)/shard_map/ppermute | solution.py:358
  9.6 0.7 %collective-permute-start.11 = (bf16[448,128]{1,0:T(8,128)(2,1)S(1)}, bf16[448,128]{1,0:T(8,128)(2,1)S(1)}, u32[]{:S(2)}, u32[]{:S(2)}) collective-permute-start(bf16[448,128]{1,0:T(8,128)(2,1)S(1)} %get-tuple-element.161.refs_0_), channel_id=1, source_target_pairs={{0,1},{1,2},{2,3},{3,0},{4,5},{5,6},{6,7},{7,4},{8,9},{9,10},{10,1... | collective-permute-start | bytes 344072 | tf_op jit(solution)/shard_map/ppermute | solution.py:358
  10.3 0.3 collective-permute-start.10
  11.4 0.0 copy-start.3
  11.4 0.1 pad_maximum_fusion.scales_ref
  11.5 0.6 copy-done.3
  12.1 1.2 %copy-done = bf16[2,288,680]{2,1,0:T(8,128)(2,1)S(1)} copy-done((bf16[2,288,680]{2,1,0:T(8,128)(2,1)S(1)}, bf16[2,288,680]{2,1,0:T(8,128)(2,1)}, u32[]{:S(2)}) %copy-start) | copy-done | bytes 783384
  13.2 1.2 %copy-done.2 = bf16[2,288,680]{2,1,0:T(8,128)(2,1)S(1)} copy-done((bf16[2,288,680]{2,1,0:T(8,128)(2,1)S(1)}, bf16[2,288,680]{2,1,0:T(8,128)(2,1)}, u32[]{:S(2)}) %copy-start.2) | copy-done | bytes 783384
  14.4 2.9 %norm_in.1 = (bf16[704,576]{1,0:T(8,128)(2,1)S(1)}, f32[2,680]{1,0:T(2,128)S(1)}, f32[2,680]{1,0:T(2,128)S(1)}, bf16[360,360]{1,0:T(8,128)(2,1)S(1)}, f32[2,360]...) custom-call(s32[1]{0:T(128)} %bitcast.6.me_ref, ...), custom_call_target="tpu_custom_call" | custom-call | bytes 3133440 | tf_op jit(solution)/shard_map/norm_in/pallas_call | solution.py:340
  17.3 0.0 collective-permute-done.8.refs_3_
  17.3 2.9 %collective-permute-start.9 = (bf16[448,128]{1,0:T(8,128)(2,1)S(1)}, bf16[448,128]{1,0:T(8,128)(2,1)S(1)}, u32[]{:S(2)}, u32[]{:S(2)}) collective-permute-start(bf16[448,128]{1,0:T(8,128)(2,1)S(1)} %get-tuple-element.161.refs_0_), channel_id=1, source_target_pairs={{0,3},{1,0},{2,1},{3,2},{4,7},{5,4},{6,5},{7,6},{8,11},{9,8},{10,9... | collective-permute-start | bytes 344072 | tf_op jit(solution)/shard_map/ppermute | solution.py:358
  20.2 0.0 collective-permute-done.7.refs_2_
  20.2 0.0 collective-permute-done.6.refs_1_
  20.2 2.9 %mix.2 = (bf16[576,360]{1,0:T(8,128)(2,1)}, bf16[704,360]{1,0:T(8,128)(2,1)}, f32[176,360]{1,0:T(8,128)S(1)}, bf16[528,128]{1,0:T(8,128)(2,1)S(1)}, bf16[528,128...) custom-call(bf16[704,576]{1,0:T(8,128)(2,1)S(1)} %get-tuple-element.154.act_ref, ...), custom_call_target="tpu_custom_call" | custom-call | flops 564019200 | bytes 1658880 | tf_op jit(solution)/shard_map/mix/pallas_call | solution.py:340
  23.1 5.4 %collective-permute-start.12 = (bf16[528,128]{1,0:T(8,128)(2,1)S(1)}, bf16[528,128]{1,0:T(8,128)(2,1)S(1)}, u32[]{:S(2)}, u32[]{:S(2)}) collective-permute-start(bf16[528,128]{1,0:T(8,128)(2,1)S(1)} %get-tuple-element.166), channel_id=1, source_target_pairs={{0,1},{1,2},{2,3},{3,0},{4,5},{5,6},{6,7},{7,4},{8,9},{9,10},{10,1... | collective-permute-start | bytes 405512 | tf_op jit(solution)/shard_map/ppermute | solution.py:358
  28.5 2.7 %collective-permute-start.13 = (bf16[528,128]{1,0:T(8,128)(2,1)S(1)}, bf16[528,128]{1,0:T(8,128)(2,1)S(1)}, u32[]{:S(2)}, u32[]{:S(2)}) collective-permute-start(bf16[528,128]{1,0:T(8,128)(2,1)S(1)} %get-tuple-element.167), channel_id=1, source_target_pairs={{0,2},{1,3},{2,0},{3,1},{4,6},{5,7},{6,4},{7,5},{8,10},{9,11},{10,... | collective-permute-start | bytes 405512 | tf_op jit(solution)/shard_map/ppermute | solution.py:358
  31.3 0.0 collective-permute-done.11.refs_3_
  31.3 0.0 collective-permute-start.14
  31.3 0.0 collective-permute-done.10.refs_2_
  31.3 0.0 collective-permute-done.9.refs_1_
  31.3 3.0 %mix.3 = (bf16[576,320]{1,0:T(8,128)(2,1)}, bf16[704,320]{1,0:T(8,128)(2,1)}, f32[176,320]{1,0:T(8,128)S(1)}, bf16[448,128]{1,0:T(8,128)(2,1)S(1)}, bf16[448,128...) custom-call(bf16[704,576]{1,0:T(8,128)(2,1)S(1)} %get-tuple-element.154.act_ref, ...), custom_call_target="tpu_custom_call" | custom-call | flops 501350400 | bytes 1474560 | tf_op jit(solution)/shard_map/mix/pallas_call | solution.py:340
  34.3 2.1 %collective-permute-start.15 = (bf16[448,128]{1,0:T(8,128)(2,1)S(1)}, bf16[448,128]{1,0:T(8,128)(2,1)S(1)}, u32[]{:S(2)}, u32[]{:S(2)}) collective-permute-start(bf16[448,128]{1,0:T(8,128)(2,1)S(1)} %get-tuple-element.171), channel_id=1, source_target_pairs={{0,1},{1,2},{2,3},{3,0},{4,5},{5,6},{6,7},{7,4},{8,9},{9,10},{10,1... | collective-permute-start | bytes 344072 | tf_op jit(solution)/shard_map/ppermute | solution.py:358
  36.3 0.2 collective-permute-start.16
  36.5 0.0 collective-permute-done.12.refs_0_
  36.5 2.2 %collective-permute-start.17 = (bf16[448,128]{1,0:T(8,128)(2,1)S(1)}, bf16[448,128]{1,0:T(8,128)(2,1)S(1)}, u32[]{:S(2)}, u32[]{:S(2)}) collective-permute-start(bf16[448,128]{1,0:T(8,128)(2,1)S(1)} %get-tuple-element.173), channel_id=1, source_target_pairs={{0,3},{1,0},{2,1},{3,2},{4,7},{5,4},{6,5},{7,6},{8,11},{9,8},{10,9... | collective-permute-start | bytes 344072 | tf_op jit(solution)/shard_map/ppermute | solution.py:358
  38.8 6.2 %input_grad.1 = bf16[2,288,680]{2,1,0:T(8,128)(2,1)} custom-call(s32[1]{0:T(128)} %bitcast.6.me_ref, f32[2,680]{1,0:T(2,128)S(1)} %get-tuple-element.151.refs_4_.mean_ref, f32[2,680]{1,0:T(2,128)S(1)} %get-tuple-element.152.inverse_ref, bf16[360,360]{1,0:T(8,128)(2,1)S(1)} %get-tuple-element.153.same_group_ref, bf16[2,288,680]{2,1,0:T(8,128)(2,1)} %x_hbm.1, ...), custom_call_target="tpu_custom_call" | custom-call | flops 532684800 | bytes 3133440 | tf_op jit(solution)/shard_map/input_grad/pallas_call | solution.py:340
  45.0 0.0 collective-permute-done.13.refs_1_
  45.0 2.8 %adam.2 = (f32[176,360]{1,0:T(8,128)S(1)}, f32[176,360]{1,0:T(8,128)S(1)}, bf16[528,128]{1,0:T(8,128)(2,1)S(1)}, f32[170,320]{1,0:T(8,128)S(1)}, f32[170,320]{1,0:T(8,128)S(1)}, /*index=5*/f32[170,320]{1,0:T(8,128)S(1)}) custom-call(f32[2]{0:T(128)S(1)} %pad_maximum_fusion.scales_ref, f32[1]{0:T(128)S(6)} %copy.28.push_ref, ...), custom_call_target="tpu_custom_call" | custom-call | bytes 924800 | tf_op jit(solution)/shard_map/adam/pallas_call | solution.py:340
  47.8 6.3 %conditional.2 = (f32[176,360]{1,0:T(8,128)S(1)}, f32[1]{0:T(128)}) conditional(s32[]{:T(128)} %clamp.4, (bf16[528,128]{1,0:T(8,128)(2,1)S(1)}, f32[1]{0:T(128)}, f32[176,360]{1,0:T(8,128)S(1)}) %tuple.38, (bf16[528,128]{1,0:T(8,128)(2,1)S(1)}, f32[1]{0:T(128)}, f32[176,360]{1,0:T(8,128)S(1)}) %tuple.38, ...), branch_computations={%region_0.1_spmd, %region_1.2_spmd, %region_2.3_spmd} | conditional | bytes 1030336 | solution.py:476
  47.9 1.6 %collective-permute-start.2 = (bf16[528,128]{1,0:T(8,128)(2,1)S(1)}, bf16[528,128]{1,0:T(8,128)(2,1)S(1)}, u32[]{:S(2)}, u32[]{:S(2)}) collective-permute-start(bf16[528,128]{1,0:T(8,128)(2,1)S(1)} %get-tuple-element.80), channel_id=1, source_target_pairs={{0,16},{4,20},{8,24},{12,28},{16,0},{20,4},{24,8},{28,12},{1,17},{... | collective-permute-start | bytes 405512 | tf_op jit(solution)/shard_map/cond/branch_2_fun/ppermute | solution.py:358
  49.5 3.5 %collective-permute-done.2.other_ref = bf16[528,128]{1,0:T(8,128)(2,1)S(1)} collective-permute-done((bf16[528,128]{1,0:T(8,128)(2,1)S(1)}, bf16[528,128]{1,0:T(8,128)(2,1)S(1)}, u32[]{:S(2)}, u32[]{:S(2)}) %collective-permute-start.2) | collective-permute-done | bytes 135200 | tf_op jit(solution)/shard_map/cond/branch_2_fun/ppermute | solution.py:358
  53.0 0.7 %half_average.5 = (f32[176,360]{1,0:T(8,128)S(1)}, f32[8,128]{1,0:T(8,128)S(1)}) custom-call(f32[1]{0:T(128)} %get-tuple-element.78.push_ref, f32[176,360]{1,0:T(8,128)S(1)} %get-tuple-element.79.moved_ref, bf16[528,128]{1,0:T(8,128)(2,1)S(1)} %collective-permute-done.2.other_ref), custom_call_target="tpu_custom_call" | custom-call | bytes 489600 | tf_op jit(solution)/shard_map/cond/branch_2_fun/half_average/pallas_call | solution.py:340
  53.6 0.5 slice.9
  54.2 0.0 copy-start.4
  54.2 0.0 copy-start.5
  54.2 0.9 %adam.3 = (f32[176,320]{1,0:T(8,128)S(1)}, f32[176,320]{1,0:T(8,128)S(1)}, bf16[448,128]{1,0:T(8,128)(2,1)S(1)}) custom-call(f32[2]{0:T(128)S(1)} %pad_maximum_fusion.scales_ref, f32[176,320]{1,0:T(8,128)S(1)} %get-tuple-element.169.refs_6_.own_ref, bf16[448,128]{1,0:T(8,128)(2,1)S(1)} %collective-permute-done.15.refs_0_, ...), custom_call_target="tpu_custom_call" | custom-call | bytes 435200 | tf_op jit(solution)/shard_map/adam/pallas_call | solution.py:340
  55.1 0.1 copy-done.4
  55.2 0.2 copy-done.5
  55.4 5.8 %conditional.3 = (f32[170,1,680]{2,1,0:T(1,128)}, f32[170,1,680]{2,1,0:T(1,128)}, f32[1,170,680]{2,0,1:T(1,128)}) conditional(s32[]{:T(128)} %clamp.4, (f32[170,1,680]{2,1,0:T(1,128)S(1)}, f32[170,1,680]{2,1,0:T(1,128)S(1)}, f32[176,360]{1,0:T(8,128)S(1)}, f32[176,320]{1,0:T(8,128)S(1)}, bf16[448,128]{1,0:T(8,128)(2,1)S(1)}, ...), branch_computations={%region_3.4_spmd, %region_4.5_spmd, %region_5.6_spmd} | conditional | bytes 2308416 | solution.py:476
  55.4 1.5 %collective-permute-start.5 = (bf16[448,128]{1,0:T(8,128)(2,1)S(1)}, bf16[448,128]{1,0:T(8,128)(2,1)S(1)}, u32[]{:S(2)}, u32[]{:S(2)}) collective-permute-start(bf16[448,128]{1,0:T(8,128)(2,1)S(1)} %get-tuple-element.109), channel_id=1, source_target_pairs={{0,16},{4,20},{8,24},{12,28},{16,0},{20,4},{24,8},{28,12},{1,17},{... | collective-permute-start | bytes 344072 | tf_op jit(solution)/shard_map/cond/branch_2_fun/ppermute | solution.py:358
  56.9 1.6 %moments.5 = (f32[170,1,680]{2,1,0:T(1,128)}, f32[170,1,680]{2,1,0:T(1,128)}) custom-call(f32[170,1,680]{2,1,0:T(1,128)S(1)} %get-tuple-element.101.first_ref, f32[170,1,680]{2,1,0:T(1,128)S(1)} %get-tuple-element.102.second_ref, f32[176,360]{1,0:T(8,128)S(1)} %get-tuple-element.103.refs_0_, f32[176,320]{1,0:T(8,128)S(1)} %get-tuple-element.104.refs_1_), custom_call_target="tpu_custom_call" | custom-call | bytes 924800 | tf_op jit(solution)/shard_map/cond/branch_2_fun/moments/pallas_call | solution.py:340
  58.5 1.7 %collective-permute-done.5.other_ref = bf16[448,128]{1,0:T(8,128)(2,1)S(1)} collective-permute-done((bf16[448,128]{1,0:T(8,128)(2,1)S(1)}, bf16[448,128]{1,0:T(8,128)(2,1)S(1)}, u32[]{:S(2)}, u32[]{:S(2)}) %collective-permute-start.5) | collective-permute-done | bytes 114720 | tf_op jit(solution)/shard_map/cond/branch_2_fun/ppermute | solution.py:358
  60.2 1.0 %average.5 = f32[170,1,680]{2,1,0:T(1,128)} custom-call(f32[176,360]{1,0:T(8,128)S(1)} %get-tuple-element.107.mean_ref, f32[176,320]{1,0:T(8,128)S(1)} %get-tuple-element.108.moved_ref, bf16[448,128]{1,0:T(8,128)(2,1)S(1)} %collective-permute-done.5.other_ref), custom_call_target="tpu_custom_call" | custom-call | bytes 924800 | tf_op jit(solution)/shard_map/cond/branch_2_fun/average/pallas_call | solution.py:340
  (6 shorter events, 0.0 us)
Async XLA Ops:
  1.3 1.0 %copy-start.1 = (f32[1,170,680]{2,0,1:T(1,128)S(1)}, f32[1,170,680]{2,0,1:T(1,128)}, u32[]{:S(2)}) copy-start(f32[1,170,680]{2,0,1:T(1,128)} %param.17) | copy-start | bytes 1387204
  2.6 14.7 %collective-permute-start.8 = (bf16[528,128]{1,0:T(8,128)(2,1)S(1)}, bf16[528,128]{1,0:T(8,128)(2,1)S(1)}, u32[]{:S(2)}, u32[]{:S(2)}) collective-permute-start(bf16[528,128]{1,0:T(8,128)(2,1)S(1)} %get-tuple-element.157.refs_0_), channel_id=1, source_target_pairs={{0,1},{1,2},{2,3},{3,0},{4,5},{5,6},{6,7},{7,4},{8,9},{9,10},{10,1... | collective-permute-start | bytes 405512 | tf_op jit(solution)/shard_map/ppermute | solution.py:358
  5.7 14.5 %collective-permute-start.7 = (bf16[528,128]{1,0:T(8,128)(2,1)S(1)}, bf16[528,128]{1,0:T(8,128)(2,1)S(1)}, u32[]{:S(2)}, u32[]{:S(2)}) collective-permute-start(bf16[528,128]{1,0:T(8,128)(2,1)S(1)} %get-tuple-element.157.refs_0_), channel_id=1, source_target_pairs={{0,2},{1,3},{2,0},{3,1},{4,6},{5,7},{6,4},{7,5},{8,10},{9,11},{10,... | collective-permute-start | bytes 405512 | tf_op jit(solution)/shard_map/ppermute | solution.py:358
  8.3 11.9 %collective-permute-start.6 = (bf16[528,128]{1,0:T(8,128)(2,1)S(1)}, bf16[528,128]{1,0:T(8,128)(2,1)S(1)}, u32[]{:S(2)}, u32[]{:S(2)}) collective-permute-start(bf16[528,128]{1,0:T(8,128)(2,1)S(1)} %get-tuple-element.157.refs_0_), channel_id=1, source_target_pairs={{0,3},{1,0},{2,1},{3,2},{4,7},{5,4},{6,5},{7,6},{8,11},{9,8},{10,9... | collective-permute-start | bytes 405512 | tf_op jit(solution)/shard_map/ppermute | solution.py:358
  9.6 21.7 %collective-permute-start.11 = (bf16[448,128]{1,0:T(8,128)(2,1)S(1)}, bf16[448,128]{1,0:T(8,128)(2,1)S(1)}, u32[]{:S(2)}, u32[]{:S(2)}) collective-permute-start(bf16[448,128]{1,0:T(8,128)(2,1)S(1)} %get-tuple-element.161.refs_0_), channel_id=1, source_target_pairs={{0,1},{1,2},{2,3},{3,0},{4,5},{5,6},{6,7},{7,4},{8,9},{9,10},{10,1... | collective-permute-start | bytes 344072 | tf_op jit(solution)/shard_map/ppermute | solution.py:358
  10.3 21.0 %collective-permute-start.10 = (bf16[448,128]{1,0:T(8,128)(2,1)S(1)}, bf16[448,128]{1,0:T(8,128)(2,1)S(1)}, u32[]{:S(2)}, u32[]{:S(2)}) collective-permute-start(bf16[448,128]{1,0:T(8,128)(2,1)S(1)} %get-tuple-element.161.refs_0_), channel_id=1, source_target_pairs={{0,2},{1,3},{2,0},{3,1},{4,6},{5,7},{6,4},{7,5},{8,10},{9,11},{10,... | collective-permute-start | bytes 344072 | tf_op jit(solution)/shard_map/ppermute | solution.py:358
  11.4 0.7 %copy-start.3 = (bf16[2,680]{1,0:T(2,128)(2,1)S(1)}, bf16[2,680]{1,0:T(2,128)(2,1)}, u32[]{:S(2)}) copy-start(bf16[2,680]{1,0:T(2,128)(2,1)} %shift_ref.1) | copy-start | bytes 8164
  12.1 1.2 %copy-start = (bf16[2,288,680]{2,1,0:T(8,128)(2,1)S(1)}, bf16[2,288,680]{2,1,0:T(8,128)(2,1)}, u32[]{:S(2)}) copy-start(bf16[2,288,680]{2,1,0:T(8,128)(2,1)} %x_hbm.1) | copy-start | bytes 2350084
  13.2 1.2 %copy-start.2 = (bf16[2,288,680]{2,1,0:T(8,128)(2,1)S(1)}, bf16[2,288,680]{2,1,0:T(8,128)(2,1)}, u32[]{:S(2)}) copy-start(bf16[2,288,680]{2,1,0:T(8,128)(2,1)} %out_grad_ref.1) | copy-start | bytes 2350084
  17.3 14.0 %collective-permute-start.9 = (bf16[448,128]{1,0:T(8,128)(2,1)S(1)}, bf16[448,128]{1,0:T(8,128)(2,1)S(1)}, u32[]{:S(2)}, u32[]{:S(2)}) collective-permute-start(bf16[448,128]{1,0:T(8,128)(2,1)S(1)} %get-tuple-element.161.refs_0_), channel_id=1, source_target_pairs={{0,3},{1,0},{2,1},{3,2},{4,7},{5,4},{6,5},{7,6},{8,11},{9,8},{10,9... | collective-permute-start | bytes 344072 | tf_op jit(solution)/shard_map/ppermute | solution.py:358
  23.1 13.4 %collective-permute-start.12 = (bf16[528,128]{1,0:T(8,128)(2,1)S(1)}, bf16[528,128]{1,0:T(8,128)(2,1)S(1)}, u32[]{:S(2)}, u32[]{:S(2)}) collective-permute-start(bf16[528,128]{1,0:T(8,128)(2,1)S(1)} %get-tuple-element.166), channel_id=1, source_target_pairs={{0,1},{1,2},{2,3},{3,0},{4,5},{5,6},{6,7},{7,4},{8,9},{9,10},{10,1... | collective-permute-start | bytes 405512 | tf_op jit(solution)/shard_map/ppermute | solution.py:358
  28.5 16.4 %collective-permute-start.13 = (bf16[528,128]{1,0:T(8,128)(2,1)S(1)}, bf16[528,128]{1,0:T(8,128)(2,1)S(1)}, u32[]{:S(2)}, u32[]{:S(2)}) collective-permute-start(bf16[528,128]{1,0:T(8,128)(2,1)S(1)} %get-tuple-element.167), channel_id=1, source_target_pairs={{0,2},{1,3},{2,0},{3,1},{4,6},{5,7},{6,4},{7,5},{8,10},{9,11},{10,... | collective-permute-start | bytes 405512 | tf_op jit(solution)/shard_map/ppermute | solution.py:358
  31.3 13.7 %collective-permute-start.14 = (bf16[528,128]{1,0:T(8,128)(2,1)S(1)}, bf16[528,128]{1,0:T(8,128)(2,1)S(1)}, u32[]{:S(2)}, u32[]{:S(2)}) collective-permute-start(bf16[528,128]{1,0:T(8,128)(2,1)S(1)} %get-tuple-element.168), channel_id=1, source_target_pairs={{0,3},{1,0},{2,1},{3,2},{4,7},{5,4},{6,5},{7,6},{8,11},{9,8},{10,9... | collective-permute-start | bytes 405512 | tf_op jit(solution)/shard_map/ppermute | solution.py:358
  34.3 19.9 %collective-permute-start.15 = (bf16[448,128]{1,0:T(8,128)(2,1)S(1)}, bf16[448,128]{1,0:T(8,128)(2,1)S(1)}, u32[]{:S(2)}, u32[]{:S(2)}) collective-permute-start(bf16[448,128]{1,0:T(8,128)(2,1)S(1)} %get-tuple-element.171), channel_id=1, source_target_pairs={{0,1},{1,2},{2,3},{3,0},{4,5},{5,6},{6,7},{7,4},{8,9},{9,10},{10,1... | collective-permute-start | bytes 344072 | tf_op jit(solution)/shard_map/ppermute | solution.py:358
  36.3 17.8 %collective-permute-start.16 = (bf16[448,128]{1,0:T(8,128)(2,1)S(1)}, bf16[448,128]{1,0:T(8,128)(2,1)S(1)}, u32[]{:S(2)}, u32[]{:S(2)}) collective-permute-start(bf16[448,128]{1,0:T(8,128)(2,1)S(1)} %get-tuple-element.172), channel_id=1, source_target_pairs={{0,2},{1,3},{2,0},{3,1},{4,6},{5,7},{6,4},{7,5},{8,10},{9,11},{10,... | collective-permute-start | bytes 344072 | tf_op jit(solution)/shard_map/ppermute | solution.py:358
  36.5 17.6 %collective-permute-start.17 = (bf16[448,128]{1,0:T(8,128)(2,1)S(1)}, bf16[448,128]{1,0:T(8,128)(2,1)S(1)}, u32[]{:S(2)}, u32[]{:S(2)}) collective-permute-start(bf16[448,128]{1,0:T(8,128)(2,1)S(1)} %get-tuple-element.173), channel_id=1, source_target_pairs={{0,3},{1,0},{2,1},{3,2},{4,7},{5,4},{6,5},{7,6},{8,11},{9,8},{10,9... | collective-permute-start | bytes 344072 | tf_op jit(solution)/shard_map/ppermute | solution.py:358
  47.9 5.1 %collective-permute-start.2 = (bf16[528,128]{1,0:T(8,128)(2,1)S(1)}, bf16[528,128]{1,0:T(8,128)(2,1)S(1)}, u32[]{:S(2)}, u32[]{:S(2)}) collective-permute-start(bf16[528,128]{1,0:T(8,128)(2,1)S(1)} %get-tuple-element.80), channel_id=1, source_target_pairs={{0,16},{4,20},{8,24},{12,28},{16,0},{20,4},{24,8},{28,12},{1,17},{... | collective-permute-start | bytes 405512 | tf_op jit(solution)/shard_map/cond/branch_2_fun/ppermute | solution.py:358
  54.2 1.0 %copy-start.4 = (f32[1,170,680]{2,0,1:T(1,128)S(1)}, f32[1,170,680]{2,0,1:T(1,128)}, u32[]{:S(2)}) copy-start(f32[1,170,680]{2,0,1:T(1,128)} %param.18) | copy-start | bytes 1387204
  54.2 1.2 %copy-start.5 = (f32[1,170,680]{2,0,1:T(1,128)S(1)}, f32[1,170,680]{2,0,1:T(1,128)}, u32[]{:S(2)}) copy-start(f32[1,170,680]{2,0,1:T(1,128)} %param.19) | copy-start | bytes 1387204
  55.4 4.8 %collective-permute-start.5 = (bf16[448,128]{1,0:T(8,128)(2,1)S(1)}, bf16[448,128]{1,0:T(8,128)(2,1)S(1)}, u32[]{:S(2)}, u32[]{:S(2)}) collective-permute-start(bf16[448,128]{1,0:T(8,128)(2,1)S(1)} %get-tuple-element.109), channel_id=1, source_target_pairs={{0,16},{4,20},{8,24},{12,28},{16,0},{20,4},{24,8},{28,12},{1,17},{... | collective-permute-start | bytes 344072 | tf_op jit(solution)/shard_map/cond/branch_2_fun/ppermute | solution.py:358

commit v6 on v5

--- a/solution.py
+++ b/solution.py
@@ -134,21 +134,27 @@
         pack.write(out_ref, rows_ref[:, pack.start : pack.stop])
 
 
-def norm_in_kernel(shards, packs, me_ref, scales_ref, x_ref, shift_ref, out_grad_ref, *refs):
+def norm_in_kernel(shards, packs, me_ref, scales_ref, shift_ref, x_hbm, out_grad_hbm, *refs):
     act_ref, mean_ref, inverse_ref, same_group_ref = refs[:4]
-    shift_refs, out_grad_refs = refs[4 : 4 + len(packs)], refs[4 + len(packs) :]
+    shift_refs, out_grad_refs = refs[4 : 4 + len(packs)], refs[4 + len(packs) : 4 + 2 * len(packs)]
+    x_ref, out_grad_ref, sems = refs[4 + 2 * len(packs) :]
+    copies = [
+        pltpu.make_async_copy(x_hbm, x_ref, sems.at[0]),
+        pltpu.make_async_copy(out_grad_hbm, out_grad_ref, sems.at[1]),
+    ]
+    for copy in copies:
+        copy.start()
     samples, positions, channels = x_ref.shape
-    for pack, shift_out, out_grad_out in zip(packs, shift_refs, out_grad_refs):
-        shift_out[...] = shift_ref[...].astype(jnp.float32)[:, pack.start : pack.stop]
-        for i in range(samples):
-            out_grad_out[i] = out_grad_ref[i][:, pack.start : pack.stop]
+    rows = channels // shards
+    deep = act_ref.shape[0] // shards
+    entries = positions * GSIZE
     group_of_row = lax.broadcasted_iota(jnp.int32, same_group_ref.shape, 0) // GSIZE
     group_of_column = lax.broadcasted_iota(jnp.int32, same_group_ref.shape, 1) // GSIZE
     same_group_ref[...] = (group_of_row == group_of_column).astype(jnp.float32).astype(jnp.bfloat16)
-    rows = channels // shards
-    deep = act_ref.shape[0] // shards
-    entries = positions * GSIZE
     same_group = same_group_ref[...]
+    for pack, shift_out in zip(packs, shift_refs):
+        shift_out[...] = shift_ref[...].astype(jnp.float32)[:, pack.start : pack.stop]
+    copies[0].wait()
     parts = [x_ref[i].astype(jnp.float32) for i in range(samples)]
     mean = table_sums(packs, position_sums(parts), same_group) / entries
     centered = [parts[i] - mean[i : i + 1] for i in range(samples)]
@@ -157,11 +163,16 @@
     mean_ref[...] = mean
     inverse_ref[...] = inverse
     normed = [centered[i] * inverse[i : i + 1] for i in range(samples)]
-    act = jnp.concatenate([part * sigmoid(part) for part in normed], axis=0)
-    turned = pltpu.roll(act.T, channels - me_ref[0] * rows, 0)
-    act_ref[...] = jnp.zeros_like(act_ref)
-    for slot in range(shards):
-        act_ref[slot * deep : slot * deep + rows, :] = turned[slot * rows : (slot + 1) * rows].astype(jnp.bfloat16)
+    act = jnp.concatenate([part * sigmoid(part) for part in normed], axis=0).T
+    for block in range(shards):
+        slot = lax.rem(block + shards - me_ref[0], shards)
+        act_ref[pl.ds(pl.multiple_of(slot * deep, TILE_ROWS), deep), :] = jnp.concatenate(
+            [act[block * rows : (block + 1) * rows], jnp.zeros((deep - rows, act.shape[1]), jnp.float32)], axis=0
+        ).astype(jnp.bfloat16)
+    copies[1].wait()
+    for pack, out_grad_out in zip(packs, out_grad_refs):
+        for i in range(samples):
+            out_grad_out[i] = out_grad_ref[i][:, pack.start : pack.stop]
 
 
 def mix_kernel(shards, pack, act_ref, shift_ref, out_grad_ref, same_group_ref, *refs):
@@ -213,8 +224,8 @@
 def input_grad_kernel(shards, packs, me_ref, mean_ref, inverse_ref, same_group_ref, x_hbm, *refs):
     count = len(packs)
     grad_hbms, weight_hbms, out_ref = refs[:count], refs[count : 2 * count], refs[2 * count]
-    rows_ref, x_ref, sems = refs[2 * count + 1 : 2 * count + 4]
-    grad_refs, weight_refs = refs[2 * count + 4 : 3 * count + 4], refs[3 * count + 4 :]
+    rows_ref, x_ref, made_ref, sems = refs[2 * count + 1 : 2 * count + 5]
+    grad_refs, weight_refs = refs[2 * count + 5 : 3 * count + 5], refs[3 * count + 5 :]
     copies = [
         pltpu.make_async_copy(source, target, sems.at[i])
         for i, (source, target) in enumerate(
@@ -229,11 +240,12 @@
     weights = []
     for index, (pack, weight_ref) in enumerate(zip(packs, weight_refs)):
         copies[index].wait()
-        for slot in range(shards):
-            rows_ref[slot * rows : (slot + 1) * rows, : pack.columns] = weight_ref[
-                slot * pack.deep : (slot + 1) * pack.deep, :
+        for block in range(shards):
+            slot = lax.rem(block + shards - me_ref[0], shards)
+            rows_ref[block * rows : (block + 1) * rows, : pack.columns] = weight_ref[
+                pl.ds(pl.multiple_of(slot * pack.deep, TILE_ROWS), pack.deep), :
             ].astype(jnp.float32)[:rows]
-        weights.append(pltpu.roll(rows_ref[:, : pack.columns], me_ref[0] * rows, 0).astype(jnp.bfloat16))
+        weights.append(rows_ref[:, : pack.columns].astype(jnp.bfloat16))
     grad_act = 0.0
     for index, (grad_ref, weight) in enumerate(zip(grad_refs, weights)):
         copies[count + index].wait()
@@ -255,7 +267,11 @@
     ) / entries
     for i in range(samples):
         first, second = means[i : i + 1], means[samples + i : samples + i + 1]
-        out_ref[i] = (inverse[i : i + 1] * (grads[i] - first - normed[i] * second)).astype(jnp.bfloat16)
+        made_ref[i] = (inverse[i : i + 1] * (grads[i] - first - normed[i] * second)).astype(jnp.bfloat16)
+        copies.append(pltpu.make_async_copy(made_ref.at[i], out_ref.at[i], sems.at[len(copies)]))
+        copies[-1].start()
+    for copy in copies[-samples:]:
+        copy.wait()
 
 
 def adam_step(shards, pack, scales_ref, own_ref, other_refs, blocks, grad_ref, moved_ref):
@@ -273,17 +289,21 @@
     moved_ref[:rows, :] = params - update
 
 
-def first_adam_kernel(shards, packs, scales_ref, push_ref, own_ref, *refs):
-    pack, later = packs
-    other_refs, refs = refs[: shards - 1], refs[shards - 1 :]
-    hbm_refs, token_ref, (grad_ref, moved_ref, sent_ref), later_refs = refs[:3], refs[3], refs[4:7], refs[7:10]
-    row_refs, sems = refs[10:13], refs[13]
+def fetch(hbm_refs, row_refs, sems):
     copies = [
         pltpu.make_async_copy(source, target, sems.at[i])
         for i, (source, target) in enumerate(zip(hbm_refs, row_refs))
     ]
     for copy in copies:
         copy.start()
+    return copies
+
+
+def first_adam_kernel(shards, pack, scales_ref, push_ref, own_ref, *refs):
+    other_refs, refs = refs[: shards - 1], refs[shards - 1 :]
+    hbm_refs, token_ref, (grad_ref, moved_ref, sent_ref) = refs[:3], refs[3], refs[4:7]
+    row_refs, sems = refs[7:10], refs[10]
+    copies = fetch(hbm_refs, row_refs, sems)
 
     def blocks():
         for copy in copies:
@@ -294,8 +314,13 @@
     moved = moved_ref[...]
     spare = lax.broadcasted_iota(jnp.int32, moved.shape, 0) == pack.rows
     pack.write(sent_ref, jnp.where(spare, push_ref[0], moved))
-    for row_ref, later_ref in zip(row_refs, later_refs):
-        later_ref[...] = row_ref[:, 0, later.start : later.stop]
+
+
+def cut_kernel(pack, *refs):
+    hbm_refs, out_refs, row_refs, sems = refs[:3], refs[3:6], refs[6:9], refs[9]
+    for copy, row_ref, out_ref in zip(fetch(hbm_refs, row_refs, sems), row_refs, out_refs):
+        copy.wait()
+        out_ref[...] = row_ref[:, 0, pack.start : pack.stop]
 
 
 def second_adam_kernel(shards, pack, scales_ref, own_ref, *refs):
@@ -310,7 +335,9 @@
 def half_average_kernel(pack, push_ref, moved_ref, other_ref, mean_ref, push_out_ref):
     other = pack.read(other_ref)
     mean_ref[...] = 0.5 * (moved_ref[...] + other)
-    push_out_ref[0:1, :] = 0.5 * (push_ref[0] + other[pack.rows : pack.rows + 1, :LANES])
+    place = other[pack.rows : pack.rows + 1, :LANES]
+    first = lax.broadcasted_iota(jnp.int32, place.shape, 1) == 0
+    push_out_ref[0] = 0.5 * (push_ref[0] + jnp.sum(jnp.where(first, place, 0.0)))
 
 
 def moments_kernel(packs, first_ref, second_ref, *refs):
@@ -407,8 +434,13 @@
             *(jax.ShapeDtypeStruct((samples, pack.columns), jnp.float32) for pack in packs),
             *(jax.ShapeDtypeStruct((samples, positions, pack.columns), jnp.bfloat16) for pack in packs),
         ),
-        [SCALARS, SCALARS, BLOCKS, BLOCKS, BLOCKS],
-        (me, scales, block_input, time_shift, out_grad),
+        [SCALARS, SCALARS, BLOCKS, IN_HBM, IN_HBM],
+        (me, scales, time_shift, stay(block_input), stay(out_grad)),
+        scratch=[
+            pltpu.VMEM(block_input.shape, jnp.bfloat16),
+            pltpu.VMEM(out_grad.shape, jnp.bfloat16),
+            pltpu.SemaphoreType.DMA((2,)),
+        ],
         elements=tokens * channels,
     )
 
@@ -442,22 +474,25 @@
         owns.append(own)
         arrived.append([moved_on(send, "dp", slot) for slot, send in enumerate(sends, 1)])
 
-    grad_input = call(
-        functools.partial(input_grad_kernel, shards, packs),
-        "input_grad",
-        jax.ShapeDtypeStruct(block_input.shape, jnp.bfloat16),
-        [SCALARS] + [BLOCKS] * 3 + [IN_HBM] * (1 + 2 * len(packs)),
-        (me, mean_in, inverse_in, same_group, *map(stay, (block_input, *hidden_grads, *full_weights))),
-        scratch=[
-            pltpu.VMEM((channels, max(pack.columns for pack in packs)), jnp.float32),
-            pltpu.VMEM(block_input.shape, jnp.bfloat16),
-            pltpu.SemaphoreType.DMA((1 + 2 * len(packs),)),
-            *(pltpu.VMEM((tokens, pack.columns), jnp.bfloat16) for pack in packs),
-            *(pltpu.VMEM((shards * deep, pack.columns), jnp.bfloat16) for pack in packs),
-        ],
-        flops=2 * tokens * channels * channels,
-        elements=tokens * channels,
-    )
+    def input_grad(*operands):
+        return call(
+            functools.partial(input_grad_kernel, shards, packs),
+            "input_grad",
+            pltpu.HBM(block_input.shape, jnp.bfloat16),
+            [SCALARS] + [BLOCKS] * 3 + [IN_HBM] * (1 + 2 * len(packs)),
+            operands[:4] + tuple(map(stay, operands[4:])),
+            scratch=[
+                pltpu.VMEM((channels, max(pack.columns for pack in packs)), jnp.float32),
+                pltpu.VMEM(block_input.shape, jnp.bfloat16),
+                pltpu.VMEM(block_input.shape, jnp.bfloat16),
+                pltpu.SemaphoreType.DMA((1 + 2 * len(packs) + samples,)),
+                *(pltpu.VMEM((tokens, pack.columns), jnp.bfloat16) for pack in packs),
+                *(pltpu.VMEM((shards * deep, pack.columns), jnp.bfloat16) for pack in packs),
+            ],
+            out_specs=IN_HBM,
+            flops=2 * tokens * channels * channels,
+            elements=tokens * channels,
+        )
 
     def moments(*grads):
         return call(
@@ -476,28 +511,56 @@
         return lax.switch(distance_bits, [branch(1 << power) for power in range(level_count)], *operands)
 
     early, late = packs
-    rows_kept = jax.ShapeDtypeStruct((rows, late.columns), jnp.float32)
-    grad_a, moved_a, sent_a, *late_blocks = call(
-        functools.partial(first_adam_kernel, shards, packs),
+    arrays = [stay(params), stay(first_moment), stay(second_moment)]
+    array_scratch = [pltpu.VMEM(params.shape, jnp.float32)] * 3 + [pltpu.SemaphoreType.DMA((3,))]
+    grad_a, moved_a, sent_a = call(
+        functools.partial(first_adam_kernel, shards, early),
         "adam",
-        (early.block(), early.block(), early.payload()) + (rows_kept,) * 3,
+        (early.block(), early.block(), early.payload()),
         [SCALARS] * 2 + [BLOCKS] * shards + [IN_HBM] * 3 + [TOKEN],
-        (scales, push_weight, owns[0], *arrived[0], stay(params), stay(first_moment), stay(second_moment), token),
-        scratch=[pltpu.VMEM(params.shape, jnp.float32)] * 3 + [pltpu.SemaphoreType.DMA((3,))],
-        elements=rows * channels,
-    )
-
-    def finish_early(move, sent, moved):
-        return call(
+        (scales, push_weight, owns[0], *arrived[0], *arrays, token),
+        scratch=array_scratch,
+        elements=rows * early.columns,
+    )
+
+    def finish_early(move, sent, moved, params, first_moment, second_moment, *operands):
+        other = move(sent)
+        grad_input = input_grad(*operands)
+        blocks = call(
+            functools.partial(cut_kernel, late),
+            "cut",
+            (jax.ShapeDtypeStruct((rows, late.columns), jnp.float32),) * 3,
+            [IN_HBM] * 3,
+            (stay(params), stay(first_moment), stay(second_moment)),
+            scratch=array_scratch,
+            elements=rows * late.columns,
+        )
+        mean, weight = call(
             functools.partial(half_average_kernel, early),
             "half_average",
-            (early.block(), jax.ShapeDtypeStruct((8, LANES), jnp.float32)),
+            (early.block(), jax.ShapeDtypeStruct((1,), jnp.float32)),
             [SCALARS] + [BLOCKS] * 2,
-            (push_weight, moved, move(sent)),
+            (push_weight, moved, other),
+            out_specs=(BLOCKS, SCALARS),
             elements=rows * early.columns,
         )
-
-    mean_a, weight_tile = from_behind(finish_early, sent_a, moved_a)
+        return (grad_input, mean, weight, *blocks)
+
+    grad_input, mean_a, new_weight, *late_blocks = from_behind(
+        finish_early,
+        sent_a,
+        moved_a,
+        params,
+        first_moment,
+        second_moment,
+        me,
+        mean_in,
+        inverse_in,
+        same_group,
+        block_input,
+        *hidden_grads,
+        *full_weights,
+    )
     grad_b, moved_b, sent_b = call(
         functools.partial(second_adam_kernel, shards, late),
         "adam",
@@ -522,7 +585,6 @@
         return (*moments(grad_a, grad_b), averaged)
 
     first_new, second_new, averaged = from_behind(finish_late, sent_b, grad_a, grad_b, mean_a, moved_b)
-    new_weight = weight_tile[0, :1]
     return (
         grad_input,
         *(jnp.transpose(array, (1, 0, 2)) for array in (averaged, first_new, second_new)),

time: 61.7 us -> 63.7 us (1.032)
  the two profiles are of different devices: /device:TPU:0 before, /device:TPU:8 now
where the time goes in v6:
time: 63.7 us; the launch traced here: 62.8 us
  Pallas kernels  24.8 us (39%)
  starting transfers between devices  17.5 us (27%)
  waiting for transfers between devices  17.1 us (27%)
  between operations  2.42 us (4%)
    pallas_call x11, Pallas kernels, call(): pl.pallas_call(kernel, out_shape=outs, in_specs=specs, out_specs=out_spec...  24.8 us
    ppermute x14, starting transfers between devices, moved_on(): lax.ppermute(block, axis, [(i, (i + distance) % size) for i in range(size)])  17.5 us
    ppermute x14, waiting for transfers between devices, moved_on(): lax.ppermute(block, axis, [(i, (i + distance) % size) for i in range(size)])  17.1 us
  transfers between devices with their start and end apart: 14, of which 5 were waited for; matrix products, arithmetic and copies ran while one was open for 0% of the time, Pallas kernels for 34%

profile of v6, /device:TPU:8, one launch (start us, length us, event | category | flops | bytes accessed | tf_op | source)
XLA Modules:
  0.0 62.8 jit_solution(17753870746504988553)
XLA Ops:
  1.3 1.3 %cast.1 = (bf16[528,128]{1,0:T(8,128)(2,1)S(1)}, bf16[448,128]{1,0:T(8,128)(2,1)S(1)}) custom-call(f32[1]{0:T(128)S(6)} %copy.40.push_ref, f32[170,1,680]{2,1,0:T(1,128)} %bitcast.24), custom_call_target="tpu_custom_call" | custom-call | bytes 924800 | tf_op jit(solution)/shard_map/cast/pallas_call | solution.py:367
  2.6 1.6 %collective-permute-start.8 = (bf16[528,128]{1,0:T(8,128)(2,1)S(1)}, bf16[528,128]{1,0:T(8,128)(2,1)S(1)}, u32[]{:S(2)}, u32[]{:S(2)}) collective-permute-start(bf16[528,128]{1,0:T(8,128)(2,1)S(1)} %get-tuple-element.268.refs_0_), channel_id=1, source_target_pairs={{0,1},{1,2},{2,3},{3,0},{4,5},{5,6},{6,7},{7,4},{8,9},{9,10},{10,1... | collective-permute-start | bytes 405512 | tf_op jit(solution)/shard_map/ppermute | solution.py:385
  4.2 1.1 %collective-permute-start.7 = (bf16[528,128]{1,0:T(8,128)(2,1)S(1)}, bf16[528,128]{1,0:T(8,128)(2,1)S(1)}, u32[]{:S(2)}, u32[]{:S(2)}) collective-permute-start(bf16[528,128]{1,0:T(8,128)(2,1)S(1)} %get-tuple-element.268.refs_0_), channel_id=1, source_target_pairs={{0,2},{1,3},{2,0},{3,1},{4,6},{5,7},{6,4},{7,5},{8,10},{9,11},{10,... | collective-permute-start | bytes 405512 | tf_op jit(solution)/shard_map/ppermute | solution.py:385
  5.3 1.9 %collective-permute-start.6 = (bf16[528,128]{1,0:T(8,128)(2,1)S(1)}, bf16[528,128]{1,0:T(8,128)(2,1)S(1)}, u32[]{:S(2)}, u32[]{:S(2)}) collective-permute-start(bf16[528,128]{1,0:T(8,128)(2,1)S(1)} %get-tuple-element.268.refs_0_), channel_id=1, source_target_pairs={{0,3},{1,0},{2,1},{3,2},{4,7},{5,4},{6,5},{7,6},{8,11},{9,8},{10,9... | collective-permute-start | bytes 405512 | tf_op jit(solution)/shard_map/ppermute | solution.py:385
  7.3 0.1 collective-permute-start.11
  7.3 3.6 %collective-permute-start.10 = (bf16[448,128]{1,0:T(8,128)(2,1)S(1)}, bf16[448,128]{1,0:T(8,128)(2,1)S(1)}, u32[]{:S(2)}, u32[]{:S(2)}) collective-permute-start(bf16[448,128]{1,0:T(8,128)(2,1)S(1)} %get-tuple-element.272.refs_0_), channel_id=1, source_target_pairs={{0,2},{1,3},{2,0},{3,1},{4,6},{5,7},{6,4},{7,5},{8,10},{9,11},{10,... | collective-permute-start | bytes 344072 | tf_op jit(solution)/shard_map/ppermute | solution.py:385
  11.7 0.0 copy-start
  11.8 0.1 pad_maximum_fusion.scales_ref
  11.9 0.6 copy-done
  12.4 3.3 %norm_in.1 = (bf16[704,576]{1,0:T(8,128)(2,1)S(1)}, f32[2,680]{1,0:T(2,128)S(1)}, f32[2,680]{1,0:T(2,128)S(1)}, bf16[360,360]{1,0:T(8,128)(2,1)S(1)}, f32[2,360]...) custom-call(s32[1]{0:T(128)} %bitcast.4.me_ref, ...), custom_call_target="tpu_custom_call" | custom-call | bytes 3133440 | tf_op jit(solution)/shard_map/norm_in/pallas_call | solution.py:367
  15.8 0.0 collective-permute-done.8.refs_3_
  15.8 0.1 collective-permute-start.9
  15.8 6.0 %collective-permute-done.7.refs_2_ = bf16[528,128]{1,0:T(8,128)(2,1)S(1)} collective-permute-done((bf16[528,128]{1,0:T(8,128)(2,1)S(1)}, bf16[528,128]{1,0:T(8,128)(2,1)S(1)}, u32[]{:S(2)}, u32[]{:S(2)}) %collective-permute-start.7) | collective-permute-done | bytes 135200 | tf_op jit(solution)/shard_map/ppermute | solution.py:385
  21.8 0.7 %collective-permute-done.6.refs_1_ = bf16[528,128]{1,0:T(8,128)(2,1)S(1)} collective-permute-done((bf16[528,128]{1,0:T(8,128)(2,1)S(1)}, bf16[528,128]{1,0:T(8,128)(2,1)S(1)}, u32[]{:S(2)}, u32[]{:S(2)}) %collective-permute-start.6) | collective-permute-done | bytes 135200 | tf_op jit(solution)/shard_map/ppermute | solution.py:385
  22.5 2.9 %mix.2 = (bf16[576,360]{1,0:T(8,128)(2,1)}, bf16[704,360]{1,0:T(8,128)(2,1)}, f32[176,360]{1,0:T(8,128)S(1)}, bf16[528,128]{1,0:T(8,128)(2,1)S(1)}, bf16[528,128...) custom-call(bf16[704,576]{1,0:T(8,128)(2,1)S(1)} %get-tuple-element.265.act_ref, ...), custom_call_target="tpu_custom_call" | custom-call | flops 564019200 | bytes 1658880 | tf_op jit(solution)/shard_map/mix/pallas_call | solution.py:367
  25.5 0.1 collective-permute-start.12
  25.5 2.8 %collective-permute-start.13 = (bf16[528,128]{1,0:T(8,128)(2,1)S(1)}, bf16[528,128]{1,0:T(8,128)(2,1)S(1)}, u32[]{:S(2)}, u32[]{:S(2)}) collective-permute-start(bf16[528,128]{1,0:T(8,128)(2,1)S(1)} %get-tuple-element.278), channel_id=1, source_target_pairs={{0,2},{1,3},{2,0},{3,1},{4,6},{5,7},{6,4},{7,5},{8,10},{9,11},{10,... | collective-permute-start | bytes 405512 | tf_op jit(solution)/shard_map/ppermute | solution.py:385
  28.3 0.0 collective-permute-done.11.refs_3_
  28.3 1.9 %collective-permute-start.14 = (bf16[528,128]{1,0:T(8,128)(2,1)S(1)}, bf16[528,128]{1,0:T(8,128)(2,1)S(1)}, u32[]{:S(2)}, u32[]{:S(2)}) collective-permute-start(bf16[528,128]{1,0:T(8,128)(2,1)S(1)} %get-tuple-element.279), channel_id=1, source_target_pairs={{0,3},{1,0},{2,1},{3,2},{4,7},{5,4},{6,5},{7,6},{8,11},{9,8},{10,9... | collective-permute-start | bytes 405512 | tf_op jit(solution)/shard_map/ppermute | solution.py:385
  30.3 0.0 collective-permute-done.10.refs_2_
  30.3 0.0 collective-permute-done.9.refs_1_
  30.3 3.0 %mix.3 = (bf16[576,320]{1,0:T(8,128)(2,1)}, bf16[704,320]{1,0:T(8,128)(2,1)}, f32[176,320]{1,0:T(8,128)S(1)}, bf16[448,128]{1,0:T(8,128)(2,1)S(1)}, bf16[448,128...) custom-call(bf16[704,576]{1,0:T(8,128)(2,1)S(1)} %get-tuple-element.265.act_ref, ...), custom_call_target="tpu_custom_call" | custom-call | flops 501350400 | bytes 1474560 | tf_op jit(solution)/shard_map/mix/pallas_call | solution.py:367
  33.2 0.1 collective-permute-start.15
  33.4 2.3 %collective-permute-start.16 = (bf16[448,128]{1,0:T(8,128)(2,1)S(1)}, bf16[448,128]{1,0:T(8,128)(2,1)S(1)}, u32[]{:S(2)}, u32[]{:S(2)}) collective-permute-start(bf16[448,128]{1,0:T(8,128)(2,1)S(1)} %get-tuple-element.286), channel_id=1, source_target_pairs={{0,2},{1,3},{2,0},{3,1},{4,6},{5,7},{6,4},{7,5},{8,10},{9,11},{10,... | collective-permute-start | bytes 344072 | tf_op jit(solution)/shard_map/ppermute | solution.py:385
  35.7 0.0 collective-permute-done.12.refs_0_
  35.7 0.0 collective-permute-start.17
  35.7 3.1 %collective-permute-done.13.refs_1_ = bf16[528,128]{1,0:T(8,128)(2,1)S(1)} collective-permute-done((bf16[528,128]{1,0:T(8,128)(2,1)S(1)}, bf16[528,128]{1,0:T(8,128)(2,1)S(1)}, u32[]{:S(2)}, u32[]{:S(2)}) %collective-permute-start.13) | collective-permute-done | bytes 135200 | tf_op jit(solution)/shard_map/ppermute | solution.py:385
  38.7 5.4 %collective-permute-done.14.refs_2_ = bf16[528,128]{1,0:T(8,128)(2,1)S(1)} collective-permute-done((bf16[528,128]{1,0:T(8,128)(2,1)S(1)}, bf16[528,128]{1,0:T(8,128)(2,1)S(1)}, u32[]{:S(2)}, u32[]{:S(2)}) %collective-permute-start.14) | collective-permute-done | bytes 135200 | tf_op jit(solution)/shard_map/ppermute | solution.py:385
  44.2 2.7 %adam.2 = (f32[176,360]{1,0:T(8,128)}, f32[176,360]{1,0:T(8,128)S(1)}, bf16[528,128]{1,0:T(8,128)(2,1)S(1)}) custom-call(f32[2]{0:T(128)S(1)} %pad_maximum_fusion.scales_ref, f32[1]{0:T(128)S(6)} %copy.40.push_ref, f32[176,360]{1,0:T(8,128)S(1)} %get-tuple-element.273.refs_4_.own_ref, bf16[528,128]{1,0:T(8,128)(2,1)S(1)} %collective-permute-done.12.refs_0_, ...), custom_call_target="tpu_custom_call" | custom-call | bytes 489600 | tf_op jit(solution)/shard_map/adam/pallas_call | solution.py:367
  46.9 0.0 copy-done.1
  46.9 0.0 copy-done.2
  46.9 8.5 %conditional.2 = (bf16[2,288,680]{2,1,0:T(8,128)(2,1)}, f32[176,360]{1,0:T(8,128)S(1)}, f32[1]{0:T(128)}, f32[170,320]{1,0:T(8,128)S(1)}, f32[170,320]{1,0:T(8,128)S(1)}, /*index=5*/f32[170,320]{1,0:T(8,128)S(1)}) conditional(s32[]{:T(128)} %clamp.4, (s32[1]{0:T(128)}, f32[2,680]{1,0:T(2,128)S(1)}, f32[2,680]{1,0:T(2,128)S(1)}, ...), branch_computations={%region_0.1_spmd, %region_1.2_spmd, %region_2.3_spmd} | conditional | flops 532684800 | bytes 4599000 | solution.py:511
  46.9 0.2 collective-permute-start
  47.2 1.6 %cut.3 = (f32[170,320]{1,0:T(8,128)S(1)}, f32[170,320]{1,0:T(8,128)S(1)}, f32[170,320]{1,0:T(8,128)S(1)}) custom-call(f32[170,1,680]{2,1,0:T(1,128)} %get-tuple-element.147.refs_0_, f32[170,1,680]{2,1,0:T(1,128)S(1)} %get-tuple-element.148.refs_1_, f32[170,1,680]{2,1,0:T(1,128)S(1)} %get-tuple-element.149.refs_2_), custom_call_target="tpu_custom_call" | custom-call | bytes 435200 | tf_op jit(solution)/shard_map/cond/branch_0_fun/cut/pallas_call | solution.py:367
  48.7 5.1 %input_grad.3 = bf16[2,288,680]{2,1,0:T(8,128)(2,1)} custom-call(s32[1]{0:T(128)} %get-tuple-element.133.me_ref, f32[2,680]{1,0:T(2,128)S(1)} %get-tuple-element.134.mean_ref, f32[2,680]{1,0:T(2,128)S(1)} %get-tuple-element.135.inverse_ref, bf16[360,360]{1,0:T(8,128)(2,1)S(1)} %get-tuple-element.136.same_group_ref, ...), custom_call_target="tpu_custom_call" | custom-call | flops 532684800 | bytes 3133440 | tf_op jit(solution)/shard_map/cond/branch_0_fun/input_grad/pallas_call | solution.py:367
  53.9 0.0 collective-permute-done.other_ref
  53.9 1.3 %half_average.3 = (f32[176,360]{1,0:T(8,128)S(1)}, f32[1]{0:T(128)}) custom-call(f32[1]{0:T(128)} %get-tuple-element.142.push_ref, f32[176,360]{1,0:T(8,128)S(1)} %get-tuple-element.143.moved_ref, bf16[528,128]{1,0:T(8,128)(2,1)S(1)} %collective-permute-done.other_ref), custom_call_target="tpu_custom_call" | custom-call | bytes 489600 | tf_op jit(solution)/shard_map/cond/branch_0_fun/half_average/pallas_call | solution.py:367
  55.4 0.0 collective-permute-done.15.refs_0_
  55.5 0.0 collective-permute-done.16.refs_1_
  55.5 0.0 collective-permute-done.17.refs_2_
  55.5 0.0 copy-start.3
  55.5 0.9 %adam.3 = (f32[176,320]{1,0:T(8,128)S(1)}, f32[176,320]{1,0:T(8,128)S(1)}, bf16[448,128]{1,0:T(8,128)(2,1)S(1)}) custom-call(f32[2]{0:T(128)S(1)} %pad_maximum_fusion.scales_ref, f32[176,320]{1,0:T(8,128)S(1)} %get-tuple-element.280.refs_6_.own_ref, bf16[448,128]{1,0:T(8,128)(2,1)S(1)} %collective-permute-done.15.refs_0_, ...), custom_call_target="tpu_custom_call" | custom-call | bytes 435200 | tf_op jit(solution)/shard_map/adam/pallas_call | solution.py:367
  56.4 0.0 copy-done.3
  56.4 6.2 %conditional.3 = (f32[170,1,680]{2,1,0:T(1,128)}, f32[170,1,680]{2,1,0:T(1,128)}, f32[1,170,680]{2,0,1:T(1,128)}) conditional(s32[]{:T(128)} %clamp.4, (f32[170,1,680]{2,1,0:T(1,128)S(1)}, f32[170,1,680]{2,1,0:T(1,128)S(1)}, f32[176,360]{1,0:T(8,128)S(1)}, f32[176,320]{1,0:T(8,128)S(1)}, bf16[448,128]{1,0:T(8,128)(2,1)S(1)}, ...), branch_computations={%region_3.4_spmd, %region_4.5_spmd, %region_5.6_spmd} | conditional | bytes 2308416 | solution.py:511
  56.5 1.6 %collective-permute-start.3 = (bf16[448,128]{1,0:T(8,128)(2,1)S(1)}, bf16[448,128]{1,0:T(8,128)(2,1)S(1)}, u32[]{:S(2)}, u32[]{:S(2)}) collective-permute-start(bf16[448,128]{1,0:T(8,128)(2,1)S(1)} %get-tuple-element.201), channel_id=1, source_target_pairs={{0,4},{4,8},{8,12},{12,16},{16,20},{20,24},{24,28},{28,0},{1,5},{5... | collective-permute-start | bytes 344072 | tf_op jit(solution)/shard_map/cond/branch_0_fun/ppermute | solution.py:385
  58.1 1.6 %moments.3 = (f32[170,1,680]{2,1,0:T(1,128)}, f32[170,1,680]{2,1,0:T(1,128)}) custom-call(f32[170,1,680]{2,1,0:T(1,128)S(1)} %get-tuple-element.193.first_ref, f32[170,1,680]{2,1,0:T(1,128)S(1)} %get-tuple-element.194.second_ref, f32[176,360]{1,0:T(8,128)S(1)} %get-tuple-element.195.refs_0_, f32[176,320]{1,0:T(8,128)S(1)} %get-tuple-element.196.refs_1_), custom_call_target="tpu_custom_call" | custom-call | bytes 924800 | tf_op jit(solution)/shard_map/cond/branch_0_fun/moments/pallas_call | solution.py:367
  59.7 1.9 %collective-permute-done.3.other_ref = bf16[448,128]{1,0:T(8,128)(2,1)S(1)} collective-permute-done((bf16[448,128]{1,0:T(8,128)(2,1)S(1)}, bf16[448,128]{1,0:T(8,128)(2,1)S(1)}, u32[]{:S(2)}, u32[]{:S(2)}) %collective-permute-start.3) | collective-permute-done | bytes 114720 | tf_op jit(solution)/shard_map/cond/branch_0_fun/ppermute | solution.py:385
  61.6 1.0 %average.3 = f32[170,1,680]{2,1,0:T(1,128)} custom-call(f32[176,360]{1,0:T(8,128)S(1)} %get-tuple-element.199.mean_ref, f32[176,320]{1,0:T(8,128)S(1)} %get-tuple-element.200.moved_ref, bf16[448,128]{1,0:T(8,128)(2,1)S(1)} %collective-permute-done.3.other_ref), custom_call_target="tpu_custom_call" | custom-call | bytes 924800 | tf_op jit(solution)/shard_map/cond/branch_0_fun/average/pallas_call | solution.py:367
  (2 shorter events, 0.0 us)
Async XLA Ops:
  2.6 13.2 %collective-permute-start.8 = (bf16[528,128]{1,0:T(8,128)(2,1)S(1)}, bf16[528,128]{1,0:T(8,128)(2,1)S(1)}, u32[]{:S(2)}, u32[]{:S(2)}) collective-permute-start(bf16[528,128]{1,0:T(8,128)(2,1)S(1)} %get-tuple-element.268.refs_0_), channel_id=1, source_target_pairs={{0,1},{1,2},{2,3},{3,0},{4,5},{5,6},{6,7},{7,4},{8,9},{9,10},{10,1... | collective-permute-start | bytes 405512 | tf_op jit(solution)/shard_map/ppermute | solution.py:385
  4.2 17.6 %collective-permute-start.7 = (bf16[528,128]{1,0:T(8,128)(2,1)S(1)}, bf16[528,128]{1,0:T(8,128)(2,1)S(1)}, u32[]{:S(2)}, u32[]{:S(2)}) collective-permute-start(bf16[528,128]{1,0:T(8,128)(2,1)S(1)} %get-tuple-element.268.refs_0_), channel_id=1, source_target_pairs={{0,2},{1,3},{2,0},{3,1},{4,6},{5,7},{6,4},{7,5},{8,10},{9,11},{10,... | collective-permute-start | bytes 405512 | tf_op jit(solution)/shard_map/ppermute | solution.py:385
  5.3 17.2 %collective-permute-start.6 = (bf16[528,128]{1,0:T(8,128)(2,1)S(1)}, bf16[528,128]{1,0:T(8,128)(2,1)S(1)}, u32[]{:S(2)}, u32[]{:S(2)}) collective-permute-start(bf16[528,128]{1,0:T(8,128)(2,1)S(1)} %get-tuple-element.268.refs_0_), channel_id=1, source_target_pairs={{0,3},{1,0},{2,1},{3,2},{4,7},{5,4},{6,5},{7,6},{8,11},{9,8},{10,9... | collective-permute-start | bytes 405512 | tf_op jit(solution)/shard_map/ppermute | solution.py:385
  7.3 21.1 %collective-permute-start.11 = (bf16[448,128]{1,0:T(8,128)(2,1)S(1)}, bf16[448,128]{1,0:T(8,128)(2,1)S(1)}, u32[]{:S(2)}, u32[]{:S(2)}) collective-permute-start(bf16[448,128]{1,0:T(8,128)(2,1)S(1)} %get-tuple-element.272.refs_0_), channel_id=1, source_target_pairs={{0,1},{1,2},{2,3},{3,0},{4,5},{5,6},{6,7},{7,4},{8,9},{9,10},{10,1... | collective-permute-start | bytes 344072 | tf_op jit(solution)/shard_map/ppermute | solution.py:385
  7.3 22.9 %collective-permute-start.10 = (bf16[448,128]{1,0:T(8,128)(2,1)S(1)}, bf16[448,128]{1,0:T(8,128)(2,1)S(1)}, u32[]{:S(2)}, u32[]{:S(2)}) collective-permute-start(bf16[448,128]{1,0:T(8,128)(2,1)S(1)} %get-tuple-element.272.refs_0_), channel_id=1, source_target_pairs={{0,2},{1,3},{2,0},{3,1},{4,6},{5,7},{6,4},{7,5},{8,10},{9,11},{10,... | collective-permute-start | bytes 344072 | tf_op jit(solution)/shard_map/ppermute | solution.py:385
  11.7 0.7 %copy-start = (bf16[2,680]{1,0:T(2,128)(2,1)S(1)}, bf16[2,680]{1,0:T(2,128)(2,1)}, u32[]{:S(2)}) copy-start(bf16[2,680]{1,0:T(2,128)(2,1)} %shift_ref.1) | copy-start | bytes 8164
  15.8 14.5 %collective-permute-start.9 = (bf16[448,128]{1,0:T(8,128)(2,1)S(1)}, bf16[448,128]{1,0:T(8,128)(2,1)S(1)}, u32[]{:S(2)}, u32[]{:S(2)}) collective-permute-start(bf16[448,128]{1,0:T(8,128)(2,1)S(1)} %get-tuple-element.272.refs_0_), channel_id=1, source_target_pairs={{0,3},{1,0},{2,1},{3,2},{4,7},{5,4},{6,5},{7,6},{8,11},{9,8},{10,9... | collective-permute-start | bytes 344072 | tf_op jit(solution)/shard_map/ppermute | solution.py:385
  25.5 10.2 %collective-permute-start.12 = (bf16[528,128]{1,0:T(8,128)(2,1)S(1)}, bf16[528,128]{1,0:T(8,128)(2,1)S(1)}, u32[]{:S(2)}, u32[]{:S(2)}) collective-permute-start(bf16[528,128]{1,0:T(8,128)(2,1)S(1)} %get-tuple-element.277), channel_id=1, source_target_pairs={{0,1},{1,2},{2,3},{3,0},{4,5},{5,6},{6,7},{7,4},{8,9},{9,10},{10,1... | collective-permute-start | bytes 405512 | tf_op jit(solution)/shard_map/ppermute | solution.py:385
  25.5 13.2 %collective-permute-start.13 = (bf16[528,128]{1,0:T(8,128)(2,1)S(1)}, bf16[528,128]{1,0:T(8,128)(2,1)S(1)}, u32[]{:S(2)}, u32[]{:S(2)}) collective-permute-start(bf16[528,128]{1,0:T(8,128)(2,1)S(1)} %get-tuple-element.278), channel_id=1, source_target_pairs={{0,2},{1,3},{2,0},{3,1},{4,6},{5,7},{6,4},{7,5},{8,10},{9,11},{10,... | collective-permute-start | bytes 405512 | tf_op jit(solution)/shard_map/ppermute | solution.py:385
  28.3 15.8 %collective-permute-start.14 = (bf16[528,128]{1,0:T(8,128)(2,1)S(1)}, bf16[528,128]{1,0:T(8,128)(2,1)S(1)}, u32[]{:S(2)}, u32[]{:S(2)}) collective-permute-start(bf16[528,128]{1,0:T(8,128)(2,1)S(1)} %get-tuple-element.279), channel_id=1, source_target_pairs={{0,3},{1,0},{2,1},{3,2},{4,7},{5,4},{6,5},{7,6},{8,11},{9,8},{10,9... | collective-permute-start | bytes 405512 | tf_op jit(solution)/shard_map/ppermute | solution.py:385
  33.2 22.2 %collective-permute-start.15 = (bf16[448,128]{1,0:T(8,128)(2,1)S(1)}, bf16[448,128]{1,0:T(8,128)(2,1)S(1)}, u32[]{:S(2)}, u32[]{:S(2)}) collective-permute-start(bf16[448,128]{1,0:T(8,128)(2,1)S(1)} %get-tuple-element.285), channel_id=1, source_target_pairs={{0,1},{1,2},{2,3},{3,0},{4,5},{5,6},{6,7},{7,4},{8,9},{9,10},{10,1... | collective-permute-start | bytes 344072 | tf_op jit(solution)/shard_map/ppermute | solution.py:385
  33.4 22.1 %collective-permute-start.16 = (bf16[448,128]{1,0:T(8,128)(2,1)S(1)}, bf16[448,128]{1,0:T(8,128)(2,1)S(1)}, u32[]{:S(2)}, u32[]{:S(2)}) collective-permute-start(bf16[448,128]{1,0:T(8,128)(2,1)S(1)} %get-tuple-element.286), channel_id=1, source_target_pairs={{0,2},{1,3},{2,0},{3,1},{4,6},{5,7},{6,4},{7,5},{8,10},{9,11},{10,... | collective-permute-start | bytes 344072 | tf_op jit(solution)/shard_map/ppermute | solution.py:385
  35.7 19.8 %collective-permute-start.17 = (bf16[448,128]{1,0:T(8,128)(2,1)S(1)}, bf16[448,128]{1,0:T(8,128)(2,1)S(1)}, u32[]{:S(2)}, u32[]{:S(2)}) collective-permute-start(bf16[448,128]{1,0:T(8,128)(2,1)S(1)} %get-tuple-element.287), channel_id=1, source_target_pairs={{0,3},{1,0},{2,1},{3,2},{4,7},{5,4},{6,5},{7,6},{8,11},{9,8},{10,9... | collective-permute-start | bytes 344072 | tf_op jit(solution)/shard_map/ppermute | solution.py:385
  44.2 2.7 %copy-start.1 = (f32[1,170,680]{2,0,1:T(1,128)S(1)}, f32[1,170,680]{2,0,1:T(1,128)}, u32[]{:S(2)}) copy-start(f32[1,170,680]{2,0,1:T(1,128)} %param.18) | copy-start | bytes 1387204
  44.2 2.7 %copy-start.2 = (f32[1,170,680]{2,0,1:T(1,128)S(1)}, f32[1,170,680]{2,0,1:T(1,128)}, u32[]{:S(2)}) copy-start(f32[1,170,680]{2,0,1:T(1,128)} %param.19) | copy-start | bytes 1387204
  46.9 7.0 %collective-permute-start = (bf16[528,128]{1,0:T(8,128)(2,1)S(1)}, bf16[528,128]{1,0:T(8,128)(2,1)S(1)}, u32[]{:S(2)}, u32[]{:S(2)}) collective-permute-start(bf16[528,128]{1,0:T(8,128)(2,1)S(1)} %get-tuple-element.144), channel_id=1, source_target_pairs={{0,4},{4,8},{8,12},{12,16},{16,20},{20,24},{24,28},{28,0},{1,5},{5... | collective-permute-start | bytes 405512 | tf_op jit(solution)/shard_map/cond/branch_0_fun/ppermute | solution.py:385
  55.5 1.0 %copy-start.3 = (f32[176,360]{1,0:T(8,128)S(1)}, f32[176,360]{1,0:T(8,128)}, u32[]{:S(2)}) copy-start(f32[176,360]{1,0:T(8,128)} %get-tuple-element.284) | copy-start | bytes 760324
  56.5 5.2 %collective-permute-start.3 = (bf16[448,128]{1,0:T(8,128)(2,1)S(1)}, bf16[448,128]{1,0:T(8,128)(2,1)S(1)}, u32[]{:S(2)}, u32[]{:S(2)}) collective-permute-start(bf16[448,128]{1,0:T(8,128)(2,1)S(1)} %get-tuple-element.201), channel_id=1, source_target_pairs={{0,4},{4,8},{8,12},{12,16},{16,20},{20,24},{24,28},{28,0},{1,5},{5... | collective-permute-start | bytes 344072 | tf_op jit(solution)/shard_map/cond/branch_0_fun/ppermute | solution.py:385

commit v7 on v6

--- a/solution.py
+++ b/solution.py
@@ -165,7 +165,7 @@
     normed = [centered[i] * inverse[i : i + 1] for i in range(samples)]
     act = jnp.concatenate([part * sigmoid(part) for part in normed], axis=0).T
     for block in range(shards):
-        slot = lax.rem(block + shards - me_ref[0], shards)
+        slot = jnp.bitwise_xor(me_ref[0], block)
         act_ref[pl.ds(pl.multiple_of(slot * deep, TILE_ROWS), deep), :] = jnp.concatenate(
             [act[block * rows : (block + 1) * rows], jnp.zeros((deep - rows, act.shape[1]), jnp.float32)], axis=0
         ).astype(jnp.bfloat16)
@@ -241,7 +241,7 @@
     for index, (pack, weight_ref) in enumerate(zip(packs, weight_refs)):
         copies[index].wait()
         for block in range(shards):
-            slot = lax.rem(block + shards - me_ref[0], shards)
+            slot = jnp.bitwise_xor(me_ref[0], block)
             rows_ref[block * rows : (block + 1) * rows, : pack.columns] = weight_ref[
                 pl.ds(pl.multiple_of(slot * pack.deep, TILE_ROWS), pack.deep), :
             ].astype(jnp.float32)[:rows]
@@ -289,6 +289,10 @@
     moved_ref[:rows, :] = params - update
 
 
+def merge_kernel(one_ref, other_ref, out_ref):
+    out_ref[...] = (one_ref[...].astype(jnp.float32) + other_ref[...].astype(jnp.float32)).astype(out_ref.dtype)
+
+
 def fetch(hbm_refs, row_refs, sems):
     copies = [
         pltpu.make_async_copy(source, target, sems.at[i])
@@ -299,8 +303,8 @@
     return copies
 
 
-def first_adam_kernel(shards, pack, scales_ref, push_ref, own_ref, *refs):
-    other_refs, refs = refs[: shards - 1], refs[shards - 1 :]
+def first_adam_kernel(shards, count, pack, scales_ref, push_ref, own_ref, *refs):
+    other_refs, refs = refs[:count], refs[count:]
     hbm_refs, token_ref, (grad_ref, moved_ref, sent_ref) = refs[:3], refs[3], refs[4:7]
     row_refs, sems = refs[7:10], refs[10]
     copies = fetch(hbm_refs, row_refs, sems)
@@ -317,15 +321,15 @@
 
 
 def cut_kernel(pack, *refs):
-    hbm_refs, out_refs, row_refs, sems = refs[:3], refs[3:6], refs[6:9], refs[9]
+    hbm_refs, out_refs, row_refs, sems = refs[:3], refs[4:7], refs[7:10], refs[10]
     for copy, row_ref, out_ref in zip(fetch(hbm_refs, row_refs, sems), row_refs, out_refs):
         copy.wait()
         out_ref[...] = row_ref[:, 0, pack.start : pack.stop]
 
 
-def second_adam_kernel(shards, pack, scales_ref, own_ref, *refs):
-    other_refs, refs = refs[: shards - 1], refs[shards - 1 :]
-    block_refs, token_ref, (grad_ref, moved_ref, sent_ref) = refs[:3], refs[3], refs[4:]
+def second_adam_kernel(shards, count, pack, scales_ref, own_ref, *refs):
+    other_refs, refs = refs[:count], refs[count:]
+    block_refs, (grad_ref, moved_ref, sent_ref) = refs[:3], refs[3:]
     adam_step(
         shards, pack, scales_ref, own_ref, other_refs, lambda: [ref[...] for ref in block_refs], grad_ref, moved_ref
     )
@@ -383,6 +387,42 @@
 def moved_on(block, axis, distance):
     size = lax.axis_size(axis)
     return lax.ppermute(block, axis, [(i, (i + distance) % size) for i in range(size)])
+
+
+def exchanged(block, axis, bit):
+    return lax.ppermute(block, axis, [(i, i ^ bit) for i in range(lax.axis_size(axis))])
+
+
+def lowest_bit(slot):
+    return slot & -slot
+
+
+def gathered(piece, shards):
+    held = [piece]
+    for slot in range(1, shards):
+        bit = lowest_bit(slot)
+        held.append(exchanged(held[slot ^ bit], "dp", bit))
+    return held
+
+
+def scattered(sends, shards):
+    held = dict(enumerate(sends, 1))
+    arrived = []
+    for slot in sorted(held, key=lambda slot: (-slot.bit_count(), slot)):
+        bit = lowest_bit(slot)
+        other = exchanged(held[slot], "dp", bit)
+        if slot == bit:
+            arrived.append(other)
+        else:
+            held[slot ^ bit] = call(
+                merge_kernel,
+                "merge",
+                jax.ShapeDtypeStruct(other.shape, other.dtype),
+                [BLOCKS] * 2,
+                (held[slot ^ bit], other),
+                elements=other.size,
+            )
+    return arrived
 
 
 def column_cuts(channels):
@@ -412,9 +452,7 @@
         scratch=[pltpu.VMEM((deep, channels), jnp.float32)],
         elements=rows * channels,
     )
-    weights = [
-        [piece] + [moved_on(piece, "dp", -slot) for slot in range(1, shards)] for piece in shard_list
-    ]
+    weights = [gathered(piece, shards) for piece in shard_list]
 
     level_count = lax.axis_size("replica").bit_length() - 1
     distance_bits = step[0] % level_count
@@ -472,7 +510,7 @@
         hidden_grads.append(grad_hidden)
         full_weights.append(full_weight)
         owns.append(own)
-        arrived.append([moved_on(send, "dp", slot) for slot, send in enumerate(sends, 1)])
+        arrived.append(scattered(sends, shards))
 
     def input_grad(*operands):
         return call(
@@ -510,81 +548,66 @@
 
         return lax.switch(distance_bits, [branch(1 << power) for power in range(level_count)], *operands)
 
+    grad_input = input_grad(
+        me, mean_in, inverse_in, same_group, block_input, *hidden_grads, *full_weights
+    )
     early, late = packs
     arrays = [stay(params), stay(first_moment), stay(second_moment)]
     array_scratch = [pltpu.VMEM(params.shape, jnp.float32)] * 3 + [pltpu.SemaphoreType.DMA((3,))]
+    late_blocks = call(
+        functools.partial(cut_kernel, late),
+        "cut",
+        (jax.ShapeDtypeStruct((rows, late.columns), jnp.float32),) * 3,
+        [IN_HBM] * 3 + [TOKEN],
+        (*arrays, token),
+        scratch=array_scratch,
+        elements=rows * late.columns,
+    )
     grad_a, moved_a, sent_a = call(
-        functools.partial(first_adam_kernel, shards, early),
+        functools.partial(first_adam_kernel, shards, len(arrived[0]), early),
         "adam",
         (early.block(), early.block(), early.payload()),
-        [SCALARS] * 2 + [BLOCKS] * shards + [IN_HBM] * 3 + [TOKEN],
+        [SCALARS] * 2 + [BLOCKS] * (1 + len(arrived[0])) + [IN_HBM] * 3 + [TOKEN],
         (scales, push_weight, owns[0], *arrived[0], *arrays, token),
         scratch=array_scratch,
         elements=rows * early.columns,
     )
 
-    def finish_early(move, sent, moved, params, first_moment, second_moment, *operands):
-        other = move(sent)
-        grad_input = input_grad(*operands)
-        blocks = call(
-            functools.partial(cut_kernel, late),
-            "cut",
-            (jax.ShapeDtypeStruct((rows, late.columns), jnp.float32),) * 3,
-            [IN_HBM] * 3,
-            (stay(params), stay(first_moment), stay(second_moment)),
-            scratch=array_scratch,
+    def finish(move, sent, grad_a, moved_a, own, *operands):
+        other_a = move(sent)
+        grad_b, moved_b, sent_b = call(
+            functools.partial(second_adam_kernel, shards, len(arrived[1]), late),
+            "adam",
+            (late.block(), late.block(), late.payload()),
+            [SCALARS] + [BLOCKS] * (4 + len(arrived[1])),
+            (scales, own, *operands),
             elements=rows * late.columns,
         )
+        other_b = move(sent_b)
         mean, weight = call(
             functools.partial(half_average_kernel, early),
             "half_average",
             (early.block(), jax.ShapeDtypeStruct((1,), jnp.float32)),
             [SCALARS] + [BLOCKS] * 2,
-            (push_weight, moved, other),
+            (push_weight, moved_a, other_a),
             out_specs=(BLOCKS, SCALARS),
             elements=rows * early.columns,
         )
-        return (grad_input, mean, weight, *blocks)
-
-    grad_input, mean_a, new_weight, *late_blocks = from_behind(
-        finish_early,
-        sent_a,
-        moved_a,
-        params,
-        first_moment,
-        second_moment,
-        me,
-        mean_in,
-        inverse_in,
-        same_group,
-        block_input,
-        *hidden_grads,
-        *full_weights,
-    )
-    grad_b, moved_b, sent_b = call(
-        functools.partial(second_adam_kernel, shards, late),
-        "adam",
-        (late.block(), late.block(), late.payload()),
-        [SCALARS] + [BLOCKS] * (3 + shards) + [TOKEN],
-        (scales, owns[1], *arrived[1], *late_blocks, mean_a),
-        elements=rows * late.columns,
-    )
-
-    def finish_late(move, sent, grad_a, grad_b, mean_a, moved_b):
-        other = move(sent)
         averaged = call(
             functools.partial(average_kernel, late),
             "average",
             pltpu.HBM(params.shape, jnp.float32),
             [BLOCKS] * 3,
-            (mean_a, moved_b, other),
+            (mean, moved_b, other_b),
             scratch=[pltpu.VMEM(params.shape, jnp.float32), pltpu.SemaphoreType.DMA],
             out_specs=IN_HBM,
             elements=rows * channels,
         )
-        return (*moments(grad_a, grad_b), averaged)
-
-    first_new, second_new, averaged = from_behind(finish_late, sent_b, grad_a, grad_b, mean_a, moved_b)
+        return (*moments(grad_a, grad_b), averaged, weight)
+
+    first_new, second_new, averaged, new_weight = from_behind(
+        finish, sent_a, grad_a, moved_a, owns[1], *arrived[1], *late_blocks
+    )
     return (
         grad_input,
         *(jnp.transpose(array, (1, 0, 2)) for array in (averaged, first_new, second_new)),

time: 63.7 us -> 59.9 us (0.940)
  the two profiles are of different devices: /device:TPU:8 before, /device:TPU:0 now
where the time goes in v7:
time: 59.9 us; the launch traced here: 59.6 us
  Pallas kernels  23.6 us (39%)
  starting transfers between devices  20 us (33%)
  waiting for transfers between devices  11.8 us (20%)
  between operations  2.43 us (4%)
  local copies, waits for them, and re-layouts  1.5 us (3%)
    pallas_call x13, Pallas kernels, call(): pl.pallas_call(kernel, out_shape=outs, in_specs=specs, out_specs=out_spec...  23.6 us
    ppermute x12, starting transfers between devices, exchanged(): lax.ppermute(block, axis, [(i, i ^ bit) for i in range(lax.axis_size(axis...  17.9 us
    ppermute x12, waiting for transfers between devices, exchanged(): lax.ppermute(block, axis, [(i, i ^ bit) for i in range(lax.axis_size(axis...  10.1 us
    ppermute x2, starting transfers between devices, moved_on(): lax.ppermute(block, axis, [(i, (i + distance) % size) for i in range(size)])  2.16 us
    ppermute x2, waiting for transfers between devices, moved_on(): lax.ppermute(block, axis, [(i, (i + distance) % size) for i in range(size)])  1.74 us
    unnamed x8, local copies, waits for them, and re-layouts  1.5 us
  transfers between devices with their start and end apart: 14, of which 4 were waited for; matrix products, arithmetic and copies ran while one was open for 0% of the time, Pallas kernels for 37%

profile of v7, /device:TPU:0, one launch (start us, length us, event | category | flops | bytes accessed | tf_op | source)
XLA Modules:
  0.0 59.6 jit_solution(14796968155779739004)
XLA Ops:
  1.3 0.0 copy-start
  1.3 1.0 %copy-done = f32[1,170,680]{2,0,1:T(1,128)S(1)} copy-done((f32[1,170,680]{2,0,1:T(1,128)S(1)}, f32[1,170,680]{2,0,1:T(1,128)}, u32[]{:S(2)}) %copy-start) | copy-done | bytes 462424
  2.3 0.3 cast.1
  2.6 4.1 %collective-permute-start.7 = (bf16[528,128]{1,0:T(8,128)(2,1)S(1)}, bf16[528,128]{1,0:T(8,128)(2,1)S(1)}, u32[]{:S(2)}, u32[]{:S(2)}) collective-permute-start(bf16[528,128]{1,0:T(8,128)(2,1)S(1)} %get-tuple-element.182.refs_0_), channel_id=1, source_target_pairs={{0,2},{1,3},{2,0},{3,1},{4,6},{5,7},{6,4},{7,5},{8,10},{9,11},{10,... | collective-permute-start | bytes 405512 | tf_op jit(solution)/shard_map/ppermute | solution.py:393
  6.7 0.1 collective-permute-start.10
  6.8 1.8 %collective-permute-start.6 = (bf16[528,128]{1,0:T(8,128)(2,1)S(1)}, bf16[528,128]{1,0:T(8,128)(2,1)S(1)}, u32[]{:S(2)}, u32[]{:S(2)}) collective-permute-start(bf16[528,128]{1,0:T(8,128)(2,1)S(1)} %get-tuple-element.182.refs_0_), channel_id=1, source_target_pairs={{0,1},{1,0},{2,3},{3,2},{4,5},{5,4},{6,7},{7,6},{8,9},{9,8},{10,11... | collective-permute-start | bytes 405512 | tf_op jit(solution)/shard_map/ppermute | solution.py:393
  8.6 7.9 %collective-permute-done.7.refs_2_ = bf16[528,128]{1,0:T(8,128)(2,1)S(1)} collective-permute-done((bf16[528,128]{1,0:T(8,128)(2,1)S(1)}, bf16[528,128]{1,0:T(8,128)(2,1)S(1)}, u32[]{:S(2)}, u32[]{:S(2)}) %collective-permute-start.7) | collective-permute-done | bytes 135200 | tf_op jit(solution)/shard_map/ppermute | solution.py:393
  16.5 0.0 collective-permute-start.8
  16.5 2.0 %collective-permute-start.9 = (bf16[448,128]{1,0:T(8,128)(2,1)S(1)}, bf16[448,128]{1,0:T(8,128)(2,1)S(1)}, u32[]{:S(2)}, u32[]{:S(2)}) collective-permute-start(bf16[448,128]{1,0:T(8,128)(2,1)S(1)} %get-tuple-element.186.refs_0_), channel_id=1, source_target_pairs={{0,1},{1,0},{2,3},{3,2},{4,5},{5,4},{6,7},{7,6},{8,9},{9,8},{10,11... | collective-permute-start | bytes 344072 | tf_op jit(solution)/shard_map/ppermute | solution.py:393
  19.3 0.0 copy-start.1
  19.3 0.0 collective-permute-done.10.refs_2_
  19.3 0.1 collective-permute-start.11
  19.4 0.1 pad_maximum_fusion.scales_ref
  19.5 0.5 copy-done.1
  19.9 3.4 %norm_in.1 = (bf16[704,576]{1,0:T(8,128)(2,1)S(1)}, f32[2,680]{1,0:T(2,128)S(1)}, f32[2,680]{1,0:T(2,128)S(1)}, bf16[360,360]{1,0:T(8,128)(2,1)S(1)}, f32[2,360]...) custom-call(s32[1]{0:T(128)} %bitcast.3.me_ref, ...), custom_call_target="tpu_custom_call" | custom-call | bytes 3133440 | tf_op jit(solution)/shard_map/norm_in/pallas_call | solution.py:371
  23.3 0.0 collective-permute-done.6.refs_1_
  23.3 0.0 collective-permute-done.8.refs_3_
  23.3 2.9 %mix.2 = (bf16[576,360]{1,0:T(8,128)(2,1)}, bf16[704,360]{1,0:T(8,128)(2,1)}, f32[176,360]{1,0:T(8,128)S(1)}, bf16[528,128]{1,0:T(8,128)(2,1)S(1)}, bf16[528,128...) custom-call(bf16[704,576]{1,0:T(8,128)(2,1)S(1)} %get-tuple-element.179.act_ref, ...), custom_call_target="tpu_custom_call" | custom-call | flops 564019200 | bytes 1658880 | tf_op jit(solution)/shard_map/mix/pallas_call | solution.py:371
  26.3 1.6 %collective-permute-start.16 = (bf16[528,128]{1,0:T(8,128)(2,1)S(1)}, bf16[528,128]{1,0:T(8,128)(2,1)S(1)}, u32[]{:S(2)}, u32[]{:S(2)}) collective-permute-start(bf16[528,128]{1,0:T(8,128)(2,1)S(1)} %get-tuple-element.200), channel_id=1, source_target_pairs={{0,1},{1,0},{2,3},{3,2},{4,5},{5,4},{6,7},{7,6},{8,9},{9,8},{10,11... | collective-permute-start | bytes 405512 | tf_op jit(solution)/shard_map/ppermute | solution.py:393
  27.9 0.0 collective-permute-done.9.refs_1_
  27.9 0.0 collective-permute-done.11.refs_3_
  27.9 3.0 %mix.3 = (bf16[576,320]{1,0:T(8,128)(2,1)}, bf16[704,320]{1,0:T(8,128)(2,1)}, f32[176,320]{1,0:T(8,128)S(1)}, bf16[448,128]{1,0:T(8,128)(2,1)S(1)}, bf16[448,128...) custom-call(bf16[704,576]{1,0:T(8,128)(2,1)S(1)} %get-tuple-element.179.act_ref, ...), custom_call_target="tpu_custom_call" | custom-call | flops 501350400 | bytes 1474560 | tf_op jit(solution)/shard_map/mix/pallas_call | solution.py:371
  30.9 0.5 collective-permute-start.13
  31.4 1.5 %collective-permute-start.15 = (bf16[528,128]{1,0:T(8,128)(2,1)S(1)}, bf16[528,128]{1,0:T(8,128)(2,1)S(1)}, u32[]{:S(2)}, u32[]{:S(2)}) collective-permute-start(bf16[528,128]{1,0:T(8,128)(2,1)S(1)} %get-tuple-element.198), channel_id=1, source_target_pairs={{0,1},{1,0},{2,3},{3,2},{4,5},{5,4},{6,7},{7,6},{8,9},{9,8},{10,11... | collective-permute-start | bytes 405512 | tf_op jit(solution)/shard_map/ppermute | solution.py:393
  33.0 0.0 collective-permute-done.16.other_ref
  33.0 1.9 %collective-permute-start.17 = (bf16[528,128]{1,0:T(8,128)(2,1)S(1)}, bf16[528,128]{1,0:T(8,128)(2,1)S(1)}, u32[]{:S(2)}, u32[]{:S(2)}) collective-permute-start(bf16[528,128]{1,0:T(8,128)(2,1)S(1)} %merge.3), channel_id=1, source_target_pairs={{0,2},{1,3},{2,0},{3,1},{4,6},{5,7},{6,4},{7,5},{8,10},{9,11},{10,... | collective-permute-start | bytes 405512 | tf_op jit(solution)/shard_map/ppermute | solution.py:393
  34.9 1.5 %collective-permute-start.12 = (bf16[448,128]{1,0:T(8,128)(2,1)S(1)}, bf16[448,128]{1,0:T(8,128)(2,1)S(1)}, u32[]{:S(2)}, u32[]{:S(2)}) collective-permute-start(bf16[448,128]{1,0:T(8,128)(2,1)S(1)} %get-tuple-element.192), channel_id=1, source_target_pairs={{0,1},{1,0},{2,3},{3,2},{4,5},{5,4},{6,7},{7,6},{8,9},{9,8},{10,11... | collective-permute-start | bytes 344072 | tf_op jit(solution)/shard_map/ppermute | solution.py:393
  36.4 2.2 %collective-permute-done.13.other_ref = bf16[448,128]{1,0:T(8,128)(2,1)S(1)} collective-permute-done((bf16[448,128]{1,0:T(8,128)(2,1)S(1)}, bf16[448,128]{1,0:T(8,128)(2,1)S(1)}, u32[]{:S(2)}, u32[]{:S(2)}) %collective-permute-start.13) | collective-permute-done | bytes 114720 | tf_op jit(solution)/shard_map/ppermute | solution.py:393
  38.6 2.6 %collective-permute-start.14 = (bf16[448,128]{1,0:T(8,128)(2,1)S(1)}, bf16[448,128]{1,0:T(8,128)(2,1)S(1)}, u32[]{:S(2)}, u32[]{:S(2)}) collective-permute-start(bf16[448,128]{1,0:T(8,128)(2,1)S(1)} %merge.2), channel_id=1, source_target_pairs={{0,2},{1,3},{2,0},{3,1},{4,6},{5,7},{6,4},{7,5},{8,10},{9,11},{10,... | collective-permute-start | bytes 344072 | tf_op jit(solution)/shard_map/ppermute | solution.py:393
  41.2 1.6 %cut.1 = (f32[170,320]{1,0:T(8,128)S(1)}, f32[170,320]{1,0:T(8,128)S(1)}, f32[170,320]{1,0:T(8,128)S(1)}) custom-call(f32[170,1,680]{2,1,0:T(1,128)} %bitcast.10, f32[170,1,680]{2,1,0:T(1,128)} %bitcast.13, f32[170,1,680]{2,1,0:T(1,128)} %bitcast.18, f32[176,320]{1,0:T(8,128)S(1)} %get-tuple-element.191.refs_3_.refs_5_), custom_call_target="tpu_custom_call" | custom-call | bytes 435200 | tf_op jit(solution)/shard_map/cut/pallas_call | solution.py:371
  42.8 5.1 %input_grad.1 = bf16[2,288,680]{2,1,0:T(8,128)(2,1)} custom-call(s32[1]{0:T(128)} %bitcast.3.me_ref, f32[2,680]{1,0:T(2,128)S(1)} %get-tuple-element.176.refs_4_.mean_ref, f32[2,680]{1,0:T(2,128)S(1)} %get-tuple-element.177.inverse_ref, bf16[360,360]{1,0:T(8,128)(2,1)S(1)} %get-tuple-element.178.same_group_ref, bf16[2,288,680]{2,1,0:T(8,128)(2,1)} %x_hbm.3, ...), custom_call_target="tpu_custom_call" | custom-call | flops 532684800 | bytes 3133440 | tf_op jit(solution)/shard_map/input_grad/pallas_call | solution.py:371
  47.9 0.0 copy-start.2
  48.0 0.0 copy-start.3
  48.0 0.0 collective-permute-done.15.refs_0_
  48.0 0.0 collective-permute-done.17.refs_1_
  48.0 2.5 %adam.7 = (f32[176,360]{1,0:T(8,128)S(1)}, f32[176,360]{1,0:T(8,128)S(1)}, bf16[528,128]{1,0:T(8,128)(2,1)S(1)}) custom-call(f32[2]{0:T(128)S(1)} %pad_maximum_fusion.scales_ref, f32[1]{0:T(128)S(6)} %copy.25.push_ref, f32[176,360]{1,0:T(8,128)S(1)} %get-tuple-element.187.refs_4_.own_ref, bf16[528,128]{1,0:T(8,128)(2,1)S(1)} %collective-permute-done.15.refs_0_, ...), custom_call_target="tpu_custom_call" | custom-call | bytes 489600 | tf_op jit(solution)/shard_map/adam/pallas_call | solution.py:371
  50.5 0.0 collective-permute-done.12
  50.5 0.0 collective-permute-done.14
  50.5 0.0 copy-done.2
  50.5 8.9 %conditional.1 = (f32[170,1,680]{2,1,0:T(1,128)}, f32[170,1,680]{2,1,0:T(1,128)}, f32[1]{0:T(128)}, f32[1,170,680]{2,0,1:T(1,128)}) conditional(s32[]{:T(128)} %clamp.3, (f32[2]{0:T(128)S(1)}, f32[176,320]{1,0:T(8,128)S(1)}, bf16[448,128]{1,0:T(8,128)(2,1)S(1)}, bf16[448,128]{1,0:T(8,128)(2,1)S(1)}, f32[170,320]{1,0:T(8,128)S(1)}, ...), branch_computations={%region_0.1_spmd, %region_1.2_spmd, %region_2.3_spmd} | conditional | bytes 3773936 | solution.py:549
  50.7 1.9 %collective-permute-start.4 = (bf16[528,128]{1,0:T(8,128)(2,1)S(1)}, bf16[528,128]{1,0:T(8,128)(2,1)S(1)}, u32[]{:S(2)}, u32[]{:S(2)}) collective-permute-start(bf16[528,128]{1,0:T(8,128)(2,1)S(1)} %get-tuple-element.134), channel_id=1, source_target_pairs={{0,16},{4,20},{8,24},{12,28},{16,0},{20,4},{24,8},{28,12},{1,17},{... | collective-permute-start | bytes 405512 | tf_op jit(solution)/shard_map/cond/branch_2_fun/ppermute | solution.py:389
  52.7 0.9 %adam.6 = (f32[176,320]{1,0:T(8,128)S(1)}, f32[176,320]{1,0:T(8,128)S(1)}, bf16[448,128]{1,0:T(8,128)(2,1)S(1)}) custom-call(f32[2]{0:T(128)S(1)} %get-tuple-element.122.scales_ref, f32[176,320]{1,0:T(8,128)S(1)} %get-tuple-element.123.own_ref, bf16[448,128]{1,0:T(8,128)(2,1)S(1)} %get-tuple-element.124.refs_0_, ...), custom_call_target="tpu_custom_call" | custom-call | bytes 435200 | tf_op jit(solution)/shard_map/cond/branch_2_fun/adam/pallas_call | solution.py:371
  53.6 0.2 collective-permute-start.5
  53.8 1.6 %moments.5 = (f32[170,1,680]{2,1,0:T(1,128)}, f32[170,1,680]{2,1,0:T(1,128)}) custom-call(f32[170,1,680]{2,1,0:T(1,128)S(1)} %get-tuple-element.119.first_ref, f32[170,1,680]{2,1,0:T(1,128)S(1)} %get-tuple-element.120.second_ref, f32[176,360]{1,0:T(8,128)S(1)} %get-tuple-element.121.refs_0_, f32[176,320]{1,0:T(8,128)S(1)} %get-tuple-element.129.refs_1_), custom_call_target="tpu_custom_call" | custom-call | bytes 924800 | tf_op jit(solution)/shard_map/cond/branch_2_fun/moments/pallas_call | solution.py:371
  55.4 0.4 collective-permute-done.4.other_ref
  55.8 1.3 %half_average.5 = (f32[176,360]{1,0:T(8,128)S(1)}, f32[1]{0:T(128)}) custom-call(f32[1]{0:T(128)} %get-tuple-element.132.push_ref, f32[176,360]{1,0:T(8,128)S(1)} %get-tuple-element.133.moved_ref, bf16[528,128]{1,0:T(8,128)(2,1)S(1)} %collective-permute-done.4.other_ref), custom_call_target="tpu_custom_call" | custom-call | bytes 489600 | tf_op jit(solution)/shard_map/cond/branch_2_fun/half_average/pallas_call | solution.py:371
  57.1 1.3 %collective-permute-done.5.other_ref = bf16[448,128]{1,0:T(8,128)(2,1)S(1)} collective-permute-done((bf16[448,128]{1,0:T(8,128)(2,1)S(1)}, bf16[448,128]{1,0:T(8,128)(2,1)S(1)}, u32[]{:S(2)}, u32[]{:S(2)}) %collective-permute-start.5) | collective-permute-done | bytes 114720 | tf_op jit(solution)/shard_map/cond/branch_2_fun/ppermute | solution.py:389
  58.5 1.0 %average.5 = f32[170,1,680]{2,1,0:T(1,128)} custom-call(f32[176,360]{1,0:T(8,128)S(1)} %get-tuple-element.136.mean_ref, f32[176,320]{1,0:T(8,128)S(1)} %get-tuple-element.137.moved_ref, bf16[448,128]{1,0:T(8,128)(2,1)S(1)} %collective-permute-done.5.other_ref), custom_call_target="tpu_custom_call" | custom-call | bytes 924800 | tf_op jit(solution)/shard_map/cond/branch_2_fun/average/pallas_call | solution.py:371
  (3 shorter events, 0.1 us)
Async XLA Ops:
  1.3 1.0 %copy-start = (f32[1,170,680]{2,0,1:T(1,128)S(1)}, f32[1,170,680]{2,0,1:T(1,128)}, u32[]{:S(2)}) copy-start(f32[1,170,680]{2,0,1:T(1,128)} %param.14) | copy-start | bytes 1387204
  2.6 13.9 %collective-permute-start.7 = (bf16[528,128]{1,0:T(8,128)(2,1)S(1)}, bf16[528,128]{1,0:T(8,128)(2,1)S(1)}, u32[]{:S(2)}, u32[]{:S(2)}) collective-permute-start(bf16[528,128]{1,0:T(8,128)(2,1)S(1)} %get-tuple-element.182.refs_0_), channel_id=1, source_target_pairs={{0,2},{1,3},{2,0},{3,1},{4,6},{5,7},{6,4},{7,5},{8,10},{9,11},{10,... | collective-permute-start | bytes 405512 | tf_op jit(solution)/shard_map/ppermute | solution.py:393
  6.7 12.6 %collective-permute-start.10 = (bf16[448,128]{1,0:T(8,128)(2,1)S(1)}, bf16[448,128]{1,0:T(8,128)(2,1)S(1)}, u32[]{:S(2)}, u32[]{:S(2)}) collective-permute-start(bf16[448,128]{1,0:T(8,128)(2,1)S(1)} %get-tuple-element.186.refs_0_), channel_id=1, source_target_pairs={{0,2},{1,3},{2,0},{3,1},{4,6},{5,7},{6,4},{7,5},{8,10},{9,11},{10,... | collective-permute-start | bytes 344072 | tf_op jit(solution)/shard_map/ppermute | solution.py:393
  6.8 16.5 %collective-permute-start.6 = (bf16[528,128]{1,0:T(8,128)(2,1)S(1)}, bf16[528,128]{1,0:T(8,128)(2,1)S(1)}, u32[]{:S(2)}, u32[]{:S(2)}) collective-permute-start(bf16[528,128]{1,0:T(8,128)(2,1)S(1)} %get-tuple-element.182.refs_0_), channel_id=1, source_target_pairs={{0,1},{1,0},{2,3},{3,2},{4,5},{5,4},{6,7},{7,6},{8,9},{9,8},{10,11... | collective-permute-start | bytes 405512 | tf_op jit(solution)/shard_map/ppermute | solution.py:393
  16.5 6.9 %collective-permute-start.8 = (bf16[528,128]{1,0:T(8,128)(2,1)S(1)}, bf16[528,128]{1,0:T(8,128)(2,1)S(1)}, u32[]{:S(2)}, u32[]{:S(2)}) collective-permute-start(bf16[528,128]{1,0:T(8,128)(2,1)S(1)} %collective-permute-done.7.refs_2_), channel_id=1, source_target_pairs={{0,1},{1,0},{2,3},{3,2},{4,5},{5,4},{6,7},{7,6},{8,9},{9,8},{10,11... | collective-permute-start | bytes 405512 | tf_op jit(solution)/shard_map/ppermute | solution.py:393
  16.5 11.4 %collective-permute-start.9 = (bf16[448,128]{1,0:T(8,128)(2,1)S(1)}, bf16[448,128]{1,0:T(8,128)(2,1)S(1)}, u32[]{:S(2)}, u32[]{:S(2)}) collective-permute-start(bf16[448,128]{1,0:T(8,128)(2,1)S(1)} %get-tuple-element.186.refs_0_), channel_id=1, source_target_pairs={{0,1},{1,0},{2,3},{3,2},{4,5},{5,4},{6,7},{7,6},{8,9},{9,8},{10,11... | collective-permute-start | bytes 344072 | tf_op jit(solution)/shard_map/ppermute | solution.py:393
  19.3 0.7 %copy-start.1 = (bf16[2,680]{1,0:T(2,128)(2,1)S(1)}, bf16[2,680]{1,0:T(2,128)(2,1)}, u32[]{:S(2)}) copy-start(bf16[2,680]{1,0:T(2,128)(2,1)} %shift_ref.1) | copy-start | bytes 8164
  19.3 8.6 %collective-permute-start.11 = (bf16[448,128]{1,0:T(8,128)(2,1)S(1)}, bf16[448,128]{1,0:T(8,128)(2,1)S(1)}, u32[]{:S(2)}, u32[]{:S(2)}) collective-permute-start(bf16[448,128]{1,0:T(8,128)(2,1)S(1)} %collective-permute-done.10.refs_2_), channel_id=1, source_target_pairs={{0,1},{1,0},{2,3},{3,2},{4,5},{5,4},{6,7},{7,6},{8,9},{9,8},{10,11... | collective-permute-start | bytes 344072 | tf_op jit(solution)/shard_map/ppermute | solution.py:393
  26.3 6.7 %collective-permute-start.16 = (bf16[528,128]{1,0:T(8,128)(2,1)S(1)}, bf16[528,128]{1,0:T(8,128)(2,1)S(1)}, u32[]{:S(2)}, u32[]{:S(2)}) collective-permute-start(bf16[528,128]{1,0:T(8,128)(2,1)S(1)} %get-tuple-element.200), channel_id=1, source_target_pairs={{0,1},{1,0},{2,3},{3,2},{4,5},{5,4},{6,7},{7,6},{8,9},{9,8},{10,11... | collective-permute-start | bytes 405512 | tf_op jit(solution)/shard_map/ppermute | solution.py:393
  30.9 7.7 %collective-permute-start.13 = (bf16[448,128]{1,0:T(8,128)(2,1)S(1)}, bf16[448,128]{1,0:T(8,128)(2,1)S(1)}, u32[]{:S(2)}, u32[]{:S(2)}) collective-permute-start(bf16[448,128]{1,0:T(8,128)(2,1)S(1)} %get-tuple-element.194), channel_id=1, source_target_pairs={{0,1},{1,0},{2,3},{3,2},{4,5},{5,4},{6,7},{7,6},{8,9},{9,8},{10,11... | collective-permute-start | bytes 344072 | tf_op jit(solution)/shard_map/ppermute | solution.py:393
  31.4 16.6 %collective-permute-start.15 = (bf16[528,128]{1,0:T(8,128)(2,1)S(1)}, bf16[528,128]{1,0:T(8,128)(2,1)S(1)}, u32[]{:S(2)}, u32[]{:S(2)}) collective-permute-start(bf16[528,128]{1,0:T(8,128)(2,1)S(1)} %get-tuple-element.198), channel_id=1, source_target_pairs={{0,1},{1,0},{2,3},{3,2},{4,5},{5,4},{6,7},{7,6},{8,9},{9,8},{10,11... | collective-permute-start | bytes 405512 | tf_op jit(solution)/shard_map/ppermute | solution.py:393
  33.0 15.0 %collective-permute-start.17 = (bf16[528,128]{1,0:T(8,128)(2,1)S(1)}, bf16[528,128]{1,0:T(8,128)(2,1)S(1)}, u32[]{:S(2)}, u32[]{:S(2)}) collective-permute-start(bf16[528,128]{1,0:T(8,128)(2,1)S(1)} %merge.3), channel_id=1, source_target_pairs={{0,2},{1,3},{2,0},{3,1},{4,6},{5,7},{6,4},{7,5},{8,10},{9,11},{10,... | collective-permute-start | bytes 405512 | tf_op jit(solution)/shard_map/ppermute | solution.py:393
  34.9 15.6 %collective-permute-start.12 = (bf16[448,128]{1,0:T(8,128)(2,1)S(1)}, bf16[448,128]{1,0:T(8,128)(2,1)S(1)}, u32[]{:S(2)}, u32[]{:S(2)}) collective-permute-start(bf16[448,128]{1,0:T(8,128)(2,1)S(1)} %get-tuple-element.192), channel_id=1, source_target_pairs={{0,1},{1,0},{2,3},{3,2},{4,5},{5,4},{6,7},{7,6},{8,9},{9,8},{10,11... | collective-permute-start | bytes 344072 | tf_op jit(solution)/shard_map/ppermute | solution.py:393
  38.6 11.8 %collective-permute-start.14 = (bf16[448,128]{1,0:T(8,128)(2,1)S(1)}, bf16[448,128]{1,0:T(8,128)(2,1)S(1)}, u32[]{:S(2)}, u32[]{:S(2)}) collective-permute-start(bf16[448,128]{1,0:T(8,128)(2,1)S(1)} %merge.2), channel_id=1, source_target_pairs={{0,2},{1,3},{2,0},{3,1},{4,6},{5,7},{6,4},{7,5},{8,10},{9,11},{10,... | collective-permute-start | bytes 344072 | tf_op jit(solution)/shard_map/ppermute | solution.py:393
  47.9 2.6 %copy-start.2 = (f32[1,170,680]{2,0,1:T(1,128)S(1)}, f32[1,170,680]{2,0,1:T(1,128)}, u32[]{:S(2)}) copy-start(f32[1,170,680]{2,0,1:T(1,128)} %param.15) | copy-start | bytes 1387204
  48.0 2.6 %copy-start.3 = (f32[1,170,680]{2,0,1:T(1,128)S(1)}, f32[1,170,680]{2,0,1:T(1,128)}, u32[]{:S(2)}) copy-start(f32[1,170,680]{2,0,1:T(1,128)} %param.16) | copy-start | bytes 1387204
  50.7 5.1 %collective-permute-start.4 = (bf16[528,128]{1,0:T(8,128)(2,1)S(1)}, bf16[528,128]{1,0:T(8,128)(2,1)S(1)}, u32[]{:S(2)}, u32[]{:S(2)}) collective-permute-start(bf16[528,128]{1,0:T(8,128)(2,1)S(1)} %get-tuple-element.134), channel_id=1, source_target_pairs={{0,16},{4,20},{8,24},{12,28},{16,0},{20,4},{24,8},{28,12},{1,17},{... | collective-permute-start | bytes 405512 | tf_op jit(solution)/shard_map/cond/branch_2_fun/ppermute | solution.py:389
  53.6 4.9 %collective-permute-start.5 = (bf16[448,128]{1,0:T(8,128)(2,1)S(1)}, bf16[448,128]{1,0:T(8,128)(2,1)S(1)}, u32[]{:S(2)}, u32[]{:S(2)}) collective-permute-start(bf16[448,128]{1,0:T(8,128)(2,1)S(1)} %get-tuple-element.138), channel_id=1, source_target_pairs={{0,16},{4,20},{8,24},{12,28},{16,0},{20,4},{24,8},{28,12},{1,17},{... | collective-permute-start | bytes 344072 | tf_op jit(solution)/shard_map/cond/branch_2_fun/ppermute | solution.py:389

commit v8 on v7

--- a/solution.py
+++ b/solution.py
@@ -125,13 +125,11 @@
     return gate * (1.0 + values * (1.0 - gate))
 
 
-def cast_kernel(packs, push_ref, params_ref, *refs):
-    out_refs, rows_ref = refs[:-1], refs[-1]
-    rows = params_ref.shape[0]
-    rows_ref[rows // 8 * 8 :, :] = jnp.zeros((rows_ref.shape[0] - rows // 8 * 8, rows_ref.shape[1]), jnp.float32)
-    rows_ref[:rows, :] = params_ref[:, 0, :] / push_ref[0]
-    for pack, out_ref in zip(packs, out_refs):
-        pack.write(out_ref, rows_ref[:, pack.start : pack.stop])
+def cast_kernel(pack, push_ref, params_ref, token_ref, out_ref, rows_ref):
+    rows = pack.rows
+    rows_ref[rows // 8 * 8 :, :] = jnp.zeros((pack.deep - rows // 8 * 8, pack.columns), jnp.float32)
+    rows_ref[:rows, :] = params_ref[:, 0, pack.start : pack.stop] / push_ref[0]
+    pack.write(out_ref, rows_ref[...])
 
 
 def norm_in_kernel(shards, packs, me_ref, scales_ref, shift_ref, x_hbm, out_grad_hbm, *refs):
@@ -274,65 +272,48 @@
         copy.wait()
 
 
-def adam_step(shards, pack, scales_ref, own_ref, other_refs, blocks, grad_ref, moved_ref):
-    rows = pack.rows
-    total = own_ref[...]
-    for other_ref in other_refs:
-        total = total + pack.read(other_ref)
-    grad_ref[...] = total / shards
-    grad = grad_ref[:rows, :]
-    params, first, second = blocks()
-    first_new = BETA_ONE * first + (1.0 - BETA_ONE) * grad
-    second_new = BETA_TWO * second + (1.0 - BETA_TWO) * grad * grad
-    update = (scales_ref[0] * first_new) / (jnp.sqrt(second_new * scales_ref[1]) + ADAM_EPS)
-    moved_ref[rows // 8 * 8 :, :] = jnp.zeros((pack.deep - rows // 8 * 8, pack.columns), jnp.float32)
-    moved_ref[:rows, :] = params - update
-
-
-def merge_kernel(one_ref, other_ref, out_ref):
+def merge_kernel(one_ref, other_ref, direct_ref, out_ref, direct_out_ref):
     out_ref[...] = (one_ref[...].astype(jnp.float32) + other_ref[...].astype(jnp.float32)).astype(out_ref.dtype)
-
-
-def fetch(hbm_refs, row_refs, sems):
+    direct_out_ref[...] = direct_ref[...]
+
+
+def cut_kernel(packs, *refs):
+    count = 3 * len(packs)
+    hbm_refs, out_refs = refs[:3], refs[4 : 4 + count]
+    row_refs, block_refs, sems = refs[4 + count : 7 + count], refs[7 + count : -1], refs[-1]
     copies = [
         pltpu.make_async_copy(source, target, sems.at[i])
         for i, (source, target) in enumerate(zip(hbm_refs, row_refs))
     ]
     for copy in copies:
         copy.start()
-    return copies
-
-
-def first_adam_kernel(shards, count, pack, scales_ref, push_ref, own_ref, *refs):
+    out_copies = []
+    for i, row_ref in enumerate(row_refs):
+        copies[i].wait()
+        for index, pack in enumerate(packs):
+            place = 3 * index + i
+            block_refs[place][...] = row_ref[:, 0, pack.start : pack.stop]
+            out_copies.append(pltpu.make_async_copy(block_refs[place], out_refs[place], sems.at[3 + place]))
+            out_copies[-1].start()
+    for copy in out_copies:
+        copy.wait()
+
+
+def adam_kernel(count, pack, spare_value, scales_ref, push_ref, own_ref, *refs):
     other_refs, refs = refs[:count], refs[count:]
-    hbm_refs, token_ref, (grad_ref, moved_ref, sent_ref) = refs[:3], refs[3], refs[4:7]
-    row_refs, sems = refs[7:10], refs[10]
-    copies = fetch(hbm_refs, row_refs, sems)
-
-    def blocks():
-        for copy in copies:
-            copy.wait()
-        return [row_ref[:, 0, pack.start : pack.stop] for row_ref in row_refs]
-
-    adam_step(shards, pack, scales_ref, own_ref, other_refs, blocks, grad_ref, moved_ref)
-    moved = moved_ref[...]
-    spare = lax.broadcasted_iota(jnp.int32, moved.shape, 0) == pack.rows
-    pack.write(sent_ref, jnp.where(spare, push_ref[0], moved))
-
-
-def cut_kernel(pack, *refs):
-    hbm_refs, out_refs, row_refs, sems = refs[:3], refs[4:7], refs[7:10], refs[10]
-    for copy, row_ref, out_ref in zip(fetch(hbm_refs, row_refs, sems), row_refs, out_refs):
-        copy.wait()
-        out_ref[...] = row_ref[:, 0, pack.start : pack.stop]
-
-
-def second_adam_kernel(shards, count, pack, scales_ref, own_ref, *refs):
-    other_refs, refs = refs[:count], refs[count:]
-    block_refs, (grad_ref, moved_ref, sent_ref) = refs[:3], refs[3:]
-    adam_step(
-        shards, pack, scales_ref, own_ref, other_refs, lambda: [ref[...] for ref in block_refs], grad_ref, moved_ref
-    )
+    (params_ref, first_ref, second_ref), (grad_ref, moved_ref, sent_ref) = refs[:3], refs[-3:]
+    rows = pack.rows
+    total = own_ref[...]
+    for other_ref in other_refs:
+        total = total + pack.read(other_ref)
+    grad_ref[...] = total * scales_ref[2]
+    grad = grad_ref[:rows, :]
+    first_new = BETA_ONE * first_ref[...] + (1.0 - BETA_ONE) * grad
+    second_new = BETA_TWO * second_ref[...] + (1.0 - BETA_TWO) * grad * grad
+    update = (scales_ref[0] * first_new) / (jnp.sqrt(second_new * scales_ref[1]) + ADAM_EPS)
+    value = push_ref[0] if spare_value else 0.0
+    moved_ref[rows // 8 * 8 :, :] = jnp.full((pack.deep - rows // 8 * 8, pack.columns), value, jnp.float32)
+    moved_ref[:rows, :] = params_ref[...] - update
     pack.write(sent_ref, moved_ref[...])
 
 
@@ -414,13 +395,9 @@
         if slot == bit:
             arrived.append(other)
         else:
-            held[slot ^ bit] = call(
-                merge_kernel,
-                "merge",
-                jax.ShapeDtypeStruct(other.shape, other.dtype),
-                [BLOCKS] * 2,
-                (held[slot ^ bit], other),
-                elements=other.size,
+            shape = jax.ShapeDtypeStruct(other.shape, other.dtype)
+            held[slot ^ bit], held[bit] = call(
+                merge_kernel, "merge", (shape,) * 2, [BLOCKS] * 3, (held[slot ^ bit], other, held[bit])
             )
     return arrived
 
@@ -443,22 +420,27 @@
     params, first_moment, second_moment = (
         jnp.transpose(array, (1, 0, 2)) for array in (params, first_moment, second_moment)
     )
-    shard_list = call(
-        functools.partial(cast_kernel, packs),
-        "cast",
-        tuple(pack.payload() for pack in packs),
-        [SCALARS, BLOCKS],
-        (push_weight, params),
-        scratch=[pltpu.VMEM((deep, channels), jnp.float32)],
-        elements=rows * channels,
-    )
-    weights = [gathered(piece, shards) for piece in shard_list]
+    def shards_of(pack, token):
+        piece = call(
+            functools.partial(cast_kernel, pack),
+            "cast",
+            pack.payload(),
+            [SCALARS, BLOCKS, TOKEN],
+            (push_weight, params, token),
+            scratch=[pltpu.VMEM((deep, pack.columns), jnp.float32)],
+            elements=rows * pack.columns,
+        )
+        return gathered(piece, shards)
 
     level_count = lax.axis_size("replica").bit_length() - 1
     distance_bits = step[0] % level_count
     step_count = (step[0] + 1).astype(jnp.float32)
     scales = jnp.stack(
-        [LEARN_RATE / (1.0 - jnp.power(BETA_ONE, step_count)), 1.0 / (1.0 - jnp.power(BETA_TWO, step_count))]
+        [
+            LEARN_RATE / (1.0 - jnp.power(BETA_ONE, step_count)),
+            1.0 / (1.0 - jnp.power(BETA_TWO, step_count)),
+            jnp.float32(1.0 / shards),
+        ]
     )
 
     activation, mean_in, inverse_in, same_group, *pieces = call(
@@ -482,8 +464,22 @@
         elements=tokens * channels,
     )
 
+    weights = [shards_of(pack, token) for pack, token in zip(packs, (push_weight, mean_in))]
+    columns = [pack.columns for pack in packs for _ in range(3)]
+    blocks = call(
+        functools.partial(cut_kernel, packs),
+        "cut",
+        tuple(pltpu.HBM((rows, width), jnp.float32) for width in columns),
+        [IN_HBM] * 3 + [TOKEN],
+        (stay(params), stay(first_moment), stay(second_moment), mean_in),
+        scratch=[pltpu.VMEM(params.shape, jnp.float32)] * 3
+        + [pltpu.VMEM((rows, width), jnp.float32) for width in columns]
+        + [pltpu.SemaphoreType.DMA((3 + len(columns),))],
+        out_specs=(IN_HBM,) * len(columns),
+        elements=rows * channels,
+    )
     hidden_grads, full_weights, owns, arrived = [], [], [], []
-    token = mean_in
+    token = blocks[-1]
     shifts, out_grads = pieces[: len(packs)], pieces[len(packs) :]
     for pack, shard_list, shift, out_grad_piece in zip(packs, weights, shifts, out_grads):
         grad_hidden, full_weight, own, *sends = call(
@@ -552,37 +548,22 @@
         me, mean_in, inverse_in, same_group, block_input, *hidden_grads, *full_weights
     )
     early, late = packs
-    arrays = [stay(params), stay(first_moment), stay(second_moment)]
-    array_scratch = [pltpu.VMEM(params.shape, jnp.float32)] * 3 + [pltpu.SemaphoreType.DMA((3,))]
-    late_blocks = call(
-        functools.partial(cut_kernel, late),
-        "cut",
-        (jax.ShapeDtypeStruct((rows, late.columns), jnp.float32),) * 3,
-        [IN_HBM] * 3 + [TOKEN],
-        (*arrays, token),
-        scratch=array_scratch,
-        elements=rows * late.columns,
-    )
-    grad_a, moved_a, sent_a = call(
-        functools.partial(first_adam_kernel, shards, len(arrived[0]), early),
-        "adam",
-        (early.block(), early.block(), early.payload()),
-        [SCALARS] * 2 + [BLOCKS] * (1 + len(arrived[0])) + [IN_HBM] * 3 + [TOKEN],
-        (scales, push_weight, owns[0], *arrived[0], *arrays, token),
-        scratch=array_scratch,
-        elements=rows * early.columns,
-    )
+
+    def adam(pack, own, others, blocks):
+        return call(
+            functools.partial(adam_kernel, len(others), pack, pack is early),
+            "adam",
+            (pack.block(), pack.block(), pack.payload()),
+            [SCALARS] * 2 + [BLOCKS] * (4 + len(others)),
+            (scales, push_weight, own, *others, *blocks),
+            elements=rows * pack.columns,
+        )
+
+    grad_a, moved_a, sent_a = adam(early, owns[0], arrived[0], blocks[:3])
 
     def finish(move, sent, grad_a, moved_a, own, *operands):
         other_a = move(sent)
-        grad_b, moved_b, sent_b = call(
-            functools.partial(second_adam_kernel, shards, len(arrived[1]), late),
-            "adam",
-            (late.block(), late.block(), late.payload()),
-            [SCALARS] + [BLOCKS] * (4 + len(arrived[1])),
-            (scales, own, *operands),
-            elements=rows * late.columns,
-        )
+        grad_b, moved_b, sent_b = adam(late, own, operands[:-3], operands[-3:])
         other_b = move(sent_b)
         mean, weight = call(
             functools.partial(half_average_kernel, early),
@@ -606,7 +587,7 @@
         return (*moments(grad_a, grad_b), averaged, weight)
 
     first_new, second_new, averaged, new_weight = from_behind(
-        finish, sent_a, grad_a, moved_a, owns[1], *arrived[1], *late_blocks
+        finish, sent_a, grad_a, moved_a, owns[1], *arrived[1], *blocks[3:]
     )
     return (
         grad_input,

time: 59.9 us -> 58.4 us (0.975)
  waiting for transfers between devices: 11.8 us -> 7.76 us
  starting transfers between devices: 20 us -> 21.5 us
    ppermute x12, waiting for transfers between devices: 10.1 us -> 7.01 us  [exchanged(): lax.ppermute(block, axis, [(i, i ^ bit) for i in range(lax.axis_size(axis...]
    ppermute x12, starting transfers between devices: 17.9 us -> 20 us  [exchanged(): lax.ppermute(block, axis, [(i, i ^ bit) for i in range(lax.axis_size(axis...]
    ppermute x2, waiting for transfers between devices: 1.74 us -> 0.75 us  [moved_on(): lax.ppermute(block, axis, [(i, (i + distance) % size) for i in range(size)])]
    ppermute x2, starting transfers between devices: 2.16 us -> 1.51 us  [moved_on(): lax.ppermute(block, axis, [(i, (i + distance) % size) for i in range(size)])]
    pallas_call x13 -> x14, Pallas kernels: 23.6 us -> 24.1 us  [call(): pl.pallas_call(kernel, out_shape=outs, in_specs=specs, out_specs=out_spec...]
    unnamed x8 -> x22, local copies, waits for them, and re-layouts: 1.5 us -> 1.93 us
  transfers between devices with their start and end apart: 14 -> 14, of which waited for: 4 -> 5; matrix products, arithmetic and copies ran while one was open for 0% -> 0% of each run, Pallas kernels for 37% -> 40%
where the time goes in v8:
time: 58.4 us; the launch traced here: 58 us
  Pallas kernels  24.1 us (41%)
  starting transfers between devices  21.5 us (37%)
  waiting for transfers between devices  7.76 us (13%)
  between operations  2.46 us (4%)
  local copies, waits for them, and re-layouts  1.93 us (3%)
    pallas_call x14, Pallas kernels, call(): pl.pallas_call(kernel, out_shape=outs, in_specs=specs, out_specs=out_spec...  24.1 us
    ppermute x12, starting transfers between devices, exchanged(): lax.ppermute(block, axis, [(i, i ^ bit) for i in range(lax.axis_size(axis...  20 us
    ppermute x12, waiting for transfers between devices, exchanged(): lax.ppermute(block, axis, [(i, i ^ bit) for i in range(lax.axis_size(axis...  7.01 us
    unnamed x22, local copies, waits for them, and re-layouts  1.93 us
    ppermute x2, starting transfers between devices, moved_on(): lax.ppermute(block, axis, [(i, (i + distance) % size) for i in range(size)])  1.51 us
  transfers between devices with their start and end apart: 14, of which 5 were waited for; matrix products, arithmetic and copies ran while one was open for 0% of the time, Pallas kernels for 40%

profile of v8, /device:TPU:0, one launch (start us, length us, event | category | flops | bytes accessed | tf_op | source)
XLA Modules:
  0.0 58.0 jit_solution(11501489928064451615)
XLA Ops:
  1.3 0.0 copy-start
  1.3 1.0 %copy-done = f32[1,170,680]{2,0,1:T(1,128)S(1)} copy-done((f32[1,170,680]{2,0,1:T(1,128)S(1)}, f32[1,170,680]{2,0,1:T(1,128)}, u32[]{:S(2)}) %copy-start) | copy-done | bytes 462424
  2.3 0.1 cast.2.refs_0_
  2.4 4.1 %collective-permute-start.7 = (bf16[528,128]{1,0:T(8,128)(2,1)S(1)}, bf16[528,128]{1,0:T(8,128)(2,1)S(1)}, u32[]{:S(2)}, u32[]{:S(2)}) collective-permute-start(bf16[528,128]{1,0:T(8,128)(2,1)S(1)} %cast.2.refs_0_), channel_id=1, source_target_pairs={{0,2},{1,3},{2,0},{3,1},{4,6},{5,7},{6,4},{7,5},{8,10},{9,11},{10,... | collective-permute-start | bytes 405512 | tf_op jit(solution)/shard_map/ppermute | solution.py:374
  7.3 0.0 copy-start.5
  7.4 0.1 pad_maximum_fusion.scales_ref
  7.4 0.6 copy-done.5
  8.0 3.4 %norm_in.1 = (bf16[704,576]{1,0:T(8,128)(2,1)S(1)}, f32[2,680]{1,0:T(2,128)S(1)}, f32[2,680]{1,0:T(2,128)S(1)}, bf16[360,360]{1,0:T(8,128)(2,1)S(1)}, f32[2,360]...) custom-call(s32[1]{0:T(128)} %bitcast.3.me_ref, ...), custom_call_target="tpu_custom_call" | custom-call | bytes 3133440 | tf_op jit(solution)/shard_map/norm_in/pallas_call | solution.py:352
  11.4 0.2 cast.3.refs_0_
  11.6 0.1 collective-permute-start.10
  11.7 1.9 %collective-permute-start.6 = (bf16[528,128]{1,0:T(8,128)(2,1)S(1)}, bf16[528,128]{1,0:T(8,128)(2,1)S(1)}, u32[]{:S(2)}, u32[]{:S(2)}) collective-permute-start(bf16[528,128]{1,0:T(8,128)(2,1)S(1)} %cast.2.refs_0_), channel_id=1, source_target_pairs={{0,1},{1,0},{2,3},{3,2},{4,5},{5,4},{6,7},{7,6},{8,9},{9,8},{10,11... | collective-permute-start | bytes 405512 | tf_op jit(solution)/shard_map/ppermute | solution.py:374
  13.6 0.0 collective-permute-done.7.refs_2_
  13.6 2.0 %collective-permute-start.8 = (bf16[528,128]{1,0:T(8,128)(2,1)S(1)}, bf16[528,128]{1,0:T(8,128)(2,1)S(1)}, u32[]{:S(2)}, u32[]{:S(2)}) collective-permute-start(bf16[528,128]{1,0:T(8,128)(2,1)S(1)} %collective-permute-done.7.refs_2_), channel_id=1, source_target_pairs={{0,1},{1,0},{2,3},{3,2},{4,5},{5,4},{6,7},{7,6},{8,9},{9,8},{10,11... | collective-permute-start | bytes 405512 | tf_op jit(solution)/shard_map/ppermute | solution.py:374
  15.6 0.1 collective-permute-start.9
  15.6 4.1 %collective-permute-done.10.refs_2_ = bf16[448,128]{1,0:T(8,128)(2,1)S(1)} collective-permute-done((bf16[448,128]{1,0:T(8,128)(2,1)S(1)}, bf16[448,128]{1,0:T(8,128)(2,1)S(1)}, u32[]{:S(2)}, u32[]{:S(2)}) %collective-permute-start.10) | collective-permute-done | bytes 114720 | tf_op jit(solution)/shard_map/ppermute | solution.py:374
  19.7 0.5 collective-permute-start.11
  20.2 2.4 %cut.1 = (f32[170,360]{1,0:T(8,128)}, f32[170,360]{1,0:T(8,128)}, f32[170,360]{1,0:T(8,128)}, f32[170,320]{1,0:T(8,128)}, f32[170,320]{1,0:T(8,128)}, /*index=5*/f32[170,320]{1,0:T(8,128)}) custom-call(f32[170,1,680]{2,1,0:T(1,128)} %bitcast.10, f32[170,1,680]{2,1,0:T(1,128)} %bitcast.13, f32[170,1,680]{2,1,0:T(1,128)} %bitcast.17, ...), custom_call_target="tpu_custom_call" | custom-call | bytes 924800 | tf_op jit(solution)/shard_map/cut/pallas_call | solution.py:352
  22.7 0.0 collective-permute-done.6.refs_1_
  22.7 0.4 collective-permute-done.8.refs_3_
  23.1 2.9 %mix.2 = (bf16[576,360]{1,0:T(8,128)(2,1)}, bf16[704,360]{1,0:T(8,128)(2,1)}, f32[176,360]{1,0:T(8,128)S(1)}, bf16[528,128]{1,0:T(8,128)(2,1)S(1)}, bf16[528,128...) custom-call(bf16[704,576]{1,0:T(8,128)(2,1)S(1)} %get-tuple-element.184.act_ref, ...), custom_call_target="tpu_custom_call" | custom-call | flops 564019200 | bytes 1658880 | tf_op jit(solution)/shard_map/mix/pallas_call | solution.py:352
  26.1 1.1 %collective-permute-start.15 = (bf16[528,128]{1,0:T(8,128)(2,1)S(1)}, bf16[528,128]{1,0:T(8,128)(2,1)S(1)}, u32[]{:S(2)}, u32[]{:S(2)}) collective-permute-start(bf16[528,128]{1,0:T(8,128)(2,1)S(1)} %get-tuple-element.204), channel_id=1, source_target_pairs={{0,1},{1,0},{2,3},{3,2},{4,5},{5,4},{6,7},{7,6},{8,9},{9,8},{10,11... | collective-permute-start | bytes 405512 | tf_op jit(solution)/shard_map/ppermute | solution.py:374
  27.2 0.0 collective-permute-done.9.refs_1_
  27.2 0.0 collective-permute-done.11.refs_3_
  27.2 3.0 %mix.3 = (bf16[576,320]{1,0:T(8,128)(2,1)}, bf16[704,320]{1,0:T(8,128)(2,1)}, f32[176,320]{1,0:T(8,128)S(1)}, bf16[448,128]{1,0:T(8,128)(2,1)S(1)}, bf16[448,128...) custom-call(bf16[704,576]{1,0:T(8,128)(2,1)S(1)} %get-tuple-element.184.act_ref, ...), custom_call_target="tpu_custom_call" | custom-call | flops 501350400 | bytes 1474560 | tf_op jit(solution)/shard_map/mix/pallas_call | solution.py:352
  30.2 1.0 %collective-permute-start.12 = (bf16[448,128]{1,0:T(8,128)(2,1)S(1)}, bf16[448,128]{1,0:T(8,128)(2,1)S(1)}, u32[]{:S(2)}, u32[]{:S(2)}) collective-permute-start(bf16[448,128]{1,0:T(8,128)(2,1)S(1)} %get-tuple-element.197), channel_id=1, source_target_pairs={{0,1},{1,0},{2,3},{3,2},{4,5},{5,4},{6,7},{7,6},{8,9},{9,8},{10,11... | collective-permute-start | bytes 344072 | tf_op jit(solution)/shard_map/ppermute | solution.py:374
  31.2 0.0 collective-permute-done.15.other_ref
  31.3 1.1 %collective-permute-start.16 = (bf16[528,128]{1,0:T(8,128)(2,1)S(1)}, bf16[528,128]{1,0:T(8,128)(2,1)S(1)}, u32[]{:S(2)}, u32[]{:S(2)}) collective-permute-start(bf16[528,128]{1,0:T(8,128)(2,1)S(1)} %get-tuple-element.206), channel_id=1, source_target_pairs={{0,1},{1,0},{2,3},{3,2},{4,5},{5,4},{6,7},{7,6},{8,9},{9,8},{10,11... | collective-permute-start | bytes 405512 | tf_op jit(solution)/shard_map/ppermute | solution.py:374
  32.4 3.5 %collective-permute-start.17 = (bf16[528,128]{1,0:T(8,128)(2,1)S(1)}, bf16[528,128]{1,0:T(8,128)(2,1)S(1)}, u32[]{:S(2)}, u32[]{:S(2)}) collective-permute-start(bf16[528,128]{1,0:T(8,128)(2,1)S(1)} %get-tuple-element.207), channel_id=1, source_target_pairs={{0,2},{1,3},{2,0},{3,1},{4,6},{5,7},{6,4},{7,5},{8,10},{9,11},{10,... | collective-permute-start | bytes 405512 | tf_op jit(solution)/shard_map/ppermute | solution.py:374
  35.9 2.5 %collective-permute-done.12.other_ref = bf16[448,128]{1,0:T(8,128)(2,1)S(1)} collective-permute-done((bf16[448,128]{1,0:T(8,128)(2,1)S(1)}, bf16[448,128]{1,0:T(8,128)(2,1)S(1)}, u32[]{:S(2)}, u32[]{:S(2)}) %collective-permute-start.12) | collective-permute-done | bytes 114720 | tf_op jit(solution)/shard_map/ppermute | solution.py:374
  38.4 0.1 collective-permute-start.13
  38.5 4.5 %collective-permute-start.14 = (bf16[448,128]{1,0:T(8,128)(2,1)S(1)}, bf16[448,128]{1,0:T(8,128)(2,1)}, u32[]{:S(2)}, u32[]{:S(2)}) collective-permute-start(bf16[448,128]{1,0:T(8,128)(2,1)S(1)} %get-tuple-element.200), channel_id=1, source_target_pairs={{0,2},{1,3},{2,0},{3,1},{4,6},{5,7},{6,4},{7,5},{8,10},{9,11},{10,... | collective-permute-start | bytes 344072 | tf_op jit(solution)/shard_map/ppermute | solution.py:374
  43.0 5.2 %input_grad.1 = bf16[2,288,680]{2,1,0:T(8,128)(2,1)} custom-call(s32[1]{0:T(128)} %bitcast.3.me_ref, f32[2,680]{1,0:T(2,128)S(1)} %get-tuple-element.181.refs_3_.token_ref.mean_ref, f32[2,680]{1,0:T(2,128)S(1)} %get-tuple-element.182.inverse_ref, bf16[360,360]{1,0:T(8,128)(2,1)S(1)} %get-tuple-element.183.same_group_ref, bf16[2,288,680]{2,1,0:T(8,128)(2,1)} %x_hbm.3, ...), custom_call_target="tpu_custom_call" | custom-call | flops 532684800 | bytes 3133440 | tf_op jit(solution)/shard_map/input_grad/pallas_call | solution.py:352
  48.2 0.0 collective-permute-done.16.refs_0_
  48.3 0.0 copy-start.6
  48.3 0.0 copy-start.7
  48.3 0.9 %adam.7 = (f32[176,360]{1,0:T(8,128)S(1)}, f32[176,360]{1,0:T(8,128)S(1)}, bf16[528,128]{1,0:T(8,128)(2,1)S(1)}) custom-call(f32[3]{0:T(128)S(1)} %pad_maximum_fusion.scales_ref, f32[1]{0:T(128)S(6)} %copy.25.push_ref.token_ref, f32[176,360]{1,0:T(8,128)S(1)} %get-tuple-element.191.refs_4_.own_ref, bf16[528,128]{1,0:T(8,128)(2,1)S(1)} %collective-permute-done.16.refs_0_, ...), custom_call_target="tpu_custom_call" | custom-call | bytes 489600 | tf_op jit(solution)/shard_map/adam/pallas_call | solution.py:352
  49.2 0.0 collective-permute-done.14
  49.2 0.1 copy-done.6
  49.3 0.2 copy-done.7
  49.5 0.1 copy-done.8
  49.5 8.3 %conditional.1 = (f32[170,1,680]{2,1,0:T(1,128)}, f32[170,1,680]{2,1,0:T(1,128)}, f32[1]{0:T(128)}, f32[1,170,680]{2,0,1:T(1,128)}) conditional(s32[]{:T(128)} %clamp.3, (f32[3]{0:T(128)S(1)}, f32[1]{0:T(128)}, f32[176,320]{1,0:T(8,128)S(1)}, bf16[448,128]{1,0:T(8,128)(2,1)}, bf16[448,128]{1,0:T(8,128)(2,1)}, ...), branch_computations={%region_0.1_spmd, %region_1.2_spmd, %region_2.3_spmd} | conditional | bytes 3773936 | solution.py:545
  49.5 2.0 %adam.4 = (f32[176,320]{1,0:T(8,128)S(1)}, f32[176,320]{1,0:T(8,128)S(1)}, bf16[448,128]{1,0:T(8,128)(2,1)S(1)}) custom-call(f32[3]{0:T(128)S(1)} %get-tuple-element.82.scales_ref, f32[1]{0:T(128)} %get-tuple-element.83.push_ref, f32[176,320]{1,0:T(8,128)S(1)} %get-tuple-element.84.own_ref, bf16[448,128]{1,0:T(8,128)(2,1)} %get-tuple-element.85.refs_0_, ...), custom_call_target="tpu_custom_call" | custom-call | bytes 435200 | tf_op jit(solution)/shard_map/cond/branch_0_fun/adam/pallas_call | solution.py:352
  51.5 1.5 %collective-permute-start.1 = (bf16[448,128]{1,0:T(8,128)(2,1)S(1)}, bf16[448,128]{1,0:T(8,128)(2,1)S(1)}, u32[]{:S(2)}, u32[]{:S(2)}) collective-permute-start(bf16[448,128]{1,0:T(8,128)(2,1)S(1)} %get-tuple-element.98), channel_id=1, source_target_pairs={{0,4},{4,8},{8,12},{12,16},{16,20},{20,24},{24,28},{28,0},{1,5},{5... | collective-permute-start | bytes 344072 | tf_op jit(solution)/shard_map/cond/branch_0_fun/ppermute | solution.py:370
  53.0 1.6 %moments.3 = (f32[170,1,680]{2,1,0:T(1,128)}, f32[170,1,680]{2,1,0:T(1,128)}) custom-call(f32[170,1,680]{2,1,0:T(1,128)S(1)} %get-tuple-element.79.first_ref, f32[170,1,680]{2,1,0:T(1,128)S(1)} %get-tuple-element.80.second_ref, f32[176,360]{1,0:T(8,128)S(1)} %get-tuple-element.81.refs_0_, f32[176,320]{1,0:T(8,128)S(1)} %get-tuple-element.90.refs_1_), custom_call_target="tpu_custom_call" | custom-call | bytes 924800 | tf_op jit(solution)/shard_map/cond/branch_0_fun/moments/pallas_call | solution.py:352
  54.6 0.3 collective-permute-done.other_ref
  54.9 1.3 %half_average.3 = (f32[176,360]{1,0:T(8,128)S(1)}, f32[1]{0:T(128)}) custom-call(f32[1]{0:T(128)} %get-tuple-element.83.push_ref, f32[176,360]{1,0:T(8,128)S(1)} %get-tuple-element.93.moved_ref, bf16[528,128]{1,0:T(8,128)(2,1)S(1)} %collective-permute-done.other_ref), custom_call_target="tpu_custom_call" | custom-call | bytes 489600 | tf_op jit(solution)/shard_map/cond/branch_0_fun/half_average/pallas_call | solution.py:352
  56.2 0.5 collective-permute-done.1.other_ref
  56.7 1.0 %average.3 = f32[170,1,680]{2,1,0:T(1,128)} custom-call(f32[176,360]{1,0:T(8,128)S(1)} %get-tuple-element.96.mean_ref, f32[176,320]{1,0:T(8,128)S(1)} %get-tuple-element.97.moved_ref, bf16[448,128]{1,0:T(8,128)(2,1)S(1)} %collective-permute-done.1.other_ref), custom_call_target="tpu_custom_call" | custom-call | bytes 924800 | tf_op jit(solution)/shard_map/cond/branch_0_fun/average/pallas_call | solution.py:352
  (18 shorter events, 0.1 us)
Async XLA Ops:
  1.3 1.0 %copy-start = (f32[1,170,680]{2,0,1:T(1,128)S(1)}, f32[1,170,680]{2,0,1:T(1,128)}, u32[]{:S(2)}) copy-start(f32[1,170,680]{2,0,1:T(1,128)} %param.14) | copy-start | bytes 1387204
  2.4 11.1 %collective-permute-start.7 = (bf16[528,128]{1,0:T(8,128)(2,1)S(1)}, bf16[528,128]{1,0:T(8,128)(2,1)S(1)}, u32[]{:S(2)}, u32[]{:S(2)}) collective-permute-start(bf16[528,128]{1,0:T(8,128)(2,1)S(1)} %cast.2.refs_0_), channel_id=1, source_target_pairs={{0,2},{1,3},{2,0},{3,1},{4,6},{5,7},{6,4},{7,5},{8,10},{9,11},{10,... | collective-permute-start | bytes 405512 | tf_op jit(solution)/shard_map/ppermute | solution.py:374
  7.3 0.7 %copy-start.5 = (bf16[2,680]{1,0:T(2,128)(2,1)S(1)}, bf16[2,680]{1,0:T(2,128)(2,1)}, u32[]{:S(2)}) copy-start(bf16[2,680]{1,0:T(2,128)(2,1)} %shift_ref.1) | copy-start | bytes 8164
  8.0 3.4 %copy-start.1 = (f32[1,170,680]{2,0,1:T(1,128)S(1)}, f32[1,170,680]{2,0,1:T(1,128)}, u32[]{:S(2)}) copy-start(f32[1,170,680]{2,0,1:T(1,128)} %param.14) | copy-start | bytes 1387204
  11.6 8.1 %collective-permute-start.10 = (bf16[448,128]{1,0:T(8,128)(2,1)S(1)}, bf16[448,128]{1,0:T(8,128)(2,1)S(1)}, u32[]{:S(2)}, u32[]{:S(2)}) collective-permute-start(bf16[448,128]{1,0:T(8,128)(2,1)S(1)} %cast.3.refs_0_), channel_id=1, source_target_pairs={{0,2},{1,3},{2,0},{3,1},{4,6},{5,7},{6,4},{7,5},{8,10},{9,11},{10,... | collective-permute-start | bytes 344072 | tf_op jit(solution)/shard_map/ppermute | solution.py:374
  11.7 11.0 %collective-permute-start.6 = (bf16[528,128]{1,0:T(8,128)(2,1)S(1)}, bf16[528,128]{1,0:T(8,128)(2,1)S(1)}, u32[]{:S(2)}, u32[]{:S(2)}) collective-permute-start(bf16[528,128]{1,0:T(8,128)(2,1)S(1)} %cast.2.refs_0_), channel_id=1, source_target_pairs={{0,1},{1,0},{2,3},{3,2},{4,5},{5,4},{6,7},{7,6},{8,9},{9,8},{10,11... | collective-permute-start | bytes 405512 | tf_op jit(solution)/shard_map/ppermute | solution.py:374
  13.6 9.5 %collective-permute-start.8 = (bf16[528,128]{1,0:T(8,128)(2,1)S(1)}, bf16[528,128]{1,0:T(8,128)(2,1)S(1)}, u32[]{:S(2)}, u32[]{:S(2)}) collective-permute-start(bf16[528,128]{1,0:T(8,128)(2,1)S(1)} %collective-permute-done.7.refs_2_), channel_id=1, source_target_pairs={{0,1},{1,0},{2,3},{3,2},{4,5},{5,4},{6,7},{7,6},{8,9},{9,8},{10,11... | collective-permute-start | bytes 405512 | tf_op jit(solution)/shard_map/ppermute | solution.py:374
  15.6 11.6 %collective-permute-start.9 = (bf16[448,128]{1,0:T(8,128)(2,1)S(1)}, bf16[448,128]{1,0:T(8,128)(2,1)S(1)}, u32[]{:S(2)}, u32[]{:S(2)}) collective-permute-start(bf16[448,128]{1,0:T(8,128)(2,1)S(1)} %cast.3.refs_0_), channel_id=1, source_target_pairs={{0,1},{1,0},{2,3},{3,2},{4,5},{5,4},{6,7},{7,6},{8,9},{9,8},{10,11... | collective-permute-start | bytes 344072 | tf_op jit(solution)/shard_map/ppermute | solution.py:374
  19.7 7.5 %collective-permute-start.11 = (bf16[448,128]{1,0:T(8,128)(2,1)S(1)}, bf16[448,128]{1,0:T(8,128)(2,1)S(1)}, u32[]{:S(2)}, u32[]{:S(2)}) collective-permute-start(bf16[448,128]{1,0:T(8,128)(2,1)S(1)} %collective-permute-done.10.refs_2_), channel_id=1, source_target_pairs={{0,1},{1,0},{2,3},{3,2},{4,5},{5,4},{6,7},{7,6},{8,9},{9,8},{10,11... | collective-permute-start | bytes 344072 | tf_op jit(solution)/shard_map/ppermute | solution.py:374
  26.1 5.1 %collective-permute-start.15 = (bf16[528,128]{1,0:T(8,128)(2,1)S(1)}, bf16[528,128]{1,0:T(8,128)(2,1)S(1)}, u32[]{:S(2)}, u32[]{:S(2)}) collective-permute-start(bf16[528,128]{1,0:T(8,128)(2,1)S(1)} %get-tuple-element.204), channel_id=1, source_target_pairs={{0,1},{1,0},{2,3},{3,2},{4,5},{5,4},{6,7},{7,6},{8,9},{9,8},{10,11... | collective-permute-start | bytes 405512 | tf_op jit(solution)/shard_map/ppermute | solution.py:374
  30.2 8.2 %collective-permute-start.12 = (bf16[448,128]{1,0:T(8,128)(2,1)S(1)}, bf16[448,128]{1,0:T(8,128)(2,1)S(1)}, u32[]{:S(2)}, u32[]{:S(2)}) collective-permute-start(bf16[448,128]{1,0:T(8,128)(2,1)S(1)} %get-tuple-element.197), channel_id=1, source_target_pairs={{0,1},{1,0},{2,3},{3,2},{4,5},{5,4},{6,7},{7,6},{8,9},{9,8},{10,11... | collective-permute-start | bytes 344072 | tf_op jit(solution)/shard_map/ppermute | solution.py:374
  31.3 17.0 %collective-permute-start.16 = (bf16[528,128]{1,0:T(8,128)(2,1)S(1)}, bf16[528,128]{1,0:T(8,128)(2,1)S(1)}, u32[]{:S(2)}, u32[]{:S(2)}) collective-permute-start(bf16[528,128]{1,0:T(8,128)(2,1)S(1)} %get-tuple-element.206), channel_id=1, source_target_pairs={{0,1},{1,0},{2,3},{3,2},{4,5},{5,4},{6,7},{7,6},{8,9},{9,8},{10,11... | collective-permute-start | bytes 405512 | tf_op jit(solution)/shard_map/ppermute | solution.py:374
  32.4 15.9 %collective-permute-start.17 = (bf16[528,128]{1,0:T(8,128)(2,1)S(1)}, bf16[528,128]{1,0:T(8,128)(2,1)S(1)}, u32[]{:S(2)}, u32[]{:S(2)}) collective-permute-start(bf16[528,128]{1,0:T(8,128)(2,1)S(1)} %get-tuple-element.207), channel_id=1, source_target_pairs={{0,2},{1,3},{2,0},{3,1},{4,6},{5,7},{6,4},{7,5},{8,10},{9,11},{10,... | collective-permute-start | bytes 405512 | tf_op jit(solution)/shard_map/ppermute | solution.py:374
  38.4 10.8 %collective-permute-start.13 = (bf16[448,128]{1,0:T(8,128)(2,1)S(1)}, bf16[448,128]{1,0:T(8,128)(2,1)}, u32[]{:S(2)}, u32[]{:S(2)}) collective-permute-start(bf16[448,128]{1,0:T(8,128)(2,1)S(1)} %get-tuple-element.199), channel_id=1, source_target_pairs={{0,1},{1,0},{2,3},{3,2},{4,5},{5,4},{6,7},{7,6},{8,9},{9,8},{10,11... | collective-permute-start | bytes 344072 | tf_op jit(solution)/shard_map/ppermute | solution.py:374
  38.5 10.7 %collective-permute-start.14 = (bf16[448,128]{1,0:T(8,128)(2,1)S(1)}, bf16[448,128]{1,0:T(8,128)(2,1)}, u32[]{:S(2)}, u32[]{:S(2)}) collective-permute-start(bf16[448,128]{1,0:T(8,128)(2,1)S(1)} %get-tuple-element.200), channel_id=1, source_target_pairs={{0,2},{1,3},{2,0},{3,1},{4,6},{5,7},{6,4},{7,5},{8,10},{9,11},{10,... | collective-permute-start | bytes 344072 | tf_op jit(solution)/shard_map/ppermute | solution.py:374
  43.0 5.3 %copy-start.2 = (f32[170,360]{1,0:T(8,128)S(1)}, f32[170,360]{1,0:T(8,128)}, u32[]{:S(2)}) copy-start(f32[170,360]{1,0:T(8,128)} %get-tuple-element.208.refs_2_) | copy-start | bytes 734404
  43.0 5.3 %copy-start.3 = (f32[170,360]{1,0:T(8,128)S(1)}, f32[170,360]{1,0:T(8,128)}, u32[]{:S(2)}) copy-start(f32[170,360]{1,0:T(8,128)} %get-tuple-element.209.refs_3_) | copy-start | bytes 734404
  43.0 5.3 %copy-start.4 = (f32[170,360]{1,0:T(8,128)S(1)}, f32[170,360]{1,0:T(8,128)}, u32[]{:S(2)}) copy-start(f32[170,360]{1,0:T(8,128)} %get-tuple-element.210.refs_4_) | copy-start | bytes 734404
  43.0 6.3 %copy-start.9 = (f32[170,320]{1,0:T(8,128)S(1)}, f32[170,320]{1,0:T(8,128)}, u32[]{:S(2)}) copy-start(f32[170,320]{1,0:T(8,128)} %get-tuple-element.201) | copy-start | bytes 652804
  43.0 6.3 %copy-start.10 = (f32[170,320]{1,0:T(8,128)S(1)}, f32[170,320]{1,0:T(8,128)}, u32[]{:S(2)}) copy-start(f32[170,320]{1,0:T(8,128)} %get-tuple-element.202) | copy-start | bytes 652804
  48.3 1.0 %copy-start.6 = (f32[1,170,680]{2,0,1:T(1,128)S(1)}, f32[1,170,680]{2,0,1:T(1,128)}, u32[]{:S(2)}) copy-start(f32[1,170,680]{2,0,1:T(1,128)} %param.15) | copy-start | bytes 1387204
  48.3 1.2 %copy-start.7 = (f32[1,170,680]{2,0,1:T(1,128)S(1)}, f32[1,170,680]{2,0,1:T(1,128)}, u32[]{:S(2)}) copy-start(f32[1,170,680]{2,0,1:T(1,128)} %param.16) | copy-start | bytes 1387204
  48.3 1.2 %copy-start.8 = (f32[170,320]{1,0:T(8,128)S(1)}, f32[170,320]{1,0:T(8,128)}, u32[]{:S(2)}) copy-start(f32[170,320]{1,0:T(8,128)} %get-tuple-element.187.refs_4_) | copy-start | bytes 652804
  49.5 5.3 %collective-permute-start = (bf16[528,128]{1,0:T(8,128)(2,1)S(1)}, bf16[528,128]{1,0:T(8,128)(2,1)S(1)}, u32[]{:S(2)}, u32[]{:S(2)}) collective-permute-start(bf16[528,128]{1,0:T(8,128)(2,1)S(1)} %get-tuple-element.94), channel_id=1, source_target_pairs={{0,4},{4,8},{8,12},{12,16},{16,20},{20,24},{24,28},{28,0},{1,5},{5... | collective-permute-start | bytes 405512 | tf_op jit(solution)/shard_map/cond/branch_0_fun/ppermute | solution.py:370
  51.5 5.2 %collective-permute-start.1 = (bf16[448,128]{1,0:T(8,128)(2,1)S(1)}, bf16[448,128]{1,0:T(8,128)(2,1)S(1)}, u32[]{:S(2)}, u32[]{:S(2)}) collective-permute-start(bf16[448,128]{1,0:T(8,128)(2,1)S(1)} %get-tuple-element.98), channel_id=1, source_target_pairs={{0,4},{4,8},{8,12},{12,16},{16,20},{20,24},{24,28},{28,0},{1,5},{5... | collective-permute-start | bytes 344072 | tf_op jit(solution)/shard_map/cond/branch_0_fun/ppermute | solution.py:370
